TPU v7x, 512 devices: a whole 4x8x8 slice. The times are simulated.
512 devices in a mesh: prow: 32 (over z, x), pcol: 16 (over y, core).
Axes of the slice: x: 4, y: 8, z: 8, core: 2. Of those that a mesh axis runs over, the one named last changes fastest.
Arguments:
- matrix: float32 [16384, 6144], P('prow', 'pcol'), may hold values from -6 to 6
- panel: float32 [16384, 512], P('prow', 'pcol'), may hold values from -0.25 to 0.25
- sources: int32 [512], replicated, may hold values from 0 to 16383, as said below
Outputs:
- updated: float32 [16384, 6144], P('prow', 'pcol')
Inputs may be any that keep to these rules, and one draw needn't show every extreme that they name: `sources`: the entries are distinct; one equals 16383 and another equals 8192.
All inputs are finite; a program needn't handle non-finite values.
Results may differ from a plain program's by a relative error of at most 0.0031.
Values may be sent and summed in bfloat16 or wider, within the bound.
No kernel may reach another device: no remote copies, remote signals or barrier semaphores. Data moves between devices by JAX's collectives and lax.ppermute only.
A program may use at most 64 MiB of HBM per device.

v0:
```python
import jax
import jax.numpy as jnp
from jax import lax
from jax.sharding import PartitionSpec as P


def broadcast(block, axis, holder):
    block = jnp.where(lax.axis_index(axis) == holder, block, jnp.zeros_like(block))
    return lax.psum(block, axis)


def assignment(sources):
    width = sources.shape[0]
    top = jnp.arange(width, dtype=jnp.int32)
    used = jnp.any(sources[None, :] == top[:, None], axis=1)
    free_rank = jnp.cumsum(jnp.where(used, 0, 1).astype(jnp.int32)) - 1
    vacated = sources >= width
    vac_rank = jnp.cumsum(vacated.astype(jnp.int32)) - 1
    match = jnp.logical_and(jnp.logical_not(used)[None, :], free_rank[None, :] == vac_rank[:, None])
    match = jnp.logical_and(match, vacated[:, None])
    fill = jnp.sum(jnp.where(match, top[None, :], 0), axis=1)
    return (vacated, fill)


def forward_solve(head_lower, right_rows):
    width = head_lower.shape[0]
    lower = jnp.tril(head_lower, -1) + jnp.eye(width, dtype=jnp.float32)
    return jax.scipy.linalg.solve_triangular(lower, right_rows, lower=True, unit_diagonal=True)


def on_device(matrix, panel, sources):
    rows, cols = matrix.shape
    width = sources.shape[0]
    myself = lax.axis_index("prow")
    global_rows = myself * rows + jnp.arange(rows, dtype=jnp.int32)
    vacated, fill = assignment(sources)
    local_index = sources - myself * rows
    owned = jnp.logical_and(local_index >= 0, local_index < rows)
    picked = jnp.take(matrix, jnp.clip(local_index, 0, rows - 1), axis=0)
    contrib = jnp.where(owned[:, None], picked, 0.0)
    head_lower = lax.all_gather(panel, "pcol", axis=1, tiled=True)
    pivot_rows = lax.psum(contrib, "prow")
    top_block = broadcast(matrix.astype(jnp.bfloat16), "prow", 0).astype(matrix.dtype)

    def solve_here():
        return forward_solve(head_lower, pivot_rows)

    def skip_solve():
        return jnp.zeros_like(pivot_rows)

    upper = lax.cond(myself == 0, solve_here, skip_solve)
    upper_half = broadcast(upper.astype(jnp.bfloat16), "prow", 0)
    hits = jnp.logical_and(vacated[None, :], sources[None, :] == global_rows[:, None])
    landed = jnp.any(hits, axis=1)
    fill_index = jnp.sum(jnp.where(hits, fill[None, :], 0), axis=1)
    incoming = jnp.take(top_block, fill_index, axis=0)
    swapped = jnp.where(landed[:, None], incoming, matrix)
    multipliers = panel.astype(jnp.bfloat16)
    product = jnp.dot(
        lax.all_gather(multipliers, "pcol", axis=1, tiled=True),
        upper_half,
        preferred_element_type=jnp.float32,
    )
    result = swapped - product
    head_rows = jnp.concatenate([upper, jnp.zeros((rows - width, cols), jnp.float32)], axis=0)
    return jnp.where((global_rows < width)[:, None], head_rows, result)


def solution(mesh):
    in_specs = (P("prow", "pcol"), P("prow", "pcol"), P())
    out_specs = P("prow", "pcol")
    return jax.shard_map(
        on_device, mesh=mesh, in_specs=in_specs, out_specs=out_specs, check_vma=False
    )
```

profile of v0, /device:TPU:8, one launch (start us, length us, event | category | flops | bytes accessed | tf_op | source)
XLA Modules:
  0.0 400.0 jit_solution(17572510499444267314)
XLA Ops:
  7.4 0.7 copy-done.5
  8.1 3.0 gather_fusion
  11.0 1.1 select_select_fusion.1
  12.2 0.5 all-gather.2.cloned.1.call-update
  12.8 0.3 copy-done.3
  13.1 0.6 convert_element_type.25
  13.7 0.3 copy.21
  14.0 0.3 reduce-window.24
  14.4 0.4 fusion.22
  14.8 0.3 reduce-window.16
  15.2 0.1 slice_reduce_fusion
  15.3 0.1 slice_reduce_fusion.1
  15.4 0.1 add_bitcast_fusion
  15.5 0.5 select_reduce_fusion.1
  16.0 0.4 select_reduce_fusion
  16.4 0.8 convert_select_fusion
  17.2 159.8 %all-reduce.4.cloned.1.call-done = f32[512,384]{1,0:T(8,128)} async-done(((f32[512,384]{1,0:T(8,128)}), f32[512,384]{1,0:T(8,128)}) %all-reduce.4.cloned.1.call-update) | async-done | bytes 786448 | tf_op jit(solution)/shard_map/psum | solution.py:42
  177.0 54.7 %conditional.1 = (bf16[512,384]{1,0:T(8,128)(2,1)S(1)}, f32[512,384]{0,1:T(8,128)S(1)}) conditional(s32[]{:T(128)} %convert_element_type.22, () %tuple.16, (f32[512,512]{0,1:T(8,128)}, f32[512,384]{1,0:T(8,128)}) %tuple.17), branch_computations={%region_1.0_spmd, %region_2.4_spmd} | conditional | flops 760037888 | bytes 16388369 | solution.py:51
  177.0 1.6 copy.19
  178.5 0.2 convert_add_fusion
  178.8 8.5 %while.1 = (s32[]{:T(128)}, f32[512,512]{1,0:T(8,128)S(1)}, s32[4,2]{0,1:T(2,128)S(1)}, f32[4,128,128]{2,1,0:T(8,128)S(1)}, s32[]{:T(128)}) while((s32[]{:T(128)}, f32[512,512]{1,0:T(8,128)S(1)}, s32[4,2]{0,1:T(2,128)S(1)}, f32[4,128,128]{2,1,0:T(8,128)S(1)}, s32[]{:T(128)}) %tuple.43), condition=%wide.while_cond, body=%wide.while_body.sunk | while | flops 2 | bytes 131189 | solution.py:28
  178.9 0.6 fusion.31
  179.5 1.4 bitcast_dynamic-update-slice_fusion.2
  181.0 0.6 fusion.31
  181.6 1.4 bitcast_dynamic-update-slice_fusion.2
  183.1 0.6 fusion.31
  183.7 1.4 bitcast_dynamic-update-slice_fusion.2
  185.2 0.6 fusion.31
  185.8 1.4 bitcast_dynamic-update-slice_fusion.2
  187.3 39.3 %custom-call.3 = f32[4,128,128]{1,2,0:T(8,128)S(1)} custom-call(f32[4,128,128]{2,1,0:T(8,128)S(1)} %get-tuple-element.25), custom_call_target="InvertDiagBlocksLowerTriangular" | custom-call | tf_op jit(solution)/shard_map/cond/branch_1_fun/jit(_solve_triangular)/triangular_solve | solution.py:28
  226.6 1.4 fusion.9
  228.0 1.2 convolution_subtract_fusion.2
  229.2 0.4 fusion.15
  229.6 0.4 convolution_subtract_fusion.1
  230.0 0.4 fusion.13
  230.4 0.6 convolution_subtract_fusion
  231.0 0.4 fusion.12
  231.4 0.3 copy.25
  231.7 0.8 broadcast_select_fusion
  232.6 0.7 copy-done.4
  233.3 18.5 %all_gather.7 = bf16[512,512]{0,1:T(8,128)(2,1)} all-gather(bf16[512,32]{0,1:T(8,128)(2,1)S(1)} %copy-done.4), channel_id=1, replica_groups=mesh['prow'=32,'pcol'=16] {'pcol'}, dimensions={1}, use_global_device_ids=true | all-gather | bytes 557056 | tf_op jit(solution)/shard_map/all_gather | solution.py:60
  251.8 134.6 %all-reduce.6.cloned.1.call-done = (bf16[512,384]{1,0:T(8,128)(2,1)}, bf16[512,384]{1,0:T(8,128)(2,1)}) async-done(((bf16[512,384]{1,0:T(8,128)(2,1)}, bf16[512,384]{1,0:T(8,128)(2,1)}), (bf16[512,384]{1,0:T(8,128)(2,1)}, bf16[512,384]{1,0:T(8,128)(2,1)})) %all-reduce.6.cloned.1.call-update) | async-done | bytes 786448 | tf_op jit(solution)/shard_map/psum | solution.py:9
  386.3 1.0 convert_element_type.24
  387.4 1.6 gather_fusion.1
  389.0 0.3 copy.20
  389.3 0.7 copy-done.2
  390.0 1.4 fusion.20
  391.4 1.1 copy.23
  (37 shorter events, 0.8 us)
Async XLA Ops:
  7.4 169.6 %all-reduce.4.cloned.1.call-start = ((), (), s32[]{:S(2)}) async-start(), calls=%async_computation.1 | async-start | bytes 1572864 | tf_op jit(solution)/shard_map/psum | solution.py:42
  7.4 0.7 copy-start.5
  12.1 1.5 copy-start
  12.2 0.9 copy-start.3
  12.2 164.8 %all-gather.2.cloned.1.call-start = ((), (), s32[]{:S(2)}) async-start(), calls=%async_computation | async-start | bytes 1114112 | tf_op jit(solution)/shard_map/all_gather | solution.py:41
  12.7 373.6 %all-reduce.6.cloned.1.call-start = ((), (), s32[]{:S(2)}) async-start(), calls=%async_computation.2 | async-start | bytes 1572864 | tf_op jit(solution)/shard_map/psum | solution.py:9
  226.6 3.0 copy-start.1
  232.5 0.8 copy-start.4
  389.0 1.0 copy-start.2
Sparse Core Ops, SparseCore 0:
  12.3 164.6 all-reduce.3
  232.7 153.6 all-reduce.5
Sparse Core Ops, SparseCore 1:
  14.8 45.2 all-gather.1
where the time goes:
time: 401 us; the launch traced here: 400 us
  waiting for transfers between devices  295 us (74%)
  other arithmetic  46 us (11%)
  local copies, waits for them, and re-layouts  19.2 us (5%)
  blocking collectives  18.5 us (5%)
  between operations  15 us (4%)
  matrix products  6.1 us (2%)
    psum x1, waiting for transfers between devices, on_device(): pivot_rows = lax.psum(contrib, 'prow')  160 us
    psum x1, waiting for transfers between devices, broadcast(): return lax.psum(block, axis)  135 us
    another operation x5, other arithmetic, forward_solve(): jax.scipy.linalg.solve_triangular(lower, right_rows, lower=True, unit_dia...  39.6 us
    all_gather x1, blocking collectives, on_device(): lax.all_gather(multipliers, 'pcol', axis=1, tiled=True)  18.5 us
    another operation x17, local copies, waits for them, and re-layouts  10.3 us
  transfers between devices with their start and end apart: 3, of which 2 were waited for; matrix products, arithmetic and copies ran while one was open for 1% of the time, Pallas kernels for 0%

commit v1 on v0

v1 whole, which is shorter than its diff:
```python
import jax
import jax.numpy as jnp
from jax import lax
from jax.experimental import pallas as pl
from jax.experimental.pallas import tpu as pltpu
from jax.sharding import Mesh, PartitionSpec as P

GRID_ROW = ("z", "x")
SCALE = 65536.0
VMEM_LIMIT = 48 * 1024 * 1024
HALF = jnp.bfloat16


def call(kernel, out_shape, flops, moved):
    return pl.pallas_call(
        kernel,
        out_shape=out_shape,
        compiler_params=pltpu.CompilerParams(vmem_limit_bytes=VMEM_LIMIT),
        cost_estimate=pl.CostEstimate(flops=flops, bytes_accessed=moved, transcendentals=0),
    )


def grid_row():
    return lax.axis_index("z") * lax.axis_size("x") + lax.axis_index("x")


def exact_dot(left, right):
    return jnp.dot(left, right, precision=lax.Precision.HIGHEST, preferred_element_type=jnp.float32)


def half_dot(left, right):
    return jnp.dot(left, right, preferred_element_type=jnp.float32)


def iota(shape, dim):
    return lax.broadcasted_iota(jnp.int32, shape, dim)


def as_column(row):
    return jnp.transpose(jnp.broadcast_to(row, (8, row.shape[1])))[:, 0:1]


def one_hot(hit):
    return jnp.where(hit, 1.0, 0.0).astype(HALF)


def offer_kernel(row_ref, sources_ref, matrix_ref, columns_ref, out_ref):
    rows, cols = matrix_ref.shape
    width = sources_ref.shape[1]
    parts, each, wide = out_ref.shape
    myself = row_ref[0, 0]

    @pl.when(myself == 0)
    def _():
        out_ref[:, :, 0:cols] = matrix_ref[...].astype(HALF).reshape(parts, each, cols)

    @pl.when(myself != 0)
    def _():
        wanted = as_column(sources_ref[...]) - myself * rows
        picks = one_hot(wanted == iota((width, rows), 1))
        found = half_dot(picks, matrix_ref[...].astype(HALF))
        out_ref[:, :, 0:cols] = found.astype(HALF).reshape(parts, each, cols)

    columns = columns_ref[...]
    first = columns.astype(HALF).astype(jnp.float32)
    rest = columns - first
    second = rest.astype(HALF).astype(jnp.float32)
    third = rest - second
    for part in range(parts):
        high, lane = 4 * (part // 4), 128 * (part % 4)
        pieces = [x[high : high + 4, lane : lane + 128] for x in (first, second, third)]
        piece = jnp.concatenate(pieces + [jnp.zeros((4, 128), jnp.float32)], axis=0)
        out_ref[part, :, cols:wide] = piece.astype(HALF)


def collect_kernel(got_ref, out_ref):
    parts, each, twice = out_ref.shape
    cols = twice // 2
    total = got_ref[1, :, 0:cols].astype(jnp.float32)
    for part in range(2, parts):
        total = total + got_ref[part, :, 0:cols].astype(jnp.float32)
    pivots = total.astype(HALF)
    top = got_ref[0, :, 0:cols]
    for part in range(parts):
        out_ref[part, :, 0:cols] = pivots
        out_ref[part, :, cols:twice] = top


def slices_kernel(pieces_ref, columns_ref, out_ref):
    for part in range(32):
        high, lane = 4 * (part // 4), 128 * (part % 4)
        out_ref[high : high + 4, lane : lane + 128] = pieces_ref[part] * SCALE
    out_ref[32:64, :] = columns_ref[...].astype(HALF).astype(jnp.float32) * SCALE


def invert_block(lower):
    n = lower.shape[0]
    row, col = iota((n, n), 0), iota((n, n), 1)
    unit = jnp.where(row == col, 1.0, 0.0)
    power = jnp.where((row // 32 == col // 32) & (row > col), lower, 0.0)
    inverse = unit - power
    for _ in range(4):
        power = exact_dot(power, power)
        inverse = inverse + exact_dot(inverse, power)
    size = 32
    while size < n:
        off = (row // (2 * size) == col // (2 * size)) & (row // size > col // size)
        below = jnp.where(off, lower, 0.0)
        inverse = inverse - exact_dot(inverse, exact_dot(below, inverse))
        size *= 2
    return inverse


def prepare_kernel(row_ref, core_ref, sources_ref, mine_ref, other_ref, lower_ref, inverse_ref, weights_ref, choose_ref):
    width = sources_ref.shape[1]
    myself = row_ref[0, 0]
    core = core_ref[0, 0]
    chips = mine_ref.shape[0]
    sources = sources_ref[...]
    mine, other = mine_ref[...], other_ref[...]
    even = jnp.where(core == 0, mine, other)
    odd = jnp.where(core == 0, other, mine)
    blocks = []
    for chip in range(chips):
        blocks += [even[chip], odd[chip]]
    spread = jnp.concatenate([b[0:32] for b in blocks], axis=0) * (1.0 / SCALE)
    lower_ref[...] = jnp.transpose(spread)
    multipliers = jnp.concatenate([b[32:64] for b in blocks], axis=0) * (-1.0 / SCALE)
    weights_ref[:, width : 2 * width] = jnp.transpose(multipliers).astype(HALF)
    rows = weights_ref.shape[0]
    weights_ref[:, 0:width] = one_hot(sources - myself * rows == iota((rows, width), 0))

    for block in range(width // 128):
        here = slice(128 * block, 128 * block + 128)
        inverse_ref[here, :] = invert_block(lower_ref[here, here])

    sources_column = as_column(sources)
    square = (width, width)
    chosen = one_hot(sources_column == iota(square, 1))
    choose_ref[0:width, :] = chosen
    used = half_dot(jnp.ones((8, width), HALF), chosen)
    before = one_hot(iota(square, 0) <= iota(square, 1))
    free = 1.0 - used
    free_rank = half_dot(free.astype(HALF), before)
    vacated = jnp.broadcast_to(jnp.where(sources >= width, 1.0, 0.0), (8, width))
    vacated_rank = half_dot(vacated.astype(HALF), before)
    rank_column = jnp.transpose(vacated_rank)[:, 0:1]
    match = (free_rank[0:1] == rank_column) & (free[0:1] > 0.5) & (sources_column >= width)
    choose_ref[width : 2 * width, :] = one_hot(match)


def finish_kernel(row_ref, got_ref, matrix_ref, lower_ref, inverse_ref, weights_ref, choose_ref, out_ref):
    rows, cols = matrix_ref.shape
    width = lower_ref.shape[0]
    top = got_ref[:, :, cols : 2 * cols].reshape(width, cols)
    moved = half_dot(choose_ref[...], top)
    pivots = got_ref[:, :, 0:cols].reshape(width, cols).astype(jnp.float32) + moved[0:width]
    upper = []
    for block in range(width // 128):
        here = slice(128 * block, 128 * block + 128)
        right = pivots[here]
        if block:
            right = right - exact_dot(lower_ref[here, 0 : 128 * block], jnp.concatenate(upper, axis=0))
        upper.append(exact_dot(inverse_ref[here, :], right))
    upper = jnp.concatenate(upper, axis=0)
    myself = row_ref[0, 0]

    @pl.when(myself == 0)
    def _():
        out_ref[...] = upper

    @pl.when(myself != 0)
    def _():
        values = jnp.concatenate([moved[width : 2 * width].astype(HALF), upper.astype(HALF)], axis=0)
        landed = half_dot(weights_ref[:, 0:width], jnp.ones((width, 128), HALF))
        landed = jnp.concatenate([landed] * (cols // 128), axis=1)
        kept = jnp.where(landed > 0.5, 0.0, matrix_ref[...])
        out_ref[...] = kept + half_dot(weights_ref[...], values)


def everyone(block, count):
    return jnp.broadcast_to(block[None], (count,) + block.shape)


def exchange(blocks, axes):
    return lax.all_to_all(blocks, axes, 0, 0, tiled=False)


def on_device(matrix, panel, sources):
    rows, cols = matrix.shape
    width = sources.shape[0]
    parts = lax.axis_size(GRID_ROW)
    chips = lax.axis_size("y")
    each = width // parts
    f32 = jnp.float32
    row = grid_row().reshape(1, 1).astype(jnp.int32)
    core = lax.axis_index("core").reshape(1, 1).astype(jnp.int32)
    sources = sources.reshape(1, width)
    columns = panel.T

    offer = call(
        offer_kernel, jax.ShapeDtypeStruct((parts, each, cols + 128), HALF), 2 * width * rows * cols, 2 * rows * cols * 4
    )(row, sources, matrix, columns)
    got = exchange(offer, GRID_ROW)

    pieces = got[0, :, cols:].astype(f32)
    pieces = pieces[0:4] + pieces[4:8] + pieces[8:12]
    pieces = exchange(everyone(pieces, parts), GRID_ROW)
    slices = call(slices_kernel, jax.ShapeDtypeStruct((64, width), f32), 0, 4 * 64 * width)(pieces, columns)
    mine = exchange(everyone(slices.astype(jnp.float16), chips), "y")
    other = lax.ppermute(mine, "core", [(0, 1), (1, 0)])

    collected = call(
        collect_kernel, jax.ShapeDtypeStruct((parts, each, 2 * cols), HALF), parts * each * cols, 4 * parts * each * cols
    )(got)
    collected, _ = lax.optimization_barrier((collected, mine))
    arrived = exchange(collected, GRID_ROW)

    lower, inverse, weights, choose = call(
        prepare_kernel,
        (
            jax.ShapeDtypeStruct((width, width), f32),
            jax.ShapeDtypeStruct((width, 128), f32),
            jax.ShapeDtypeStruct((rows, 2 * width), HALF),
            jax.ShapeDtypeStruct((2 * width, width), HALF),
        ),
        10 * width * width * width,
        8 * width * width * 4,
    )(row, core, sources, mine.astype(f32), other.astype(f32))
    return call(finish_kernel, jax.ShapeDtypeStruct((rows, cols), f32), 8 * rows * cols * width, 12 * rows * cols * 4)(
        row, arrived, matrix, lower, inverse, weights, choose
    )


def solution(mesh):
    shape = mesh.devices.shape
    chips = mesh.devices.reshape(shape[0] // 8, 8, shape[1] // 2, 2)
    grid = Mesh(chips, ("z", "x", "y", "core"))
    spec = P(GRID_ROW, ("y", "core"))
    return jax.shard_map(on_device, mesh=grid, in_specs=(spec, spec, P()), out_specs=spec, check_vma=False)
```

time: 401 us -> 103 us (0.26)
  the two profiles are of different devices: /device:TPU:8 before, /device:TPU:2 now
where the time goes in v1:
time: 103 us; the launch traced here: 102 us
  blocking collectives  44.1 us (43%)
  waiting for transfers between devices  21.4 us (21%)
  Pallas kernels  14.3 us (14%)
  starting transfers between devices  14.1 us (14%)
  local copies, waits for them, and re-layouts  7.93 us (8%)
    all_to_all x2, blocking collectives, exchange(): return lax.all_to_all(blocks, axes, 0, 0, tiled=False)  44.1 us
    all_to_all x2, waiting for transfers between devices, exchange(): return lax.all_to_all(blocks, axes, 0, 0, tiled=False)  19.7 us
    all_to_all x2, starting transfers between devices, exchange(): return lax.all_to_all(blocks, axes, 0, 0, tiled=False)  12.2 us
    pallas_call x1, Pallas kernels, on_device(): call(prepare_kernel, (jax.ShapeDtypeStruct((width, width), f32), jax.Shap...  7.86 us
    unnamed x16, local copies, waits for them, and re-layouts  7.07 us
    pallas_call x1, Pallas kernels, on_device(): call(finish_kernel, jax.ShapeDtypeStruct((rows, cols), f32), 8 * rows * c...  4.68 us
  transfers between devices with their start and end apart: 3, of which 3 were waited for; matrix products, arithmetic and copies ran while one was open for 0% of the time, Pallas kernels for 9%

profile of v1, /device:TPU:2, one launch (start us, length us, event | category | flops | bytes accessed | tf_op | source)
XLA Modules:
  0.0 102.2 jit_solution(5926762019303423396)
XLA Ops:
  0.0 0.0 copy-start.7
  0.0 0.7 copy-done.7
  0.7 0.0 copy-start
  0.7 1.1 %copy-done = f32[512,384]{1,0:T(8,128)S(1)} copy-done((f32[512,384]{1,0:T(8,128)S(1)}, f32[512,384]{1,0:T(8,128)}, u32[]{:S(2)}) %copy-start) | copy-done | bytes 786456
  1.8 0.0 copy-start.6
  1.8 0.8 copy-done.6
  2.7 0.8 shard_map.37
  3.5 30.1 %all_to_all.20.got_ref = bf16[32,16,512]{2,1,0:T(8,128)(2,1)S(1)} all-to-all(bf16[32,16,512]{2,1,0:T(8,128)(2,1)S(1)} %shard_map.37), channel_id=1, replica_groups=mesh['z'=4,'x'=8,'y'=8,'core'=2] {'z','x'}, dimensions={0} | all-to-all | bytes 1048576 | tf_op jit(solution)/shard_map/all_to_all | solution.py:186
  33.6 14.0 %all_to_all.21.pieces_ref = f32[32,4,128]{2,1,0:T(4,128)S(1)} all-to-all(f32[32,4,128]{2,1,0:T(4,128)S(1)} %broadcast_in_dim.4), channel_id=1, replica_groups=mesh['z'=4,'x'=8,'y'=8,'core'=2] {'z','x'}, dimensions={0} | all-to-all | bytes 131072 | tf_op jit(solution)/shard_map/all_to_all | solution.py:186
  47.6 0.8 broadcast_in_dim.5
  48.5 7.1 %all-to-all-start.2 = ((f16[8,64,512]{2,1,0:T(8,128)(2,1)}), f16[8,64,512]{2,1,0:T(8,128)(2,1)S(1)}, u32[]{:S(2)}, u32[]{:S(2)}) async-start(f16[8,64,512]{2,1,0:T(8,128)(2,1)} %broadcast_in_dim.5), calls=%async_computation.2 | async-start | bytes 1048576 | tf_op jit(solution)/shard_map/all_to_all | solution.py:186
  55.6 1.0 shard_map.38
  56.6 14.3 %all-to-all-done.2 = f16[8,64,512]{2,1,0:T(8,128)(2,1)S(1)} async-done(((f16[8,64,512]{2,1,0:T(8,128)(2,1)}), f16[8,64,512]{2,1,0:T(8,128)(2,1)S(1)}, u32[]{:S(2)}, u32[]{:S(2)}) %all-to-all-start.2) | async-done | bytes 524320 | tf_op jit(solution)/shard_map/all_to_all | solution.py:186
  70.8 5.1 %all-to-all-start.3 = ((bf16[32,16,768]{2,1,0:T(8,128)(2,1)}), bf16[32,16,768]{2,1,0:T(8,128)(2,1)S(1)}, u32[]{:S(2)}, u32[]{:S(2)}) async-start(bf16[32,16,768]{2,1,0:T(8,128)(2,1)} %shard_map.38), calls=%async_computation.3 | async-start | bytes 1572864 | tf_op jit(solution)/shard_map/all_to_all | solution.py:186
  75.9 1.9 %collective-permute-start = (f16[8,64,512]{2,1,0:T(8,128)(2,1)S(1)}, f16[8,64,512]{2,1,0:T(8,128)(2,1)S(1)}, u32[]{:S(2)}, u32[]{:S(2)}) collective-permute-start(f16[8,64,512]{2,1,0:T(8,128)(2,1)S(1)} %all-to-all-done.2), channel_id=1, source_target_pairs={{0,1},{1,0},{2,3},{3,2},{4,5},{5,4},{6,7},{7,6},{8,9},{9,8},{10,11... | collective-permute-start | bytes 1572872 | tf_op jit(solution)/shard_map/ppermute | solution.py:211
  77.8 0.1 convert_element_type.15.mine_ref
  77.9 1.7 %collective-permute-done = f16[8,64,512]{2,1,0:T(8,128)(2,1)S(1)} collective-permute-done((f16[8,64,512]{2,1,0:T(8,128)(2,1)S(1)}, f16[8,64,512]{2,1,0:T(8,128)(2,1)S(1)}, u32[]{:S(2)}, u32[]{:S(2)}) %collective-permute-start) | collective-permute-done | bytes 524320 | tf_op jit(solution)/shard_map/ppermute | solution.py:211
  79.7 0.1 convert_element_type.16.other_ref
  79.8 0.0 copy-start.1
  79.8 7.9 %shard_map.40 = (f32[512,512]{1,0:T(8,128)S(1)}, f32[512,128]{1,0:T(8,128)S(1)}, bf16[512,1024]{1,0:T(8,128)(2,1)S(1)}, bf16[1024,512]{1,0:T(8,128)(2,1)S(1)}) custom-call(s32[1,1]{1,0:T(1,128)} %bitcast.row_ref, s32[1,1]{1,0:T(1,128)} %bitcast.4.core_ref, s32[1,512]{1,0:T(1,128)S(1)} %bitcast.9, f32[8,64,512]{2,1,0:T(8,128)S(1)} %convert_element_type.15.mine_ref, ...), custom_call_target="tpu_custom_call" | custom-call | flops 1342177280 | bytes 8388608 | tf_op jit(solution)/shard_map/pallas_call | solution.py:219
  87.7 0.0 copy-start.2
  87.7 1.0 copy-done.2
  88.7 0.0 copy-start.4
  88.7 1.0 copy-done.4
  89.7 5.4 %all-to-all-done.3.got_ref = bf16[32,16,768]{2,1,0:T(8,128)(2,1)S(1)} async-done(((bf16[32,16,768]{2,1,0:T(8,128)(2,1)}), bf16[32,16,768]{2,1,0:T(8,128)(2,1)S(1)}, u32[]{:S(2)}, u32[]{:S(2)}) %all-to-all-start.3) | async-done | bytes 786464 | tf_op jit(solution)/shard_map/all_to_all | solution.py:186
  95.1 0.0 copy-done.1
  95.1 0.0 copy-start.3
  95.1 1.2 %copy-done.3 = bf16[512,1024]{1,0:T(8,128)(2,1)S(1)} copy-done((bf16[512,1024]{1,0:T(8,128)(2,1)S(1)}, bf16[512,1024]{1,0:T(8,128)(2,1)}, u32[]{:S(2)}) %copy-start.3) | copy-done | bytes 1048600
  96.3 0.0 copy-start.5
  96.3 1.2 %copy-done.5 = bf16[1024,512]{1,0:T(8,128)(2,1)S(1)} copy-done((bf16[1024,512]{1,0:T(8,128)(2,1)S(1)}, bf16[1024,512]{1,0:T(8,128)(2,1)}, u32[]{:S(2)}) %copy-start.5) | copy-done | bytes 1048600
  97.6 4.7 %shard_map.41 = f32[512,384]{1,0:T(8,128)} custom-call(s32[1,1]{1,0:T(1,128)} %bitcast.row_ref, bf16[32,16,768]{2,1,0:T(8,128)(2,1)S(1)} %all-to-all-done.3.got_ref, f32[512,384]{1,0:T(8,128)S(1)} %copy-done.1, f32[512,512]{1,0:T(8,128)S(1)} %get-tuple-element.11.lower_ref, f32[512,128]{1,0:T(8,128)S(1)} %get-tuple-element.12.inverse_ref, ...), custom_call_target="tpu_custom_call" | custom-call | flops 805306368 | bytes 9437184 | tf_op jit(solution)/shard_map/pallas_call | solution.py:230
  (5 shorter events, 0.1 us)
Async XLA Ops:
  0.0 0.7 copy-start.7
  0.7 1.1 %copy-start = (f32[512,384]{1,0:T(8,128)S(1)}, f32[512,384]{1,0:T(8,128)}, u32[]{:S(2)}) copy-start(f32[512,384]{1,0:T(8,128)} %matrix_ref.3) | copy-start | bytes 2359300
  1.8 0.8 copy-start.6
  48.5 22.3 %all-to-all-start.2 = ((f16[8,64,512]{2,1,0:T(8,128)(2,1)}), f16[8,64,512]{2,1,0:T(8,128)(2,1)S(1)}, u32[]{:S(2)}, u32[]{:S(2)}) async-start(f16[8,64,512]{2,1,0:T(8,128)(2,1)} %broadcast_in_dim.5), calls=%async_computation.2 | async-start | bytes 1048576 | tf_op jit(solution)/shard_map/all_to_all | solution.py:186
  70.8 24.3 %all-to-all-start.3 = ((bf16[32,16,768]{2,1,0:T(8,128)(2,1)}), bf16[32,16,768]{2,1,0:T(8,128)(2,1)S(1)}, u32[]{:S(2)}, u32[]{:S(2)}) async-start(bf16[32,16,768]{2,1,0:T(8,128)(2,1)} %shard_map.38), calls=%async_computation.3 | async-start | bytes 1572864 | tf_op jit(solution)/shard_map/all_to_all | solution.py:186
  75.9 3.8 %collective-permute-start = (f16[8,64,512]{2,1,0:T(8,128)(2,1)S(1)}, f16[8,64,512]{2,1,0:T(8,128)(2,1)S(1)}, u32[]{:S(2)}, u32[]{:S(2)}) collective-permute-start(f16[8,64,512]{2,1,0:T(8,128)(2,1)S(1)} %all-to-all-done.2), channel_id=1, source_target_pairs={{0,1},{1,0},{2,3},{3,2},{4,5},{5,4},{6,7},{7,6},{8,9},{9,8},{10,11... | collective-permute-start | bytes 1572872 | tf_op jit(solution)/shard_map/ppermute | solution.py:211
  79.8 15.3 %copy-start.1 = (f32[512,384]{1,0:T(8,128)S(1)}, f32[512,384]{1,0:T(8,128)}, u32[]{:S(2)}) copy-start(f32[512,384]{1,0:T(8,128)} %matrix_ref.3) | copy-start | bytes 2359300
  87.7 1.0 copy-start.2
  88.7 1.0 copy-start.4
  95.1 1.2 %copy-start.3 = (bf16[512,1024]{1,0:T(8,128)(2,1)S(1)}, bf16[512,1024]{1,0:T(8,128)(2,1)}, u32[]{:S(2)}) copy-start(bf16[512,1024]{1,0:T(8,128)(2,1)} %copy-done.2) | copy-start | bytes 3145732
  96.3 1.2 %copy-start.5 = (bf16[1024,512]{1,0:T(8,128)(2,1)S(1)}, bf16[1024,512]{1,0:T(8,128)(2,1)}, u32[]{:S(2)}) copy-start(bf16[1024,512]{1,0:T(8,128)(2,1)} %copy-done.4) | copy-start | bytes 3145732

commit v2 on v1

v2 whole, which is shorter than its diff:
```python
import jax
import jax.numpy as jnp
from jax import lax
from jax.experimental import pallas as pl
from jax.experimental.pallas import tpu as pltpu
from jax.sharding import Mesh, PartitionSpec as P

GRID_ROW = ("z", "x")
SCALE = 65536.0
ARRIVALS = (0, 4, 1, 5, 2, 6, 7, 3)
VMEM_LIMIT = 20 * 1024 * 1024
VMEM_MOST = 60 * 1024 * 1024
HALF = jnp.bfloat16


def call(kernel, out_shape, flops, moved, limit=VMEM_LIMIT, **more):
    return pl.pallas_call(
        kernel,
        out_shape=out_shape,
        **more,
        compiler_params=pltpu.CompilerParams(vmem_limit_bytes=limit),
        cost_estimate=pl.CostEstimate(flops=flops, bytes_accessed=moved, transcendentals=0),
    )


def grid_row():
    return lax.axis_index("z") * lax.axis_size("x") + lax.axis_index("x")


def exact_dot(left, right):
    return jnp.dot(left, right, precision=lax.Precision.HIGHEST, preferred_element_type=jnp.float32)


def half_dot(left, right):
    return jnp.dot(left, right, preferred_element_type=jnp.float32)


def in_two(values):
    high = values.astype(HALF)
    low = (values - high.astype(jnp.float32)).astype(HALF)
    return jnp.stack([high, low])


def split_dot(left, right):
    high = right.astype(HALF)
    low = (right - high.astype(jnp.float32)).astype(HALF)
    sides = jnp.concatenate([left[0], left[1], left[0]], axis=1)
    return half_dot(sides, jnp.concatenate([high, high, low], axis=0))


def iota(shape, dim):
    return lax.broadcasted_iota(jnp.int32, shape, dim)


def as_column(row):
    return jnp.transpose(jnp.broadcast_to(row, (8, row.shape[1])))[:, 0:1]


def one_hot(hit):
    return jnp.where(hit, 1.0, 0.0).astype(HALF)


def offer_kernel(
    place_ref, sources_hbm, matrix_hbm, columns_hbm, out_hbm, own_ref, sources_ref, matrix_ref, columns_ref, out_ref, sems, sent
):
    rows, cols = matrix_ref.shape
    width = sources_ref.shape[1]
    parts, each, wide = out_ref.shape
    myself = place_ref[0, 0]
    quarter, some = rows // 4, parts // 4
    small = [
        pltpu.make_async_copy(sources_hbm, sources_ref, sems.at[0]),
        pltpu.make_async_copy(columns_hbm, columns_ref, sems.at[1]),
    ]
    large = []
    for at in range(4):
        here = pl.ds(at * quarter, quarter)
        large.append(pltpu.make_async_copy(matrix_hbm.at[here], matrix_ref.at[here], sems.at[2 + at]))
    for copy in small + large:
        copy.start()
    for copy in small:
        copy.wait()

    columns = columns_ref[...]
    own_ref[...] = columns.astype(HALF)
    first = columns.astype(HALF).astype(jnp.float32)
    second = columns - first
    holders = columns.shape[0] // 4
    for part in range(parts):
        high = 4 * (part % holders)
        for piece, lane in ((first, cols), (second, cols + 128)):
            piece = jnp.concatenate([piece[high : high + 4, 128 * q : 128 * q + 128] for q in range(4)], axis=0)
            out_ref[part, :, lane : lane + 128] = piece.astype(HALF)

    def send(at):
        here = pl.ds(at * some, some)
        return pltpu.make_async_copy(out_ref.at[here], out_hbm.at[here], sent.at[at])

    @pl.when(myself == 0)
    def _():
        for at in range(4):
            large[at].wait()
            block = matrix_ref[quarter * at : quarter * (at + 1)].astype(HALF)
            out_ref[some * at : some * (at + 1), :, 0:cols] = block.reshape(some, each, cols)
            send(at).start()

    @pl.when(myself != 0)
    def _():
        wanted = as_column(sources_ref[...]) - myself * rows
        picks = one_hot(wanted == iota((width, rows), 1))
        for copy in large:
            copy.wait()
        block = matrix_ref[...].astype(HALF)
        for at in range(4):
            found = half_dot(picks[quarter * at : quarter * (at + 1)], block).astype(HALF)
            out_ref[some * at : some * (at + 1), :, 0:cols] = found.reshape(some, each, cols)
            send(at).start()

    for at in range(4):
        send(at).wait()


def collect_kernel(got_ref, out_ref):
    parts, each, twice = out_ref.shape
    cols = twice // 2
    total = got_ref[1, :, 0:cols].astype(jnp.float32)
    for part in range(2, parts):
        total = total + got_ref[part, :, 0:cols].astype(jnp.float32)
    pivots = total.astype(HALF)
    top = got_ref[0, :, 0:cols]
    for part in range(parts):
        out_ref[part, :, 0:cols] = pivots
        out_ref[part, :, cols:twice] = top


def invert_block(lower):
    n = lower.shape[0]
    row, col = iota((n, n), 0), iota((n, n), 1)
    unit = jnp.where(row == col, 1.0, 0.0)
    power = jnp.where((row // 32 == col // 32) & (row > col), lower, 0.0)
    inverse = unit - power
    for _ in range(4):
        power = exact_dot(power, power)
        inverse = inverse + exact_dot(inverse, power)
    size = 32
    while size < n:
        off = (row // (2 * size) == col // (2 * size)) & (row // size > col // size)
        below = jnp.where(off, lower, 0.0)
        inverse = inverse - exact_dot(inverse, exact_dot(below, inverse))
        size *= 2
    return inverse


def prepare_kernel(
    place_ref,
    sources_ref,
    mine_ref,
    other_ref,
    own_ref,
    across_ref,
    matrix_ref,
    below_ref,
    inverse_ref,
    weights_ref,
    choose_ref,
    kept_ref,
    lower_ref,
    gathered_ref,
):
    width = sources_ref.shape[1]
    core, chip = place_ref[0, 1], place_ref[0, 2]
    sources = sources_ref[...]
    mine, other = mine_ref[...], other_ref[...]
    pair = (jnp.where(core == 0, mine, other), jnp.where(core == 0, other, mine))
    lines = []
    for at in range(8):
        for half in pair:
            lanes = []
            for q in range(4):
                lanes.append(jnp.concatenate([half[8 * x + at, 4 * q : 4 * q + 4] for x in range(8)], axis=0))
            lines.append(jnp.concatenate(lanes, axis=1))
    lower_ref[...] = jnp.transpose(jnp.concatenate(lines, axis=0)) * (1.0 / SCALE)

    for at, ahead in enumerate(ARRIVALS):
        start = 64 * lax.rem(chip + ahead, 8)
        here = slice(32 * at, 32 * at + 32)
        gathered_ref[pl.ds(pl.multiple_of(start + 32 * core, 32), 32), :] = own_ref[here, :]
        gathered_ref[pl.ds(pl.multiple_of(start + 32 * (1 - core), 32), 32), :] = across_ref[here, :]
    weights_ref[...] = -jnp.transpose(gathered_ref[...])
    rows, cols = matrix_ref.shape
    lands = one_hot(sources - place_ref[0, 0] * rows == iota((rows, width), 0))
    landed = half_dot(lands, jnp.ones((width, 128), HALF))
    kept_ref[...] = jnp.where(jnp.concatenate([landed] * (cols // 128), axis=1) > 0.5, 0.0, matrix_ref[...])

    count = width // 128
    for block in range(count):
        here = slice(128 * block, 128 * block + 128)
        inverse_ref[:, block] = in_two(invert_block(lower_ref[here, here]))
        for at in range(block):
            below_ref[:, block * (block - 1) // 2 + at] = in_two(lower_ref[here, 128 * at : 128 * at + 128])

    sources_column = as_column(sources)
    square = (width, width)
    chosen = one_hot(sources_column == iota(square, 1))
    used = half_dot(jnp.ones((8, width), HALF), chosen)
    before = one_hot(iota(square, 0) <= iota(square, 1))
    free = 1.0 - used
    free_rank = half_dot(free.astype(HALF), before)
    vacated = jnp.broadcast_to(jnp.where(sources >= width, 1.0, 0.0), (8, width))
    vacated_rank = half_dot(vacated.astype(HALF), before)
    rank_column = jnp.transpose(vacated_rank)[:, 0:1]
    match = (free_rank[0:1] == rank_column) & (free[0:1] > 0.5) & (sources_column >= width)
    choose_ref[...] = chosen + one_hot(match)


def finish_kernel(
    place_ref, sources_ref, got_ref, kept_ref, below_ref, inverse_ref, weights_ref, choose_ref, out_hbm, out_ref, sems
):
    rows, cols = kept_ref.shape
    width = sources_ref.shape[1]
    myself = place_ref[0, 0]
    sources = sources_ref[...]
    moved = half_dot(choose_ref[...], got_ref[:, :, cols : 2 * cols].reshape(width, cols))
    found = got_ref[:, :, 0:cols].reshape(width, cols).astype(jnp.float32)
    pivots = jnp.where(as_column(sources) >= width, found, moved)
    upper = []
    for block in range(width // 128):
        here = slice(128 * block, 128 * block + 128)
        right = pivots[here]
        for at in range(block):
            right = right - split_dot(below_ref[:, block * (block - 1) // 2 + at], upper[at])
        upper.append(split_dot(inverse_ref[:, block], right))
    upper = jnp.concatenate(upper, axis=0)

    quarter = rows // 4
    copies = []
    for at in range(4):
        here = pl.ds(at * quarter, quarter)
        copies.append(pltpu.make_async_copy(out_ref.at[here], out_hbm.at[here], sems.at[at]))

    @pl.when(myself == 0)
    def _():
        for at in range(4):
            here = slice(at * quarter, at * quarter + quarter)
            out_ref[here, :] = upper[here]
            copies[at].start()

    @pl.when(myself != 0)
    def _():
        fills, half = moved.astype(HALF), upper.astype(HALF)
        for at in range(4):
            here = slice(at * quarter, at * quarter + quarter)
            lands = one_hot(sources - (myself * rows + at * quarter) == iota((quarter, width), 0))
            change = half_dot(lands, fills) + half_dot(weights_ref[here, :], half)
            out_ref[here, :] = kept_ref[here, :] + change
            copies[at].start()

    for copy in copies:
        copy.wait()


def everyone(block, count):
    return jnp.broadcast_to(block[None], (count,) + block.shape)


def exchange(blocks, axes):
    return lax.all_to_all(blocks, axes, 0, 0, tiled=False)


def on_device(matrix, panel, sources):
    rows, cols = matrix.shape
    width = sources.shape[0]
    parts = lax.axis_size(GRID_ROW)
    chips = lax.axis_size("y")
    each = width // parts
    f32 = jnp.float32
    row = grid_row().astype(jnp.int32)
    place = jnp.stack([row, lax.axis_index("core"), lax.axis_index("y")]).reshape(1, 3).astype(jnp.int32)
    sources = sources.reshape(1, width)
    columns = panel.T
    smem, vmem = pl.BlockSpec(memory_space=pltpu.SMEM), pl.BlockSpec(memory_space=pltpu.VMEM)
    hbm = pl.BlockSpec(memory_space=pltpu.HBM)

    offer, own = call(
        offer_kernel,
        (jax.ShapeDtypeStruct((parts, each, cols + 256), HALF), jax.ShapeDtypeStruct(columns.shape, HALF)),
        2 * width * rows * cols,
        2 * rows * cols * 4,
        limit=VMEM_MOST,
        in_specs=[smem, hbm, hbm, hbm],
        out_specs=[hbm, vmem],
        scratch_shapes=[
            pltpu.VMEM((1, width), jnp.int32),
            pltpu.VMEM((rows, cols), f32),
            pltpu.VMEM(columns.shape, f32),
            pltpu.VMEM((parts, each, cols + 256), HALF),
            pltpu.SemaphoreType.DMA((6,)),
            pltpu.SemaphoreType.DMA((4,)),
        ],
    )(place, sources, matrix, columns)
    got = exchange(offer, GRID_ROW)

    def bring(block, ahead):
        return lax.ppermute(block, "y", [(i, (i - ahead) % chips) for i in range(chips)])

    own = jnp.concatenate([own, bring(own, 4)], axis=0)
    came = [bring(own, 1), bring(own, 2), bring(own, 7)]

    piece = got[0, :, cols : cols + 128].astype(f32) + got[0, :, cols + 128 : cols + 256].astype(f32)
    piece = (piece * SCALE).astype(jnp.float16)
    piece, own, came[0], came[1] = lax.optimization_barrier((piece, own, came[0], came[1]))
    mine = exchange(everyone(piece, 8 * chips), ("x", "y"))

    collected = call(
        collect_kernel, jax.ShapeDtypeStruct((parts, each, 2 * cols), HALF), parts * each * cols, 4 * parts * each * cols
    )(got)
    own = jnp.concatenate([own] + came, axis=0)
    collected, mine, own = lax.optimization_barrier((collected, mine, own))
    arrived = exchange(collected, GRID_ROW)
    other = lax.ppermute(mine, "core", [(0, 1), (1, 0)])
    across = lax.ppermute(own, "core", [(0, 1), (1, 0)])

    below, inverse, weights, choose, kept = call(
        prepare_kernel,
        (
            jax.ShapeDtypeStruct((2, 6, 128, 128), HALF),
            jax.ShapeDtypeStruct((2, 4, 128, 128), HALF),
            jax.ShapeDtypeStruct((rows, width), HALF),
            jax.ShapeDtypeStruct((width, width), HALF),
            jax.ShapeDtypeStruct((rows, cols), f32),
        ),
        10 * width * width * width,
        8 * width * width * 4,
        in_specs=[smem] + [vmem] * 6,
        scratch_shapes=[pltpu.VMEM((width, width), f32), pltpu.VMEM((width, rows), HALF)],
    )(place, sources, mine.astype(f32), other.astype(f32), own, across, matrix)
    return call(
        finish_kernel,
        jax.ShapeDtypeStruct((rows, cols), f32),
        8 * rows * cols * width,
        12 * rows * cols * 4,
        in_specs=[smem] + [vmem] * 7,
        out_specs=hbm,
        scratch_shapes=[pltpu.VMEM((rows, cols), f32), pltpu.SemaphoreType.DMA((4,))],
    )(place, sources, arrived, kept, below, inverse, weights, choose)


def solution(mesh):
    shape = mesh.devices.shape
    chips = mesh.devices.reshape(shape[0] // 8, 8, shape[1] // 2, 2)
    grid = Mesh(chips, ("z", "x", "y", "core"))
    spec = P(GRID_ROW, ("y", "core"))
    return jax.shard_map(on_device, mesh=grid, in_specs=(spec, spec, P()), out_specs=spec, check_vma=False)
```

time: 103 us -> 92.7 us (0.900)
  blocking collectives: 44.1 us -> 0 us
  starting transfers between devices: 14.1 us -> 55.4 us
  local copies, waits for them, and re-layouts: 7.93 us -> 0.76 us
  waiting for transfers between devices: 21.4 us -> 18.1 us
  Pallas kernels: 14.3 us -> 16.9 us
    all_to_all x2 -> x0, blocking collectives: 44.1 us -> none  [exchange(): return lax.all_to_all(blocks, axes, 0, 0, tiled=False)]
    ppermute x0 -> x5, starting transfers between devices: none -> 23.2 us  [the longest x4 20.8 us: bring(): lax.ppermute(block, 'y', [(i, (i - ahead) % chips) for i in range(chips)])]
    all_to_all x2 -> x3, starting transfers between devices: 12.2 us -> 30.2 us  [exchange(): return lax.all_to_all(blocks, axes, 0, 0, tiled=False)]
    all_to_all x2 -> x3, waiting for transfers between devices: 19.7 us -> 8.88 us  [exchange(): return lax.all_to_all(blocks, axes, 0, 0, tiled=False)]
    ppermute x0 -> x5, waiting for transfers between devices: none -> 9.22 us  [the longest x4 8.2 us: bring(): lax.ppermute(block, 'y', [(i, (i - ahead) % chips) for i in range(chips)])]
    unnamed x16 -> x9, local copies, waits for them, and re-layouts: 7.07 us -> 0.03 us
    pallas_call x3 -> x2, Pallas kernels: 8.68 us -> 12.1 us  [the longest x1 8.39 us: on_device(): call(prepare_kernel, (jax.ShapeDtypeStruct((2, 6, 128, 128), HALF), jax.S...]
    ppermute x1, waiting for transfers between devices: 1.75 us -> 0.01 us  [on_device(): other = lax.ppermute(mine, 'core', [(0, 1), (1, 0)])]
  transfers between devices with their start and end apart: 3 -> 9, of which waited for: 3 -> 7; matrix products, arithmetic and copies ran while one was open for 0% -> 0% of each run, Pallas kernels for 9% -> 10%
where the time goes in v2:
time: 92.7 us; the launch traced here: 92.1 us
  starting transfers between devices  55.4 us (60%)
  waiting for transfers between devices  18.1 us (20%)
  Pallas kernels  16.9 us (18%)
    all_to_all x3, starting transfers between devices, exchange(): return lax.all_to_all(blocks, axes, 0, 0, tiled=False)  30.2 us
    ppermute x4, starting transfers between devices, bring(): lax.ppermute(block, 'y', [(i, (i - ahead) % chips) for i in range(chips)])  20.8 us
    all_to_all x3, waiting for transfers between devices, exchange(): return lax.all_to_all(blocks, axes, 0, 0, tiled=False)  8.88 us
    pallas_call x1, Pallas kernels, on_device(): call(prepare_kernel, (jax.ShapeDtypeStruct((2, 6, 128, 128), HALF), jax.S...  8.39 us
    ppermute x4, waiting for transfers between devices, bring(): lax.ppermute(block, 'y', [(i, (i - ahead) % chips) for i in range(chips)])  8.2 us
    pallas_call x1, Pallas kernels, on_device(): call(finish_kernel, jax.ShapeDtypeStruct((rows, cols), f32), 8 * rows * c...  3.79 us
    pallas_call x1, Pallas kernels, on_device(): call(offer_kernel, (jax.ShapeDtypeStruct((parts, each, cols + 256), HALF)...  3.71 us
    ppermute x1, starting transfers between devices, on_device(): across = lax.ppermute(own, 'core', [(0, 1), (1, 0)])  2.41 us
  transfers between devices with their start and end apart: 9, of which 7 were waited for; matrix products, arithmetic and copies ran while one was open for 0% of the time, Pallas kernels for 10%

profile of v2, /device:TPU:2, one launch (start us, length us, event | category | flops | bytes accessed | tf_op | source)
XLA Modules:
  0.0 92.1 jit_solution(4249256544909811274)
XLA Ops:
  0.0 0.7 add_bitcast_fusion.place_ref
  0.7 3.7 %shard_map.37 = (bf16[32,16,640]{2,1,0:T(8,128)(2,1)}, bf16[32,512]{1,0:T(8,128)(2,1)}) custom-call(s32[1,3]{1,0:T(1,128)} %add_bitcast_fusion.place_ref, s32[1,512]{1,0:T(1,128)} %bitcast.9, f32[512,384]{1,0:T(8,128)} %matrix_ref.1, f32[32,512]{1,0:T(8,128)} %bitcast.12), custom_call_target="tpu_custom_call" | custom-call | flops 201326592 | bytes 1572864 | tf_op jit(solution)/shard_map/pallas_call | solution.py:284
  4.4 0.0 copy-start.3
  4.4 13.5 %all-to-all-start = ((bf16[32,16,640]{2,1,0:T(8,128)(2,1)}), bf16[32,16,640]{2,1,0:T(8,128)(2,1)S(1)}, u32[]{:S(2)}, u32[]{:S(2)}) async-start(bf16[32,16,640]{2,1,0:T(8,128)(2,1)} %get-tuple-element.19), calls=%async_computation | async-start | bytes 1310720 | tf_op jit(solution)/shard_map/all_to_all | solution.py:267
  17.9 0.0 copy-done.3
  17.9 7.7 %collective-permute-start = (bf16[32,512]{1,0:T(8,128)(2,1)S(1)}, bf16[32,512]{1,0:T(8,128)(2,1)S(1)}, u32[]{:S(2)}, u32[]{:S(2)}) collective-permute-start(bf16[32,512]{1,0:T(8,128)(2,1)S(1)} %copy-done.3), channel_id=1, source_target_pairs={{0,8},{2,10},{4,12},{6,14},{8,0},{10,2},{12,4},{14,6},{1,9},{3,11}... | collective-permute-start | bytes 98312 | tf_op jit(solution)/shard_map/ppermute | solution.py:304
  25.6 2.0 %collective-permute-done = bf16[32,512]{1,0:T(8,128)(2,1)S(1)} collective-permute-done((bf16[32,512]{1,0:T(8,128)(2,1)S(1)}, bf16[32,512]{1,0:T(8,128)(2,1)S(1)}, u32[]{:S(2)}, u32[]{:S(2)}) %collective-permute-start) | collective-permute-done | bytes 32800 | tf_op jit(solution)/shard_map/ppermute | solution.py:304
  27.6 6.4 %collective-permute-start.2 = (bf16[64,512]{1,0:T(8,128)(2,1)S(1)}, bf16[64,512]{1,0:T(8,128)(2,1)S(1)}, u32[]{:S(2)}, u32[]{:S(2)}) collective-permute-start(bf16[64,512]{1,0:T(8,128)(2,1)S(1)} %constant_dynamic-update-slice_fusion), channel_id=1, source_target_pairs={{0,12},{2,14},{4,0},{6,2},{8,4},{10,6},{12,8},{14,10},{1,13},{3,15... | collective-permute-start | bytes 196616 | tf_op jit(solution)/shard_map/ppermute | solution.py:304
  34.0 3.3 %collective-permute-start.1 = (bf16[64,512]{1,0:T(8,128)(2,1)S(1)}, bf16[64,512]{1,0:T(8,128)(2,1)S(1)}, u32[]{:S(2)}, u32[]{:S(2)}) collective-permute-start(bf16[64,512]{1,0:T(8,128)(2,1)S(1)} %constant_dynamic-update-slice_fusion), channel_id=1, source_target_pairs={{0,14},{2,0},{4,2},{6,4},{8,6},{10,8},{12,10},{14,12},{1,15},{3,1}... | collective-permute-start | bytes 196616 | tf_op jit(solution)/shard_map/ppermute | solution.py:304
  37.3 0.2 all-to-all-done.got_ref
  37.5 0.0 collective-permute-done.2
  37.5 2.6 %collective-permute-done.1 = bf16[64,512]{1,0:T(8,128)(2,1)S(1)} collective-permute-done((bf16[64,512]{1,0:T(8,128)(2,1)S(1)}, bf16[64,512]{1,0:T(8,128)(2,1)S(1)}, u32[]{:S(2)}, u32[]{:S(2)}) %collective-permute-start.1) | collective-permute-done | bytes 65568 | tf_op jit(solution)/shard_map/ppermute | solution.py:304
  40.2 0.7 broadcast_in_dim.2
  40.9 8.3 %all-to-all-start.1 = ((f16[64,16,128]{2,1,0:T(8,128)(2,1)}), f16[64,16,128]{2,1,0:T(8,128)(2,1)S(1)}, u32[]{:S(2)}, u32[]{:S(2)}) async-start(f16[64,16,128]{2,1,0:T(8,128)(2,1)} %broadcast_in_dim.2), calls=%async_computation.1 | async-start | bytes 524288 | tf_op jit(solution)/shard_map/all_to_all | solution.py:267
  49.2 3.4 %collective-permute-start.3 = (bf16[64,512]{1,0:T(8,128)(2,1)S(1)}, bf16[64,512]{1,0:T(8,128)(2,1)S(1)}, u32[]{:S(2)}, u32[]{:S(2)}) collective-permute-start(bf16[64,512]{1,0:T(8,128)(2,1)S(1)} %constant_dynamic-update-slice_fusion), channel_id=1, source_target_pairs={{0,2},{2,4},{4,6},{6,8},{8,10},{10,12},{12,14},{14,0},{1,3},{3,5},... | collective-permute-start | bytes 196616 | tf_op jit(solution)/shard_map/ppermute | solution.py:304
  52.6 1.0 %shard_map.38 = bf16[32,16,768]{2,1,0:T(8,128)(2,1)} custom-call(bf16[32,16,640]{2,1,0:T(8,128)(2,1)S(1)} %all-to-all-done.got_ref), custom_call_target="tpu_custom_call" | custom-call | flops 196608 | bytes 786432 | tf_op jit(solution)/shard_map/pallas_call | solution.py:314
  53.6 3.6 %collective-permute-done.3 = bf16[64,512]{1,0:T(8,128)(2,1)S(1)} collective-permute-done((bf16[64,512]{1,0:T(8,128)(2,1)S(1)}, bf16[64,512]{1,0:T(8,128)(2,1)S(1)}, u32[]{:S(2)}, u32[]{:S(2)}) %collective-permute-start.3) | collective-permute-done | bytes 65568 | tf_op jit(solution)/shard_map/ppermute | solution.py:304
  57.2 3.6 %all-to-all-done.1 = f16[64,16,128]{2,1,0:T(8,128)(2,1)S(1)} async-done(((f16[64,16,128]{2,1,0:T(8,128)(2,1)}), f16[64,16,128]{2,1,0:T(8,128)(2,1)S(1)}, u32[]{:S(2)}, u32[]{:S(2)}) %all-to-all-start.1) | async-done | bytes 262176 | tf_op jit(solution)/shard_map/all_to_all | solution.py:267
  60.8 8.4 %all-to-all-start.2 = ((bf16[32,16,768]{2,1,0:T(8,128)(2,1)}), bf16[32,16,768]{2,1,0:T(8,128)(2,1)S(1)}, u32[]{:S(2)}, u32[]{:S(2)}) async-start(bf16[32,16,768]{2,1,0:T(8,128)(2,1)} %shard_map.38), calls=%async_computation.2 | async-start | bytes 1572864 | tf_op jit(solution)/shard_map/all_to_all | solution.py:267
  69.2 0.0 copy-start
  69.2 2.1 %collective-permute-start.4 = (f16[64,16,128]{2,1,0:T(8,128)(2,1)S(1)}, f16[64,16,128]{2,1,0:T(8,128)(2,1)S(1)}, u32[]{:S(2)}, u32[]{:S(2)}) collective-permute-start(f16[64,16,128]{2,1,0:T(8,128)(2,1)S(1)} %all-to-all-done.1), channel_id=1, source_target_pairs={{0,1},{1,0},{2,3},{3,2},{4,5},{5,4},{6,7},{7,6},{8,9},{9,8},{10,11... | collective-permute-start | bytes 786440 | tf_op jit(solution)/shard_map/ppermute | solution.py:320
  71.3 2.4 %collective-permute-start.5 = (bf16[256,512]{1,0:T(8,128)(2,1)S(1)}, bf16[256,512]{1,0:T(8,128)(2,1)S(1)}, u32[]{:S(2)}, u32[]{:S(2)}) collective-permute-start(bf16[256,512]{1,0:T(8,128)(2,1)S(1)} %pad_maximum_fusion.own_ref), channel_id=1, source_target_pairs={{0,1},{1,0},{2,3},{3,2},{4,5},{5,4},{6,7},{7,6},{8,9},{9,8},{10,11... | collective-permute-start | bytes 786440 | tf_op jit(solution)/shard_map/ppermute | solution.py:321
  73.7 0.0 copy-start.1
  73.7 0.0 copy-start.2
  73.7 0.0 collective-permute-done.4
  73.8 1.0 %collective-permute-done.5.across_ref = bf16[256,512]{1,0:T(8,128)(2,1)S(1)} collective-permute-done((bf16[256,512]{1,0:T(8,128)(2,1)S(1)}, bf16[256,512]{1,0:T(8,128)(2,1)S(1)}, u32[]{:S(2)}, u32[]{:S(2)}) %collective-permute-start.5) | collective-permute-done | bytes 262176 | tf_op jit(solution)/shard_map/ppermute | solution.py:321
  74.8 0.0 copy-done
  74.8 0.0 copy-done.1
  74.8 0.0 copy-done.2
  74.8 8.4 %shard_map.39 = (bf16[2,6,128,128]{3,2,1,0:T(8,128)(2,1)S(1)}, bf16[2,4,128,128]{3,2,1,0:T(8,128)(2,1)S(1)}, bf16[512,512]{1,0:T(8,128)(2,1)S(1)}, bf16[512,512]{1,0:T(8,128)(2,1)S(1)}, f32[512,384]{1,0:T(8,128)S(1)}) custom-call(s32[1,3]{1,0:T(1,128)S(1)} %copy-done.2, s32[1,512]{1,0:T(1,128)S(1)} %bitcast.10, ...), custom_call_target="tpu_custom_call" | custom-call | flops 1342177280 | bytes 8388608 | tf_op jit(solution)/shard_map/pallas_call | solution.py:323
  83.2 5.1 %all-to-all-done.2.got_ref = bf16[32,16,768]{2,1,0:T(8,128)(2,1)S(1)} async-done(((bf16[32,16,768]{2,1,0:T(8,128)(2,1)}), bf16[32,16,768]{2,1,0:T(8,128)(2,1)S(1)}, u32[]{:S(2)}, u32[]{:S(2)}) %all-to-all-start.2) | async-done | bytes 786464 | tf_op jit(solution)/shard_map/all_to_all | solution.py:267
  88.3 3.8 %shard_map.40 = f32[512,384]{1,0:T(8,128)} custom-call(s32[1,3]{1,0:T(1,128)S(1)} %copy-done.2, s32[1,512]{1,0:T(1,128)S(1)} %bitcast.11, bf16[32,16,768]{2,1,0:T(8,128)(2,1)S(1)} %all-to-all-done.2.got_ref, f32[512,384]{1,0:T(8,128)S(1)} %get-tuple-element.28.kept_ref, bf16[2,6,128,128]{3,2,1,0:T(8,128)(2,1)S(1)} %get-tuple-element.29.below_ref, ...), custom_call_target="tpu_custom_call" | custom-call | flops 805306368 | bytes 9437184 | tf_op jit(solution)/shard_map/pallas_call | solution.py:337
  (6 shorter events, 0.1 us)
Async XLA Ops:
  4.4 13.5 %copy-start.3 = (bf16[32,512]{1,0:T(8,128)(2,1)S(1)}, bf16[32,512]{1,0:T(8,128)(2,1)}, u32[]{:S(2)}) copy-start(bf16[32,512]{1,0:T(8,128)(2,1)} %get-tuple-element.20) | copy-start | bytes 98308
  4.4 33.1 %all-to-all-start = ((bf16[32,16,640]{2,1,0:T(8,128)(2,1)}), bf16[32,16,640]{2,1,0:T(8,128)(2,1)S(1)}, u32[]{:S(2)}, u32[]{:S(2)}) async-start(bf16[32,16,640]{2,1,0:T(8,128)(2,1)} %get-tuple-element.19), calls=%async_computation | async-start | bytes 1310720 | tf_op jit(solution)/shard_map/all_to_all | solution.py:267
  17.9 9.7 %collective-permute-start = (bf16[32,512]{1,0:T(8,128)(2,1)S(1)}, bf16[32,512]{1,0:T(8,128)(2,1)S(1)}, u32[]{:S(2)}, u32[]{:S(2)}) collective-permute-start(bf16[32,512]{1,0:T(8,128)(2,1)S(1)} %copy-done.3), channel_id=1, source_target_pairs={{0,8},{2,10},{4,12},{6,14},{8,0},{10,2},{12,4},{14,6},{1,9},{3,11}... | collective-permute-start | bytes 98312 | tf_op jit(solution)/shard_map/ppermute | solution.py:304
  27.6 9.9 %collective-permute-start.2 = (bf16[64,512]{1,0:T(8,128)(2,1)S(1)}, bf16[64,512]{1,0:T(8,128)(2,1)S(1)}, u32[]{:S(2)}, u32[]{:S(2)}) collective-permute-start(bf16[64,512]{1,0:T(8,128)(2,1)S(1)} %constant_dynamic-update-slice_fusion), channel_id=1, source_target_pairs={{0,12},{2,14},{4,0},{6,2},{8,4},{10,6},{12,8},{14,10},{1,13},{3,15... | collective-permute-start | bytes 196616 | tf_op jit(solution)/shard_map/ppermute | solution.py:304
  34.0 6.2 %collective-permute-start.1 = (bf16[64,512]{1,0:T(8,128)(2,1)S(1)}, bf16[64,512]{1,0:T(8,128)(2,1)S(1)}, u32[]{:S(2)}, u32[]{:S(2)}) collective-permute-start(bf16[64,512]{1,0:T(8,128)(2,1)S(1)} %constant_dynamic-update-slice_fusion), channel_id=1, source_target_pairs={{0,14},{2,0},{4,2},{6,4},{8,6},{10,8},{12,10},{14,12},{1,15},{3,1}... | collective-permute-start | bytes 196616 | tf_op jit(solution)/shard_map/ppermute | solution.py:304
  40.9 19.9 %all-to-all-start.1 = ((f16[64,16,128]{2,1,0:T(8,128)(2,1)}), f16[64,16,128]{2,1,0:T(8,128)(2,1)S(1)}, u32[]{:S(2)}, u32[]{:S(2)}) async-start(f16[64,16,128]{2,1,0:T(8,128)(2,1)} %broadcast_in_dim.2), calls=%async_computation.1 | async-start | bytes 524288 | tf_op jit(solution)/shard_map/all_to_all | solution.py:267
  49.2 7.9 %collective-permute-start.3 = (bf16[64,512]{1,0:T(8,128)(2,1)S(1)}, bf16[64,512]{1,0:T(8,128)(2,1)S(1)}, u32[]{:S(2)}, u32[]{:S(2)}) collective-permute-start(bf16[64,512]{1,0:T(8,128)(2,1)S(1)} %constant_dynamic-update-slice_fusion), channel_id=1, source_target_pairs={{0,2},{2,4},{4,6},{6,8},{8,10},{10,12},{12,14},{14,0},{1,3},{3,5},... | collective-permute-start | bytes 196616 | tf_op jit(solution)/shard_map/ppermute | solution.py:304
  60.8 27.5 %all-to-all-start.2 = ((bf16[32,16,768]{2,1,0:T(8,128)(2,1)}), bf16[32,16,768]{2,1,0:T(8,128)(2,1)S(1)}, u32[]{:S(2)}, u32[]{:S(2)}) async-start(bf16[32,16,768]{2,1,0:T(8,128)(2,1)} %shard_map.38), calls=%async_computation.2 | async-start | bytes 1572864 | tf_op jit(solution)/shard_map/all_to_all | solution.py:267
  69.2 5.6 %copy-start = (f32[512,384]{1,0:T(8,128)S(1)}, f32[512,384]{1,0:T(8,128)}, u32[]{:S(2)}) copy-start(f32[512,384]{1,0:T(8,128)} %matrix_ref.1) | copy-start | bytes 2359300
  69.2 4.5 %collective-permute-start.4 = (f16[64,16,128]{2,1,0:T(8,128)(2,1)S(1)}, f16[64,16,128]{2,1,0:T(8,128)(2,1)S(1)}, u32[]{:S(2)}, u32[]{:S(2)}) collective-permute-start(f16[64,16,128]{2,1,0:T(8,128)(2,1)S(1)} %all-to-all-done.1), channel_id=1, source_target_pairs={{0,1},{1,0},{2,3},{3,2},{4,5},{5,4},{6,7},{7,6},{8,9},{9,8},{10,11... | collective-permute-start | bytes 786440 | tf_op jit(solution)/shard_map/ppermute | solution.py:320
  71.3 3.6 %collective-permute-start.5 = (bf16[256,512]{1,0:T(8,128)(2,1)S(1)}, bf16[256,512]{1,0:T(8,128)(2,1)S(1)}, u32[]{:S(2)}, u32[]{:S(2)}) collective-permute-start(bf16[256,512]{1,0:T(8,128)(2,1)S(1)} %pad_maximum_fusion.own_ref), channel_id=1, source_target_pairs={{0,1},{1,0},{2,3},{3,2},{4,5},{5,4},{6,7},{7,6},{8,9},{9,8},{10,11... | collective-permute-start | bytes 786440 | tf_op jit(solution)/shard_map/ppermute | solution.py:321
  73.7 1.1 %copy-start.1 = (s32[512]{0:T(512)S(1)}, s32[512]{0:T(512)}, u32[]{:S(2)}) copy-start(s32[512]{0:T(512)} %param.5) | copy-start | bytes 6148
  73.7 1.1 %copy-start.2 = (s32[1,3]{1,0:T(1,128)S(1)}, s32[1,3]{1,0:T(1,128)}, u32[]{:S(2)}) copy-start(s32[1,3]{1,0:T(1,128)} %add_bitcast_fusion.place_ref) | copy-start | bytes 40

commit v3 on v2

--- a/solution.py
+++ b/solution.py
@@ -7,7 +7,7 @@
 
 GRID_ROW = ("z", "x")
 SCALE = 65536.0
-ARRIVALS = (0, 4, 1, 5, 2, 6, 7, 3)
+ARRIVALS = (0, 4, 2, 6, 1, 5, 3, 7)
 VMEM_LIMIT = 20 * 1024 * 1024
 VMEM_MOST = 60 * 1024 * 1024
 HALF = jnp.bfloat16
@@ -61,12 +61,12 @@
 
 
 def offer_kernel(
-    place_ref, sources_hbm, matrix_hbm, columns_hbm, out_hbm, own_ref, sources_ref, matrix_ref, columns_ref, out_ref, sems, sent
+    sources_hbm, matrix_hbm, columns_hbm, out_hbm, own_ref, sources_ref, matrix_ref, columns_ref, out_ref, sems, sent
 ):
     rows, cols = matrix_ref.shape
     width = sources_ref.shape[1]
     parts, each, wide = out_ref.shape
-    myself = place_ref[0, 0]
+    myself = grid_row()
     quarter, some = rows // 4, parts // 4
     small = [
         pltpu.make_async_copy(sources_hbm, sources_ref, sems.at[0]),
@@ -86,11 +86,13 @@
     first = columns.astype(HALF).astype(jnp.float32)
     second = columns - first
     holders = columns.shape[0] // 4
-    for part in range(parts):
-        high = 4 * (part % holders)
-        for piece, lane in ((first, cols), (second, cols + 128)):
-            piece = jnp.concatenate([piece[high : high + 4, 128 * q : 128 * q + 128] for q in range(4)], axis=0)
-            out_ref[part, :, lane : lane + 128] = piece.astype(HALF)
+    for holder in range(holders):
+        high = 4 * holder
+        for values, lane in ((first, cols), (second, cols + 128)):
+            piece = jnp.concatenate([values[high : high + 4, 128 * q : 128 * q + 128] for q in range(4)], axis=0)
+            piece = piece.astype(HALF)
+            for part in range(holder, parts, holders):
+                out_ref[part, :, lane : lane + 128] = piece
 
     def send(at):
         here = pl.ds(at * some, some)
@@ -152,24 +154,18 @@
 
 
 def prepare_kernel(
-    place_ref,
-    sources_ref,
     mine_ref,
     other_ref,
     own_ref,
     across_ref,
-    matrix_ref,
     below_ref,
     inverse_ref,
     weights_ref,
-    choose_ref,
-    kept_ref,
     lower_ref,
     gathered_ref,
 ):
-    width = sources_ref.shape[1]
-    core, chip = place_ref[0, 1], place_ref[0, 2]
-    sources = sources_ref[...]
+    width = lower_ref.shape[0]
+    core, chip = lax.axis_index("core"), lax.axis_index("y")
     mine, other = mine_ref[...], other_ref[...]
     pair = (jnp.where(core == 0, mine, other), jnp.where(core == 0, other, mine))
     lines = []
@@ -187,10 +183,6 @@
         gathered_ref[pl.ds(pl.multiple_of(start + 32 * core, 32), 32), :] = own_ref[here, :]
         gathered_ref[pl.ds(pl.multiple_of(start + 32 * (1 - core), 32), 32), :] = across_ref[here, :]
     weights_ref[...] = -jnp.transpose(gathered_ref[...])
-    rows, cols = matrix_ref.shape
-    lands = one_hot(sources - place_ref[0, 0] * rows == iota((rows, width), 0))
-    landed = half_dot(lands, jnp.ones((width, 128), HALF))
-    kept_ref[...] = jnp.where(jnp.concatenate([landed] * (cols // 128), axis=1) > 0.5, 0.0, matrix_ref[...])
 
     count = width // 128
     for block in range(count):
@@ -198,6 +190,15 @@
         inverse_ref[:, block] = in_two(invert_block(lower_ref[here, here]))
         for at in range(block):
             below_ref[:, block * (block - 1) // 2 + at] = in_two(lower_ref[here, 128 * at : 128 * at + 128])
+
+
+def choose_kernel(sources_ref, matrix_ref, choose_ref, kept_ref):
+    width = sources_ref.shape[1]
+    sources = sources_ref[...]
+    rows, cols = matrix_ref.shape
+    lands = one_hot(sources - grid_row() * rows == iota((rows, width), 0))
+    landed = half_dot(lands, jnp.ones((width, 128), HALF))
+    kept_ref[...] = jnp.where(jnp.concatenate([landed] * (cols // 128), axis=1) > 0.5, 0.0, matrix_ref[...])
 
     sources_column = as_column(sources)
     square = (width, width)
@@ -214,11 +215,11 @@
 
 
 def finish_kernel(
-    place_ref, sources_ref, got_ref, kept_ref, below_ref, inverse_ref, weights_ref, choose_ref, out_hbm, out_ref, sems
+    sources_ref, got_ref, kept_ref, below_ref, inverse_ref, weights_ref, choose_ref, out_hbm, out_ref, sems
 ):
     rows, cols = kept_ref.shape
     width = sources_ref.shape[1]
-    myself = place_ref[0, 0]
+    myself = grid_row()
     sources = sources_ref[...]
     moved = half_dot(choose_ref[...], got_ref[:, :, cols : 2 * cols].reshape(width, cols))
     found = got_ref[:, :, 0:cols].reshape(width, cols).astype(jnp.float32)
@@ -274,11 +275,9 @@
     chips = lax.axis_size("y")
     each = width // parts
     f32 = jnp.float32
-    row = grid_row().astype(jnp.int32)
-    place = jnp.stack([row, lax.axis_index("core"), lax.axis_index("y")]).reshape(1, 3).astype(jnp.int32)
     sources = sources.reshape(1, width)
     columns = panel.T
-    smem, vmem = pl.BlockSpec(memory_space=pltpu.SMEM), pl.BlockSpec(memory_space=pltpu.VMEM)
+    vmem = pl.BlockSpec(memory_space=pltpu.VMEM)
     hbm = pl.BlockSpec(memory_space=pltpu.HBM)
 
     offer, own = call(
@@ -287,7 +286,7 @@
         2 * width * rows * cols,
         2 * rows * cols * 4,
         limit=VMEM_MOST,
-        in_specs=[smem, hbm, hbm, hbm],
+        in_specs=[hbm, hbm, hbm],
         out_specs=[hbm, vmem],
         scratch_shapes=[
             pltpu.VMEM((1, width), jnp.int32),
@@ -297,52 +296,56 @@
             pltpu.SemaphoreType.DMA((6,)),
             pltpu.SemaphoreType.DMA((4,)),
         ],
-    )(place, sources, matrix, columns)
+    )(sources, matrix, columns)
     got = exchange(offer, GRID_ROW)
+
+    choose, kept = call(
+        choose_kernel,
+        (jax.ShapeDtypeStruct((width, width), HALF), jax.ShapeDtypeStruct((rows, cols), f32)),
+        4 * width * width * width,
+        4 * rows * cols * 4,
+    )(sources, matrix)
 
     def bring(block, ahead):
         return lax.ppermute(block, "y", [(i, (i - ahead) % chips) for i in range(chips)])
 
     own = jnp.concatenate([own, bring(own, 4)], axis=0)
-    came = [bring(own, 1), bring(own, 2), bring(own, 7)]
+    own = jnp.concatenate([own, bring(own, 2)], axis=0)
 
     piece = got[0, :, cols : cols + 128].astype(f32) + got[0, :, cols + 128 : cols + 256].astype(f32)
     piece = (piece * SCALE).astype(jnp.float16)
-    piece, own, came[0], came[1] = lax.optimization_barrier((piece, own, came[0], came[1]))
+    piece, own, choose, kept = lax.optimization_barrier((piece, own, choose, kept))
     mine = exchange(everyone(piece, 8 * chips), ("x", "y"))
 
     collected = call(
         collect_kernel, jax.ShapeDtypeStruct((parts, each, 2 * cols), HALF), parts * each * cols, 4 * parts * each * cols
     )(got)
-    own = jnp.concatenate([own] + came, axis=0)
+    own = jnp.concatenate([own, bring(own, 1)], axis=0)
     collected, mine, own = lax.optimization_barrier((collected, mine, own))
     arrived = exchange(collected, GRID_ROW)
     other = lax.ppermute(mine, "core", [(0, 1), (1, 0)])
     across = lax.ppermute(own, "core", [(0, 1), (1, 0)])
 
-    below, inverse, weights, choose, kept = call(
+    below, inverse, weights = call(
         prepare_kernel,
         (
             jax.ShapeDtypeStruct((2, 6, 128, 128), HALF),
             jax.ShapeDtypeStruct((2, 4, 128, 128), HALF),
             jax.ShapeDtypeStruct((rows, width), HALF),
-            jax.ShapeDtypeStruct((width, width), HALF),
-            jax.ShapeDtypeStruct((rows, cols), f32),
         ),
         10 * width * width * width,
         8 * width * width * 4,
-        in_specs=[smem] + [vmem] * 6,
         scratch_shapes=[pltpu.VMEM((width, width), f32), pltpu.VMEM((width, rows), HALF)],
-    )(place, sources, mine.astype(f32), other.astype(f32), own, across, matrix)
+    )(mine.astype(f32), other.astype(f32), own, across)
     return call(
         finish_kernel,
         jax.ShapeDtypeStruct((rows, cols), f32),
         8 * rows * cols * width,
         12 * rows * cols * 4,
-        in_specs=[smem] + [vmem] * 7,
+        in_specs=[vmem] * 7,
         out_specs=hbm,
         scratch_shapes=[pltpu.VMEM((rows, cols), f32), pltpu.SemaphoreType.DMA((4,))],
-    )(place, sources, arrived, kept, below, inverse, weights, choose)
+    )(sources, arrived, kept, below, inverse, weights, choose)
 
 
 def solution(mesh):

time: 92.7 us -> 89.4 us (0.964)
  Pallas kernels: 16.9 us -> 15.7 us
  waiting for transfers between devices: 18.1 us -> 17.1 us
    ppermute x4 -> x3, starting transfers between devices: 20.8 us -> 18.7 us  [bring(): lax.ppermute(block, 'y', [(i, (i - ahead) % chips) for i in range(chips)])]
    ppermute x4 -> x3, waiting for transfers between devices: 8.2 us -> 6.17 us  [bring(): lax.ppermute(block, 'y', [(i, (i - ahead) % chips) for i in range(chips)])]
    all_to_all x3, starting transfers between devices: 30.2 us -> 32 us  [exchange(): return lax.all_to_all(blocks, axes, 0, 0, tiled=False)]
    pallas_call x1, Pallas kernels: 8.39 us -> 7.22 us  [on_device(): call(prepare_kernel, (jax.ShapeDtypeStruct((2, 6, 128, 128), HALF), jax.S...]
    pallas_call x0 -> x1, Pallas kernels: none -> 1.14 us  [on_device(): call(choose_kernel, (jax.ShapeDtypeStruct((width, width), HALF), jax.Shap...]
    all_to_all x3, waiting for transfers between devices: 8.88 us -> 9.86 us  [exchange(): return lax.all_to_all(blocks, axes, 0, 0, tiled=False)]
  transfers between devices with their start and end apart: 9 -> 8, of which waited for: 7 -> 7; matrix products, arithmetic and copies ran while one was open for 0% -> 0% of each run, Pallas kernels for 10% -> 11%
where the time goes in v3:
time: 89.4 us; the launch traced here: 88.8 us
  starting transfers between devices  55.1 us (62%)
  waiting for transfers between devices  17.1 us (19%)
  Pallas kernels  15.7 us (18%)
    all_to_all x3, starting transfers between devices, exchange(): return lax.all_to_all(blocks, axes, 0, 0, tiled=False)  32 us
    ppermute x3, starting transfers between devices, bring(): lax.ppermute(block, 'y', [(i, (i - ahead) % chips) for i in range(chips)])  18.7 us
    all_to_all x3, waiting for transfers between devices, exchange(): return lax.all_to_all(blocks, axes, 0, 0, tiled=False)  9.86 us
    pallas_call x1, Pallas kernels, on_device(): call(prepare_kernel, (jax.ShapeDtypeStruct((2, 6, 128, 128), HALF), jax.S...  7.22 us
    ppermute x3, waiting for transfers between devices, bring(): lax.ppermute(block, 'y', [(i, (i - ahead) % chips) for i in range(chips)])  6.17 us
    pallas_call x1, Pallas kernels, on_device(): call(finish_kernel, jax.ShapeDtypeStruct((rows, cols), f32), 8 * rows * c...  3.27 us
    pallas_call x1, Pallas kernels, on_device(): call(offer_kernel, (jax.ShapeDtypeStruct((parts, each, cols + 256), HALF)...  3.05 us
    ppermute x1, starting transfers between devices, on_device(): across = lax.ppermute(own, 'core', [(0, 1), (1, 0)])  2.41 us
  transfers between devices with their start and end apart: 8, of which 7 were waited for; matrix products, arithmetic and copies ran while one was open for 0% of the time, Pallas kernels for 11%

profile of v3, /device:TPU:2, one launch (start us, length us, event | category | flops | bytes accessed | tf_op | source)
XLA Modules:
  0.0 88.8 jit_solution(18095540710933681082)
XLA Ops:
  0.0 3.1 %shard_map.37 = (bf16[32,16,640]{2,1,0:T(8,128)(2,1)}, bf16[32,512]{1,0:T(8,128)(2,1)}) custom-call(s32[1,512]{1,0:T(1,128)} %bitcast.4, f32[512,384]{1,0:T(8,128)} %matrix_ref.1, f32[32,512]{1,0:T(8,128)} %bitcast.7), custom_call_target="tpu_custom_call" | custom-call | flops 201326592 | bytes 1572864 | tf_op jit(solution)/shard_map/pallas_call | solution.py:283
  3.1 0.0 copy-start
  3.1 0.0 copy-start.2
  3.1 13.6 %all-to-all-start = ((bf16[32,16,640]{2,1,0:T(8,128)(2,1)}), bf16[32,16,640]{2,1,0:T(8,128)(2,1)S(1)}, u32[]{:S(2)}, u32[]{:S(2)}) async-start(bf16[32,16,640]{2,1,0:T(8,128)(2,1)} %get-tuple-element.19), calls=%async_computation | async-start | bytes 1310720 | tf_op jit(solution)/shard_map/all_to_all | solution.py:268
  16.7 0.0 copy-done.2
  16.7 0.0 copy-start.1
  16.7 7.7 %collective-permute-start = (bf16[32,512]{1,0:T(8,128)(2,1)S(1)}, bf16[32,512]{1,0:T(8,128)(2,1)S(1)}, u32[]{:S(2)}, u32[]{:S(2)}) collective-permute-start(bf16[32,512]{1,0:T(8,128)(2,1)S(1)} %copy-done.2), channel_id=1, source_target_pairs={{0,8},{2,10},{4,12},{6,14},{8,0},{10,2},{12,4},{14,6},{1,9},{3,11}... | collective-permute-start | bytes 98312 | tf_op jit(solution)/shard_map/ppermute | solution.py:310
  24.5 2.0 %collective-permute-done = bf16[32,512]{1,0:T(8,128)(2,1)S(1)} collective-permute-done((bf16[32,512]{1,0:T(8,128)(2,1)S(1)}, bf16[32,512]{1,0:T(8,128)(2,1)S(1)}, u32[]{:S(2)}, u32[]{:S(2)}) %collective-permute-start) | collective-permute-done | bytes 32800 | tf_op jit(solution)/shard_map/ppermute | solution.py:310
  26.5 6.4 %collective-permute-start.1 = (bf16[64,512]{1,0:T(8,128)(2,1)S(1)}, bf16[64,512]{1,0:T(8,128)(2,1)S(1)}, u32[]{:S(2)}, u32[]{:S(2)}) collective-permute-start(bf16[64,512]{1,0:T(8,128)(2,1)S(1)} %pad_maximum_fusion.2), channel_id=1, source_target_pairs={{0,12},{2,14},{4,0},{6,2},{8,4},{10,6},{12,8},{14,10},{1,13},{3,15... | collective-permute-start | bytes 196616 | tf_op jit(solution)/shard_map/ppermute | solution.py:310
  32.8 0.0 copy-done
  32.9 0.0 copy-done.1
  32.9 1.1 %shard_map.39 = (bf16[512,512]{1,0:T(8,128)(2,1)S(1)}, f32[512,384]{1,0:T(8,128)S(1)}) custom-call(s32[1,512]{1,0:T(1,128)S(1)} %bitcast.5, f32[512,384]{1,0:T(8,128)S(1)} %copy-done), custom_call_target="tpu_custom_call" | custom-call | flops 536870912 | bytes 3145728 | tf_op jit(solution)/shard_map/pallas_call | solution.py:302
  34.0 1.3 %collective-permute-done.1 = bf16[64,512]{1,0:T(8,128)(2,1)S(1)} collective-permute-done((bf16[64,512]{1,0:T(8,128)(2,1)S(1)}, bf16[64,512]{1,0:T(8,128)(2,1)S(1)}, u32[]{:S(2)}, u32[]{:S(2)}) %collective-permute-start.1) | collective-permute-done | bytes 65568 | tf_op jit(solution)/shard_map/ppermute | solution.py:310
  35.4 1.0 %all-to-all-done.got_ref = bf16[32,16,640]{2,1,0:T(8,128)(2,1)S(1)} async-done(((bf16[32,16,640]{2,1,0:T(8,128)(2,1)}), bf16[32,16,640]{2,1,0:T(8,128)(2,1)S(1)}, u32[]{:S(2)}, u32[]{:S(2)}) %all-to-all-start) | async-done | bytes 655392 | tf_op jit(solution)/shard_map/all_to_all | solution.py:268
  36.3 0.7 broadcast_in_dim.2
  37.1 10.7 %all-to-all-start.1 = ((f16[64,16,128]{2,1,0:T(8,128)(2,1)}), f16[64,16,128]{2,1,0:T(8,128)(2,1)S(1)}, u32[]{:S(2)}, u32[]{:S(2)}) async-start(f16[64,16,128]{2,1,0:T(8,128)(2,1)} %broadcast_in_dim.2), calls=%async_computation.1 | async-start | bytes 524288 | tf_op jit(solution)/shard_map/all_to_all | solution.py:268
  47.7 4.6 %collective-permute-start.2 = (bf16[128,512]{1,0:T(8,128)(2,1)S(1)}, bf16[128,512]{1,0:T(8,128)(2,1)S(1)}, u32[]{:S(2)}, u32[]{:S(2)}) collective-permute-start(bf16[128,512]{1,0:T(8,128)(2,1)S(1)} %pad_maximum_fusion.1), channel_id=1, source_target_pairs={{0,14},{2,0},{4,2},{6,4},{8,6},{10,8},{12,10},{14,12},{1,15},{3,1}... | collective-permute-start | bytes 393224 | tf_op jit(solution)/shard_map/ppermute | solution.py:310
  52.3 1.0 %shard_map.38 = bf16[32,16,768]{2,1,0:T(8,128)(2,1)} custom-call(bf16[32,16,640]{2,1,0:T(8,128)(2,1)S(1)} %all-to-all-done.got_ref), custom_call_target="tpu_custom_call" | custom-call | flops 196608 | bytes 786432 | tf_op jit(solution)/shard_map/pallas_call | solution.py:320
  53.3 2.8 %collective-permute-done.2 = bf16[128,512]{1,0:T(8,128)(2,1)S(1)} collective-permute-done((bf16[128,512]{1,0:T(8,128)(2,1)S(1)}, bf16[128,512]{1,0:T(8,128)(2,1)S(1)}, u32[]{:S(2)}, u32[]{:S(2)}) %collective-permute-start.2) | collective-permute-done | bytes 131104 | tf_op jit(solution)/shard_map/ppermute | solution.py:310
  56.2 2.7 %all-to-all-done.1 = f16[64,16,128]{2,1,0:T(8,128)(2,1)S(1)} async-done(((f16[64,16,128]{2,1,0:T(8,128)(2,1)}), f16[64,16,128]{2,1,0:T(8,128)(2,1)S(1)}, u32[]{:S(2)}, u32[]{:S(2)}) %all-to-all-start.1) | async-done | bytes 262176 | tf_op jit(solution)/shard_map/all_to_all | solution.py:268
  58.8 7.8 %all-to-all-start.2 = ((bf16[32,16,768]{2,1,0:T(8,128)(2,1)}), bf16[32,16,768]{2,1,0:T(8,128)(2,1)S(1)}, u32[]{:S(2)}, u32[]{:S(2)}) async-start(bf16[32,16,768]{2,1,0:T(8,128)(2,1)} %shard_map.38), calls=%async_computation.2 | async-start | bytes 1572864 | tf_op jit(solution)/shard_map/all_to_all | solution.py:268
  66.6 1.9 %collective-permute-start.3 = (f16[64,16,128]{2,1,0:T(8,128)(2,1)S(1)}, f16[64,16,128]{2,1,0:T(8,128)(2,1)S(1)}, u32[]{:S(2)}, u32[]{:S(2)}) collective-permute-start(f16[64,16,128]{2,1,0:T(8,128)(2,1)S(1)} %all-to-all-done.1), channel_id=1, source_target_pairs={{0,1},{1,0},{2,3},{3,2},{4,5},{5,4},{6,7},{7,6},{8,9},{9,8},{10,11... | collective-permute-start | bytes 786440 | tf_op jit(solution)/shard_map/ppermute | solution.py:326
  68.5 2.4 %collective-permute-start.4 = (bf16[256,512]{1,0:T(8,128)(2,1)S(1)}, bf16[256,512]{1,0:T(8,128)(2,1)S(1)}, u32[]{:S(2)}, u32[]{:S(2)}) collective-permute-start(bf16[256,512]{1,0:T(8,128)(2,1)S(1)} %pad_maximum_fusion.own_ref), channel_id=1, source_target_pairs={{0,1},{1,0},{2,3},{3,2},{4,5},{5,4},{6,7},{7,6},{8,9},{9,8},{10,11... | collective-permute-start | bytes 786440 | tf_op jit(solution)/shard_map/ppermute | solution.py:327
  71.0 0.0 collective-permute-done.3
  71.1 1.0 %collective-permute-done.4.across_ref = bf16[256,512]{1,0:T(8,128)(2,1)S(1)} collective-permute-done((bf16[256,512]{1,0:T(8,128)(2,1)S(1)}, bf16[256,512]{1,0:T(8,128)(2,1)S(1)}, u32[]{:S(2)}, u32[]{:S(2)}) %collective-permute-start.4) | collective-permute-done | bytes 262176 | tf_op jit(solution)/shard_map/ppermute | solution.py:327
  72.1 7.2 %shard_map.40 = (bf16[2,6,128,128]{3,2,1,0:T(8,128)(2,1)S(1)}, bf16[2,4,128,128]{3,2,1,0:T(8,128)(2,1)S(1)}, bf16[512,512]{1,0:T(8,128)(2,1)S(1)}) custom-call(f32[64,16,128]{2,1,0:T(8,128)S(1)} %convert_element_type.24.mine_ref, f32[64,16,128]{2,1,0:T(8,128)S(1)} %convert_element_type.25.other_ref, bf16[256,512]{1,0:T(8,128)(2,1)S(1)} %pad_maximum_fusion.own_ref, ...), custom_call_target="tpu_custom_call" | custom-call | flops 1342177280 | bytes 8388608 | tf_op jit(solution)/shard_map/pallas_call | solution.py:329
  79.3 6.2 %all-to-all-done.2.got_ref = bf16[32,16,768]{2,1,0:T(8,128)(2,1)S(1)} async-done(((bf16[32,16,768]{2,1,0:T(8,128)(2,1)}), bf16[32,16,768]{2,1,0:T(8,128)(2,1)S(1)}, u32[]{:S(2)}, u32[]{:S(2)}) %all-to-all-start.2) | async-done | bytes 786464 | tf_op jit(solution)/shard_map/all_to_all | solution.py:268
  85.6 3.3 %shard_map.41 = f32[512,384]{1,0:T(8,128)} custom-call(s32[1,512]{1,0:T(1,128)S(1)} %bitcast.6, bf16[32,16,768]{2,1,0:T(8,128)(2,1)S(1)} %all-to-all-done.2.got_ref, f32[512,384]{1,0:T(8,128)S(1)} %get-tuple-element.26.kept_ref, bf16[2,6,128,128]{3,2,1,0:T(8,128)(2,1)S(1)} %get-tuple-element.29.below_ref, ...), custom_call_target="tpu_custom_call" | custom-call | flops 805306368 | bytes 9437184 | tf_op jit(solution)/shard_map/pallas_call | solution.py:340
  (6 shorter events, 0.1 us)
Async XLA Ops:
  3.1 29.8 %copy-start = (f32[512,384]{1,0:T(8,128)S(1)}, f32[512,384]{1,0:T(8,128)}, u32[]{:S(2)}) copy-start(f32[512,384]{1,0:T(8,128)} %matrix_ref.1) | copy-start | bytes 2359300
  3.1 13.6 %copy-start.2 = (bf16[32,512]{1,0:T(8,128)(2,1)S(1)}, bf16[32,512]{1,0:T(8,128)(2,1)}, u32[]{:S(2)}) copy-start(bf16[32,512]{1,0:T(8,128)(2,1)} %get-tuple-element.20) | copy-start | bytes 98308
  3.1 33.3 %all-to-all-start = ((bf16[32,16,640]{2,1,0:T(8,128)(2,1)}), bf16[32,16,640]{2,1,0:T(8,128)(2,1)S(1)}, u32[]{:S(2)}, u32[]{:S(2)}) async-start(bf16[32,16,640]{2,1,0:T(8,128)(2,1)} %get-tuple-element.19), calls=%async_computation | async-start | bytes 1310720 | tf_op jit(solution)/shard_map/all_to_all | solution.py:268
  16.7 16.2 %copy-start.1 = (s32[512]{0:T(512)S(1)}, s32[512]{0:T(512)}, u32[]{:S(2)}) copy-start(s32[512]{0:T(512)} %param.5) | copy-start | bytes 6148
  16.7 9.7 %collective-permute-start = (bf16[32,512]{1,0:T(8,128)(2,1)S(1)}, bf16[32,512]{1,0:T(8,128)(2,1)S(1)}, u32[]{:S(2)}, u32[]{:S(2)}) collective-permute-start(bf16[32,512]{1,0:T(8,128)(2,1)S(1)} %copy-done.2), channel_id=1, source_target_pairs={{0,8},{2,10},{4,12},{6,14},{8,0},{10,2},{12,4},{14,6},{1,9},{3,11}... | collective-permute-start | bytes 98312 | tf_op jit(solution)/shard_map/ppermute | solution.py:310
  26.5 8.9 %collective-permute-start.1 = (bf16[64,512]{1,0:T(8,128)(2,1)S(1)}, bf16[64,512]{1,0:T(8,128)(2,1)S(1)}, u32[]{:S(2)}, u32[]{:S(2)}) collective-permute-start(bf16[64,512]{1,0:T(8,128)(2,1)S(1)} %pad_maximum_fusion.2), channel_id=1, source_target_pairs={{0,12},{2,14},{4,0},{6,2},{8,4},{10,6},{12,8},{14,10},{1,13},{3,15... | collective-permute-start | bytes 196616 | tf_op jit(solution)/shard_map/ppermute | solution.py:310
  37.1 21.8 %all-to-all-start.1 = ((f16[64,16,128]{2,1,0:T(8,128)(2,1)}), f16[64,16,128]{2,1,0:T(8,128)(2,1)S(1)}, u32[]{:S(2)}, u32[]{:S(2)}) async-start(f16[64,16,128]{2,1,0:T(8,128)(2,1)} %broadcast_in_dim.2), calls=%async_computation.1 | async-start | bytes 524288 | tf_op jit(solution)/shard_map/all_to_all | solution.py:268
  47.7 8.4 %collective-permute-start.2 = (bf16[128,512]{1,0:T(8,128)(2,1)S(1)}, bf16[128,512]{1,0:T(8,128)(2,1)S(1)}, u32[]{:S(2)}, u32[]{:S(2)}) collective-permute-start(bf16[128,512]{1,0:T(8,128)(2,1)S(1)} %pad_maximum_fusion.1), channel_id=1, source_target_pairs={{0,14},{2,0},{4,2},{6,4},{8,6},{10,8},{12,10},{14,12},{1,15},{3,1}... | collective-permute-start | bytes 393224 | tf_op jit(solution)/shard_map/ppermute | solution.py:310
  58.8 26.7 %all-to-all-start.2 = ((bf16[32,16,768]{2,1,0:T(8,128)(2,1)}), bf16[32,16,768]{2,1,0:T(8,128)(2,1)S(1)}, u32[]{:S(2)}, u32[]{:S(2)}) async-start(bf16[32,16,768]{2,1,0:T(8,128)(2,1)} %shard_map.38), calls=%async_computation.2 | async-start | bytes 1572864 | tf_op jit(solution)/shard_map/all_to_all | solution.py:268
  66.6 4.4 %collective-permute-start.3 = (f16[64,16,128]{2,1,0:T(8,128)(2,1)S(1)}, f16[64,16,128]{2,1,0:T(8,128)(2,1)S(1)}, u32[]{:S(2)}, u32[]{:S(2)}) collective-permute-start(f16[64,16,128]{2,1,0:T(8,128)(2,1)S(1)} %all-to-all-done.1), channel_id=1, source_target_pairs={{0,1},{1,0},{2,3},{3,2},{4,5},{5,4},{6,7},{7,6},{8,9},{9,8},{10,11... | collective-permute-start | bytes 786440 | tf_op jit(solution)/shard_map/ppermute | solution.py:326
  68.5 3.6 %collective-permute-start.4 = (bf16[256,512]{1,0:T(8,128)(2,1)S(1)}, bf16[256,512]{1,0:T(8,128)(2,1)S(1)}, u32[]{:S(2)}, u32[]{:S(2)}) collective-permute-start(bf16[256,512]{1,0:T(8,128)(2,1)S(1)} %pad_maximum_fusion.own_ref), channel_id=1, source_target_pairs={{0,1},{1,0},{2,3},{3,2},{4,5},{5,4},{6,7},{7,6},{8,9},{9,8},{10,11... | collective-permute-start | bytes 786440 | tf_op jit(solution)/shard_map/ppermute | solution.py:327

commit v4 on v3

--- a/solution.py
+++ b/solution.py
@@ -8,19 +8,23 @@
 GRID_ROW = ("z", "x")
 SCALE = 65536.0
 ARRIVALS = (0, 4, 2, 6, 1, 5, 3, 7)
+STEPS = ((0, 1, 0), (0, 2, 1), (0, 3, 2), (1, 2, 3), (1, 3, 4), (2, 3, 5))
 VMEM_LIMIT = 20 * 1024 * 1024
-VMEM_MOST = 60 * 1024 * 1024
 HALF = jnp.bfloat16
 
 
-def call(kernel, out_shape, flops, moved, limit=VMEM_LIMIT, **more):
+def call(kernel, out_shape, flops, moved, **more):
     return pl.pallas_call(
         kernel,
         out_shape=out_shape,
         **more,
-        compiler_params=pltpu.CompilerParams(vmem_limit_bytes=limit),
+        compiler_params=pltpu.CompilerParams(vmem_limit_bytes=VMEM_LIMIT),
         cost_estimate=pl.CostEstimate(flops=flops, bytes_accessed=moved, transcendentals=0),
     )
+
+
+def in_hbm(array):
+    return pltpu.with_memory_space_constraint(array, pltpu.HBM)
 
 
 def grid_row():
@@ -185,11 +189,14 @@
     weights_ref[...] = -jnp.transpose(gathered_ref[...])
 
     count = width // 128
+    inverses = []
     for block in range(count):
         here = slice(128 * block, 128 * block + 128)
-        inverse_ref[:, block] = in_two(invert_block(lower_ref[here, here]))
-        for at in range(block):
-            below_ref[:, block * (block - 1) // 2 + at] = in_two(lower_ref[here, 128 * at : 128 * at + 128])
+        inverses.append(invert_block(lower_ref[here, here]))
+        inverse_ref[:, block] = in_two(inverses[block])
+    for at, block, place in STEPS:
+        here = slice(128 * block, 128 * block + 128)
+        below_ref[:, place] = in_two(-exact_dot(inverses[block], lower_ref[here, 128 * at : 128 * at + 128]))
 
 
 def choose_kernel(sources_ref, matrix_ref, choose_ref, kept_ref):
@@ -224,13 +231,17 @@
     moved = half_dot(choose_ref[...], got_ref[:, :, cols : 2 * cols].reshape(width, cols))
     found = got_ref[:, :, 0:cols].reshape(width, cols).astype(jnp.float32)
     pivots = jnp.where(as_column(sources) >= width, found, moved)
+    count = width // 128
     upper = []
-    for block in range(width // 128):
-        here = slice(128 * block, 128 * block + 128)
-        right = pivots[here]
-        for at in range(block):
-            right = right - split_dot(below_ref[:, block * (block - 1) // 2 + at], upper[at])
-        upper.append(split_dot(inverse_ref[:, block], right))
+    for block in range(count):
+        upper.append(split_dot(inverse_ref[:, block], pivots[128 * block : 128 * block + 128]))
+    first = 0
+    for at in range(count - 1):
+        more = count - 1 - at
+        change = split_dot(below_ref[:, first : first + more].reshape(2, 128 * more, 128), upper[at])
+        for block in range(more):
+            upper[at + 1 + block] = upper[at + 1 + block] + change[128 * block : 128 * block + 128]
+        first += more
     upper = jnp.concatenate(upper, axis=0)
 
     quarter = rows // 4
@@ -285,7 +296,6 @@
         (jax.ShapeDtypeStruct((parts, each, cols + 256), HALF), jax.ShapeDtypeStruct(columns.shape, HALF)),
         2 * width * rows * cols,
         2 * rows * cols * 4,
-        limit=VMEM_MOST,
         in_specs=[hbm, hbm, hbm],
         out_specs=[hbm, vmem],
         scratch_shapes=[
@@ -296,7 +306,7 @@
             pltpu.SemaphoreType.DMA((6,)),
             pltpu.SemaphoreType.DMA((4,)),
         ],
-    )(sources, matrix, columns)
+    )(in_hbm(sources), in_hbm(matrix), in_hbm(columns))
     got = exchange(offer, GRID_ROW)
 
     choose, kept = call(
@@ -310,18 +320,20 @@
         return lax.ppermute(block, "y", [(i, (i - ahead) % chips) for i in range(chips)])
 
     own = jnp.concatenate([own, bring(own, 4)], axis=0)
-    own = jnp.concatenate([own, bring(own, 2)], axis=0)
+    came = bring(own, 2)
 
     piece = got[0, :, cols : cols + 128].astype(f32) + got[0, :, cols + 128 : cols + 256].astype(f32)
     piece = (piece * SCALE).astype(jnp.float16)
-    piece, own, choose, kept = lax.optimization_barrier((piece, own, choose, kept))
+    piece, came, choose, kept = lax.optimization_barrier((piece, came, choose, kept))
     mine = exchange(everyone(piece, 8 * chips), ("x", "y"))
 
     collected = call(
         collect_kernel, jax.ShapeDtypeStruct((parts, each, 2 * cols), HALF), parts * each * cols, 4 * parts * each * cols
     )(got)
-    own = jnp.concatenate([own, bring(own, 1)], axis=0)
-    collected, mine, own = lax.optimization_barrier((collected, mine, own))
+    own = jnp.concatenate([own, came], axis=0)
+    came = bring(own, 1)
+    collected, mine, came = lax.optimization_barrier((collected, mine, came))
+    own = jnp.concatenate([own, came], axis=0)
     arrived = exchange(collected, GRID_ROW)
     other = lax.ppermute(mine, "core", [(0, 1), (1, 0)])
     across = lax.ppermute(own, "core", [(0, 1), (1, 0)])

time: 89.4 us -> 88.2 us (0.987)
    ppermute x3, waiting for transfers between devices: 6.17 us -> 3.65 us  [bring(): lax.ppermute(block, 'y', [(i, (i - ahead) % chips) for i in range(chips)])]
    all_to_all x3, waiting for transfers between devices: 9.86 us -> 12 us  [exchange(): return lax.all_to_all(blocks, axes, 0, 0, tiled=False)]
  transfers between devices with their start and end apart: 8 -> 8, of which waited for: 7 -> 6; matrix products, arithmetic and copies ran while one was open for 0% -> 0% of each run, Pallas kernels for 11% -> 11%
where the time goes in v4:
time: 88.2 us; the launch traced here: 87.7 us
  starting transfers between devices  55 us (62%)
  waiting for transfers between devices  16.7 us (19%)
  Pallas kernels  14.9 us (17%)
    all_to_all x3, starting transfers between devices, exchange(): return lax.all_to_all(blocks, axes, 0, 0, tiled=False)  32 us
    ppermute x3, starting transfers between devices, bring(): lax.ppermute(block, 'y', [(i, (i - ahead) % chips) for i in range(chips)])  18.7 us
    all_to_all x3, waiting for transfers between devices, exchange(): return lax.all_to_all(blocks, axes, 0, 0, tiled=False)  12 us
    pallas_call x1, Pallas kernels, on_device(): call(prepare_kernel, (jax.ShapeDtypeStruct((2, 6, 128, 128), HALF), jax.S...  7.56 us
    ppermute x3, waiting for transfers between devices, bring(): lax.ppermute(block, 'y', [(i, (i - ahead) % chips) for i in range(chips)])  3.65 us
    pallas_call x1, Pallas kernels, on_device(): call(finish_kernel, jax.ShapeDtypeStruct((rows, cols), f32), 8 * rows * c...  2.79 us
    pallas_call x1, Pallas kernels, on_device(): call(offer_kernel, (jax.ShapeDtypeStruct((parts, each, cols + 256), HALF)...  2.44 us
    ppermute x1, starting transfers between devices, on_device(): across = lax.ppermute(own, 'core', [(0, 1), (1, 0)])  2.41 us
  transfers between devices with their start and end apart: 8, of which 6 were waited for; matrix products, arithmetic and copies ran while one was open for 0% of the time, Pallas kernels for 11%

profile of v4, /device:TPU:2, one launch (start us, length us, event | category | flops | bytes accessed | tf_op | source)
XLA Modules:
  0.0 87.7 jit_solution(13849547466612780432)
XLA Ops:
  0.0 2.4 %shard_map.37 = (bf16[32,16,640]{2,1,0:T(8,128)(2,1)}, bf16[32,512]{1,0:T(8,128)(2,1)S(1)}) custom-call(s32[1,512]{1,0:T(1,128)} %bitcast.4, f32[512,384]{1,0:T(8,128)} %matrix_ref.1, f32[32,512]{1,0:T(8,128)} %bitcast.7), custom_call_target="tpu_custom_call" | custom-call | flops 201326592 | bytes 1572864 | tf_op jit(solution)/shard_map/pallas_call | solution.py:294
  2.5 0.0 copy-start
  2.5 0.0 copy-start.1
  2.5 13.6 %all-to-all-start = ((bf16[32,16,640]{2,1,0:T(8,128)(2,1)}), bf16[32,16,640]{2,1,0:T(8,128)(2,1)S(1)}, u32[]{:S(2)}, u32[]{:S(2)}) async-start(bf16[32,16,640]{2,1,0:T(8,128)(2,1)} %get-tuple-element.19), calls=%async_computation | async-start | bytes 1310720 | tf_op jit(solution)/shard_map/all_to_all | solution.py:279
  16.1 7.7 %collective-permute-start = (bf16[32,512]{1,0:T(8,128)(2,1)S(1)}, bf16[32,512]{1,0:T(8,128)(2,1)S(1)}, u32[]{:S(2)}, u32[]{:S(2)}) collective-permute-start(bf16[32,512]{1,0:T(8,128)(2,1)S(1)} %get-tuple-element.20), channel_id=1, source_target_pairs={{0,8},{2,10},{4,12},{6,14},{8,0},{10,2},{12,4},{14,6},{1,9},{3,11}... | collective-permute-start | bytes 98312 | tf_op jit(solution)/shard_map/ppermute | solution.py:320
  23.8 0.0 copy-done
  23.8 0.0 copy-done.1
  23.9 1.1 %shard_map.39 = (bf16[512,512]{1,0:T(8,128)(2,1)S(1)}, f32[512,384]{1,0:T(8,128)S(1)}) custom-call(s32[1,512]{1,0:T(1,128)S(1)} %bitcast.5, f32[512,384]{1,0:T(8,128)S(1)} %copy-done), custom_call_target="tpu_custom_call" | custom-call | flops 536870912 | bytes 3145728 | tf_op jit(solution)/shard_map/pallas_call | solution.py:312
  25.0 0.8 collective-permute-done
  25.8 6.4 %collective-permute-start.1 = (bf16[64,512]{1,0:T(8,128)(2,1)S(1)}, bf16[64,512]{1,0:T(8,128)(2,1)S(1)}, u32[]{:S(2)}, u32[]{:S(2)}) collective-permute-start(bf16[64,512]{1,0:T(8,128)(2,1)S(1)} %pad_maximum_fusion.1), channel_id=1, source_target_pairs={{0,12},{2,14},{4,0},{6,2},{8,4},{10,6},{12,8},{14,10},{1,13},{3,15... | collective-permute-start | bytes 196616 | tf_op jit(solution)/shard_map/ppermute | solution.py:320
  32.2 3.5 %all-to-all-done.got_ref = bf16[32,16,640]{2,1,0:T(8,128)(2,1)S(1)} async-done(((bf16[32,16,640]{2,1,0:T(8,128)(2,1)}), bf16[32,16,640]{2,1,0:T(8,128)(2,1)S(1)}, u32[]{:S(2)}, u32[]{:S(2)}) %all-to-all-start) | async-done | bytes 655392 | tf_op jit(solution)/shard_map/all_to_all | solution.py:279
  35.7 0.0 collective-permute-done.1
  35.7 0.7 broadcast_in_dim.2
  36.5 10.7 %all-to-all-start.1 = ((f16[64,16,128]{2,1,0:T(8,128)(2,1)}), f16[64,16,128]{2,1,0:T(8,128)(2,1)S(1)}, u32[]{:S(2)}, u32[]{:S(2)}) async-start(f16[64,16,128]{2,1,0:T(8,128)(2,1)} %broadcast_in_dim.2), calls=%async_computation.1 | async-start | bytes 524288 | tf_op jit(solution)/shard_map/all_to_all | solution.py:279
  47.2 4.6 %collective-permute-start.2 = (bf16[128,512]{1,0:T(8,128)(2,1)S(1)}, bf16[128,512]{1,0:T(8,128)(2,1)S(1)}, u32[]{:S(2)}, u32[]{:S(2)}) collective-permute-start(bf16[128,512]{1,0:T(8,128)(2,1)S(1)} %pad_maximum_fusion), channel_id=1, source_target_pairs={{0,14},{2,0},{4,2},{6,4},{8,6},{10,8},{12,10},{14,12},{1,15},{3,1}... | collective-permute-start | bytes 393224 | tf_op jit(solution)/shard_map/ppermute | solution.py:320
  51.8 1.0 %shard_map.38 = bf16[32,16,768]{2,1,0:T(8,128)(2,1)} custom-call(bf16[32,16,640]{2,1,0:T(8,128)(2,1)S(1)} %all-to-all-done.got_ref), custom_call_target="tpu_custom_call" | custom-call | flops 196608 | bytes 786432 | tf_op jit(solution)/shard_map/pallas_call | solution.py:330
  52.7 2.8 %collective-permute-done.2 = bf16[128,512]{1,0:T(8,128)(2,1)S(1)} collective-permute-done((bf16[128,512]{1,0:T(8,128)(2,1)S(1)}, bf16[128,512]{1,0:T(8,128)(2,1)S(1)}, u32[]{:S(2)}, u32[]{:S(2)}) %collective-permute-start.2) | collective-permute-done | bytes 131104 | tf_op jit(solution)/shard_map/ppermute | solution.py:320
  55.6 2.7 %all-to-all-done.1 = f16[64,16,128]{2,1,0:T(8,128)(2,1)S(1)} async-done(((f16[64,16,128]{2,1,0:T(8,128)(2,1)}), f16[64,16,128]{2,1,0:T(8,128)(2,1)S(1)}, u32[]{:S(2)}, u32[]{:S(2)}) %all-to-all-start.1) | async-done | bytes 262176 | tf_op jit(solution)/shard_map/all_to_all | solution.py:279
  58.2 7.7 %all-to-all-start.2 = ((bf16[32,16,768]{2,1,0:T(8,128)(2,1)}), bf16[32,16,768]{2,1,0:T(8,128)(2,1)S(1)}, u32[]{:S(2)}, u32[]{:S(2)}) async-start(bf16[32,16,768]{2,1,0:T(8,128)(2,1)} %shard_map.38), calls=%async_computation.2 | async-start | bytes 1572864 | tf_op jit(solution)/shard_map/all_to_all | solution.py:279
  66.0 1.9 %collective-permute-start.3 = (f16[64,16,128]{2,1,0:T(8,128)(2,1)S(1)}, f16[64,16,128]{2,1,0:T(8,128)(2,1)S(1)}, u32[]{:S(2)}, u32[]{:S(2)}) collective-permute-start(f16[64,16,128]{2,1,0:T(8,128)(2,1)S(1)} %all-to-all-done.1), channel_id=1, source_target_pairs={{0,1},{1,0},{2,3},{3,2},{4,5},{5,4},{6,7},{7,6},{8,9},{9,8},{10,11... | collective-permute-start | bytes 786440 | tf_op jit(solution)/shard_map/ppermute | solution.py:338
  68.0 2.4 %collective-permute-start.4 = (bf16[256,512]{1,0:T(8,128)(2,1)S(1)}, bf16[256,512]{1,0:T(8,128)(2,1)S(1)}, u32[]{:S(2)}, u32[]{:S(2)}) collective-permute-start(bf16[256,512]{1,0:T(8,128)(2,1)S(1)} %constant_dynamic-update-slice_fusion.own_ref), channel_id=1, source_target_pairs={{0,1},{1,0},{2,3},{3,2},{4,5},{5,4},{6,7},{7,6},{8,9},{9,8},{10,11... | collective-permute-start | bytes 786440 | tf_op jit(solution)/shard_map/ppermute | solution.py:339
  70.4 0.0 collective-permute-done.3
  70.5 1.0 %collective-permute-done.4.across_ref = bf16[256,512]{1,0:T(8,128)(2,1)S(1)} collective-permute-done((bf16[256,512]{1,0:T(8,128)(2,1)S(1)}, bf16[256,512]{1,0:T(8,128)(2,1)S(1)}, u32[]{:S(2)}, u32[]{:S(2)}) %collective-permute-start.4) | collective-permute-done | bytes 262176 | tf_op jit(solution)/shard_map/ppermute | solution.py:339
  71.5 7.6 %shard_map.40 = (bf16[2,6,128,128]{3,2,1,0:T(8,128)(2,1)S(1)}, bf16[2,4,128,128]{3,2,1,0:T(8,128)(2,1)S(1)}, bf16[512,512]{1,0:T(8,128)(2,1)S(1)}) custom-call(f32[64,16,128]{2,1,0:T(8,128)S(1)} %convert_element_type.24.mine_ref, f32[64,16,128]{2,1,0:T(8,128)S(1)} %convert_element_type.25.other_ref, ...), custom_call_target="tpu_custom_call" | custom-call | flops 1342177280 | bytes 8388608 | tf_op jit(solution)/shard_map/pallas_call | solution.py:341
  79.1 5.8 %all-to-all-done.2.got_ref = bf16[32,16,768]{2,1,0:T(8,128)(2,1)S(1)} async-done(((bf16[32,16,768]{2,1,0:T(8,128)(2,1)}), bf16[32,16,768]{2,1,0:T(8,128)(2,1)S(1)}, u32[]{:S(2)}, u32[]{:S(2)}) %all-to-all-start.2) | async-done | bytes 786464 | tf_op jit(solution)/shard_map/all_to_all | solution.py:279
  84.9 2.8 %shard_map.41 = f32[512,384]{1,0:T(8,128)} custom-call(s32[1,512]{1,0:T(1,128)S(1)} %bitcast.6, bf16[32,16,768]{2,1,0:T(8,128)(2,1)S(1)} %all-to-all-done.2.got_ref, f32[512,384]{1,0:T(8,128)S(1)} %get-tuple-element.26.kept_ref, bf16[2,6,128,128]{3,2,1,0:T(8,128)(2,1)S(1)} %get-tuple-element.29.below_ref, ...), custom_call_target="tpu_custom_call" | custom-call | flops 805306368 | bytes 9437184 | tf_op jit(solution)/shard_map/pallas_call | solution.py:352
  (9 shorter events, 0.1 us)
Async XLA Ops:
  2.5 21.4 %copy-start = (f32[512,384]{1,0:T(8,128)S(1)}, f32[512,384]{1,0:T(8,128)}, u32[]{:S(2)}) copy-start(f32[512,384]{1,0:T(8,128)} %matrix_ref.1) | copy-start | bytes 2359300
  2.5 21.4 %copy-start.1 = (s32[512]{0:T(512)S(1)}, s32[512]{0:T(512)}, u32[]{:S(2)}) copy-start(s32[512]{0:T(512)} %param.5) | copy-start | bytes 6148
  2.5 33.3 %all-to-all-start = ((bf16[32,16,640]{2,1,0:T(8,128)(2,1)}), bf16[32,16,640]{2,1,0:T(8,128)(2,1)S(1)}, u32[]{:S(2)}, u32[]{:S(2)}) async-start(bf16[32,16,640]{2,1,0:T(8,128)(2,1)} %get-tuple-element.19), calls=%async_computation | async-start | bytes 1310720 | tf_op jit(solution)/shard_map/all_to_all | solution.py:279
  16.1 9.7 %collective-permute-start = (bf16[32,512]{1,0:T(8,128)(2,1)S(1)}, bf16[32,512]{1,0:T(8,128)(2,1)S(1)}, u32[]{:S(2)}, u32[]{:S(2)}) collective-permute-start(bf16[32,512]{1,0:T(8,128)(2,1)S(1)} %get-tuple-element.20), channel_id=1, source_target_pairs={{0,8},{2,10},{4,12},{6,14},{8,0},{10,2},{12,4},{14,6},{1,9},{3,11}... | collective-permute-start | bytes 98312 | tf_op jit(solution)/shard_map/ppermute | solution.py:320
  25.8 9.9 %collective-permute-start.1 = (bf16[64,512]{1,0:T(8,128)(2,1)S(1)}, bf16[64,512]{1,0:T(8,128)(2,1)S(1)}, u32[]{:S(2)}, u32[]{:S(2)}) collective-permute-start(bf16[64,512]{1,0:T(8,128)(2,1)S(1)} %pad_maximum_fusion.1), channel_id=1, source_target_pairs={{0,12},{2,14},{4,0},{6,2},{8,4},{10,6},{12,8},{14,10},{1,13},{3,15... | collective-permute-start | bytes 196616 | tf_op jit(solution)/shard_map/ppermute | solution.py:320
  36.5 21.8 %all-to-all-start.1 = ((f16[64,16,128]{2,1,0:T(8,128)(2,1)}), f16[64,16,128]{2,1,0:T(8,128)(2,1)S(1)}, u32[]{:S(2)}, u32[]{:S(2)}) async-start(f16[64,16,128]{2,1,0:T(8,128)(2,1)} %broadcast_in_dim.2), calls=%async_computation.1 | async-start | bytes 524288 | tf_op jit(solution)/shard_map/all_to_all | solution.py:279
  47.2 8.4 %collective-permute-start.2 = (bf16[128,512]{1,0:T(8,128)(2,1)S(1)}, bf16[128,512]{1,0:T(8,128)(2,1)S(1)}, u32[]{:S(2)}, u32[]{:S(2)}) collective-permute-start(bf16[128,512]{1,0:T(8,128)(2,1)S(1)} %pad_maximum_fusion), channel_id=1, source_target_pairs={{0,14},{2,0},{4,2},{6,4},{8,6},{10,8},{12,10},{14,12},{1,15},{3,1}... | collective-permute-start | bytes 393224 | tf_op jit(solution)/shard_map/ppermute | solution.py:320
  58.2 26.7 %all-to-all-start.2 = ((bf16[32,16,768]{2,1,0:T(8,128)(2,1)}), bf16[32,16,768]{2,1,0:T(8,128)(2,1)S(1)}, u32[]{:S(2)}, u32[]{:S(2)}) async-start(bf16[32,16,768]{2,1,0:T(8,128)(2,1)} %shard_map.38), calls=%async_computation.2 | async-start | bytes 1572864 | tf_op jit(solution)/shard_map/all_to_all | solution.py:279
  66.0 4.4 %collective-permute-start.3 = (f16[64,16,128]{2,1,0:T(8,128)(2,1)S(1)}, f16[64,16,128]{2,1,0:T(8,128)(2,1)S(1)}, u32[]{:S(2)}, u32[]{:S(2)}) collective-permute-start(f16[64,16,128]{2,1,0:T(8,128)(2,1)S(1)} %all-to-all-done.1), channel_id=1, source_target_pairs={{0,1},{1,0},{2,3},{3,2},{4,5},{5,4},{6,7},{7,6},{8,9},{9,8},{10,11... | collective-permute-start | bytes 786440 | tf_op jit(solution)/shard_map/ppermute | solution.py:338
  68.0 3.6 %collective-permute-start.4 = (bf16[256,512]{1,0:T(8,128)(2,1)S(1)}, bf16[256,512]{1,0:T(8,128)(2,1)S(1)}, u32[]{:S(2)}, u32[]{:S(2)}) collective-permute-start(bf16[256,512]{1,0:T(8,128)(2,1)S(1)} %constant_dynamic-update-slice_fusion.own_ref), channel_id=1, source_target_pairs={{0,1},{1,0},{2,3},{3,2},{4,5},{5,4},{6,7},{7,6},{8,9},{9,8},{10,11... | collective-permute-start | bytes 786440 | tf_op jit(solution)/shard_map/ppermute | solution.py:339

commit v5 on v4

--- a/solution.py
+++ b/solution.py
@@ -7,10 +7,11 @@
 
 GRID_ROW = ("z", "x")
 SCALE = 65536.0
-ARRIVALS = (0, 4, 2, 6, 1, 5, 3, 7)
+ARRIVALS = (0, 4, 2, 1, 5, 3, 6, 7)
 STEPS = ((0, 1, 0), (0, 2, 1), (0, 3, 2), (1, 2, 3), (1, 3, 4), (2, 3, 5))
 VMEM_LIMIT = 20 * 1024 * 1024
 HALF = jnp.bfloat16
+SHORT = jnp.float16
 
 
 def call(kernel, out_shape, flops, moved, **more):
@@ -64,14 +65,17 @@
     return jnp.where(hit, 1.0, 0.0).astype(HALF)
 
 
-def offer_kernel(
-    sources_hbm, matrix_hbm, columns_hbm, out_hbm, own_ref, sources_ref, matrix_ref, columns_ref, out_ref, sems, sent
-):
+def range_power(block):
+    largest = jnp.maximum(jnp.max(jnp.abs(block)), 1e-30)
+    return 13.0 - jnp.ceil(jnp.log2(jnp.full((1, 1), largest, jnp.float32)))
+
+
+def offer_kernel(sources_hbm, matrix_hbm, columns_hbm, out_ref, own_ref, sources_ref, matrix_ref, columns_ref, sems):
     rows, cols = matrix_ref.shape
     width = sources_ref.shape[1]
     parts, each, wide = out_ref.shape
     myself = grid_row()
-    quarter, some = rows // 4, parts // 4
+    quarter = rows // 4
     small = [
         pltpu.make_async_copy(sources_hbm, sources_ref, sems.at[0]),
         pltpu.make_async_copy(columns_hbm, columns_ref, sems.at[1]),
@@ -87,53 +91,40 @@
 
     columns = columns_ref[...]
     own_ref[...] = columns.astype(HALF)
-    first = columns.astype(HALF).astype(jnp.float32)
-    second = columns - first
+    columns = columns * SCALE
+    picks = one_hot(as_column(sources_ref[...]) - myself * rows == iota((width, rows), 1))
+    for copy in large:
+        copy.wait()
+    block = matrix_ref[...]
+    power = range_power(block)
+    block = (block * jnp.exp2(power)).astype(HALF)
+    corner = (iota((each, wide - cols), 0) == 0) & (iota((each, wide - cols), 1) == 0)
     holders = columns.shape[0] // 4
     for holder in range(holders):
         high = 4 * holder
-        for values, lane in ((first, cols), (second, cols + 128)):
-            piece = jnp.concatenate([values[high : high + 4, 128 * q : 128 * q + 128] for q in range(4)], axis=0)
-            piece = piece.astype(HALF)
-            for part in range(holder, parts, holders):
-                out_ref[part, :, lane : lane + 128] = piece
-
-    def send(at):
-        here = pl.ds(at * some, some)
-        return pltpu.make_async_copy(out_ref.at[here], out_hbm.at[here], sent.at[at])
+        piece = jnp.concatenate([columns[high : high + 4, 128 * q : 128 * q + 128] for q in range(4)], axis=0)
+        piece = jnp.where(corner, power, piece)
+        for part in range(holder, parts, holders):
+            out_ref[part, :, cols:wide] = piece
 
     @pl.when(myself == 0)
     def _():
-        for at in range(4):
-            large[at].wait()
-            block = matrix_ref[quarter * at : quarter * (at + 1)].astype(HALF)
-            out_ref[some * at : some * (at + 1), :, 0:cols] = block.reshape(some, each, cols)
-            send(at).start()
+        out_ref[:, :, 0:cols] = block.astype(jnp.float32).reshape(parts, each, cols)
 
     @pl.when(myself != 0)
     def _():
-        wanted = as_column(sources_ref[...]) - myself * rows
-        picks = one_hot(wanted == iota((width, rows), 1))
-        for copy in large:
-            copy.wait()
-        block = matrix_ref[...].astype(HALF)
-        for at in range(4):
-            found = half_dot(picks[quarter * at : quarter * (at + 1)], block).astype(HALF)
-            out_ref[some * at : some * (at + 1), :, 0:cols] = found.reshape(some, each, cols)
-            send(at).start()
-
-    for at in range(4):
-        send(at).wait()
+        out_ref[:, :, 0:cols] = half_dot(picks, block).reshape(parts, each, cols)
 
 
 def collect_kernel(got_ref, out_ref):
     parts, each, twice = out_ref.shape
     cols = twice // 2
-    total = got_ref[1, :, 0:cols].astype(jnp.float32)
+    factors = jnp.exp2(-got_ref[:, 0:1, cols : cols + 1])
+    total = got_ref[1, :, 0:cols] * factors[1]
     for part in range(2, parts):
-        total = total + got_ref[part, :, 0:cols].astype(jnp.float32)
+        total = total + got_ref[part, :, 0:cols] * factors[part]
     pivots = total.astype(HALF)
-    top = got_ref[0, :, 0:cols]
+    top = (got_ref[0, :, 0:cols] * factors[0]).astype(HALF)
     for part in range(parts):
         out_ref[part, :, 0:cols] = pivots
         out_ref[part, :, cols:twice] = top
@@ -157,19 +148,9 @@
     return inverse
 
 
-def prepare_kernel(
-    mine_ref,
-    other_ref,
-    own_ref,
-    across_ref,
-    below_ref,
-    inverse_ref,
-    weights_ref,
-    lower_ref,
-    gathered_ref,
-):
+def invert_kernel(mine_ref, other_ref, below_ref, inverse_ref, lower_ref):
     width = lower_ref.shape[0]
-    core, chip = lax.axis_index("core"), lax.axis_index("y")
+    core = lax.axis_index("core")
     mine, other = mine_ref[...], other_ref[...]
     pair = (jnp.where(core == 0, mine, other), jnp.where(core == 0, other, mine))
     lines = []
@@ -181,13 +162,6 @@
             lines.append(jnp.concatenate(lanes, axis=1))
     lower_ref[...] = jnp.transpose(jnp.concatenate(lines, axis=0)) * (1.0 / SCALE)
 
-    for at, ahead in enumerate(ARRIVALS):
-        start = 64 * lax.rem(chip + ahead, 8)
-        here = slice(32 * at, 32 * at + 32)
-        gathered_ref[pl.ds(pl.multiple_of(start + 32 * core, 32), 32), :] = own_ref[here, :]
-        gathered_ref[pl.ds(pl.multiple_of(start + 32 * (1 - core), 32), 32), :] = across_ref[here, :]
-    weights_ref[...] = -jnp.transpose(gathered_ref[...])
-
     count = width // 128
     inverses = []
     for block in range(count):
@@ -197,6 +171,16 @@
     for at, block, place in STEPS:
         here = slice(128 * block, 128 * block + 128)
         below_ref[:, place] = in_two(-exact_dot(inverses[block], lower_ref[here, 128 * at : 128 * at + 128]))
+
+
+def weights_kernel(own_ref, across_ref, weights_ref, gathered_ref):
+    core, chip = lax.axis_index("core"), lax.axis_index("y")
+    for at, ahead in enumerate(ARRIVALS):
+        start = 64 * lax.rem(chip + ahead, 8)
+        here = slice(32 * at, 32 * at + 32)
+        gathered_ref[pl.ds(pl.multiple_of(start + 32 * core, 32), 32), :] = own_ref[here, :]
+        gathered_ref[pl.ds(pl.multiple_of(start + 32 * (1 - core), 32), 32), :] = across_ref[here, :]
+    weights_ref[...] = -jnp.transpose(gathered_ref[...])
 
 
 def choose_kernel(sources_ref, matrix_ref, choose_ref, kept_ref):
@@ -293,21 +277,18 @@
 
     offer, own = call(
         offer_kernel,
-        (jax.ShapeDtypeStruct((parts, each, cols + 256), HALF), jax.ShapeDtypeStruct(columns.shape, HALF)),
+        (jax.ShapeDtypeStruct((parts, each, cols + 128), f32), jax.ShapeDtypeStruct(columns.shape, HALF)),
         2 * width * rows * cols,
         2 * rows * cols * 4,
         in_specs=[hbm, hbm, hbm],
-        out_specs=[hbm, vmem],
         scratch_shapes=[
             pltpu.VMEM((1, width), jnp.int32),
             pltpu.VMEM((rows, cols), f32),
             pltpu.VMEM(columns.shape, f32),
-            pltpu.VMEM((parts, each, cols + 256), HALF),
             pltpu.SemaphoreType.DMA((6,)),
-            pltpu.SemaphoreType.DMA((4,)),
         ],
     )(in_hbm(sources), in_hbm(matrix), in_hbm(columns))
-    got = exchange(offer, GRID_ROW)
+    got = exchange(offer.astype(SHORT), GRID_ROW)
 
     choose, kept = call(
         choose_kernel,
@@ -319,36 +300,38 @@
     def bring(block, ahead):
         return lax.ppermute(block, "y", [(i, (i - ahead) % chips) for i in range(chips)])
 
-    own = jnp.concatenate([own, bring(own, 4)], axis=0)
-    came = bring(own, 2)
-
-    piece = got[0, :, cols : cols + 128].astype(f32) + got[0, :, cols + 128 : cols + 256].astype(f32)
-    piece = (piece * SCALE).astype(jnp.float16)
+    came = [bring(own, 4), bring(own, 2)]
+    piece = got[0, :, cols:]
     piece, came, choose, kept = lax.optimization_barrier((piece, came, choose, kept))
     mine = exchange(everyone(piece, 8 * chips), ("x", "y"))
 
     collected = call(
         collect_kernel, jax.ShapeDtypeStruct((parts, each, 2 * cols), HALF), parts * each * cols, 4 * parts * each * cols
-    )(got)
-    own = jnp.concatenate([own, came], axis=0)
-    came = bring(own, 1)
+    )(got.astype(f32))
+    three = jnp.concatenate([own] + came, axis=0)
+    came = bring(three, 1)
     collected, mine, came = lax.optimization_barrier((collected, mine, came))
-    own = jnp.concatenate([own, came], axis=0)
+    last = bring(jnp.concatenate([own, came[0:32]], axis=0), 6)
     arrived = exchange(collected, GRID_ROW)
     other = lax.ppermute(mine, "core", [(0, 1), (1, 0)])
-    across = lax.ppermute(own, "core", [(0, 1), (1, 0)])
-
-    below, inverse, weights = call(
-        prepare_kernel,
-        (
-            jax.ShapeDtypeStruct((2, 6, 128, 128), HALF),
-            jax.ShapeDtypeStruct((2, 4, 128, 128), HALF),
-            jax.ShapeDtypeStruct((rows, width), HALF),
-        ),
+
+    below, inverse = call(
+        invert_kernel,
+        (jax.ShapeDtypeStruct((2, 6, 128, 128), HALF), jax.ShapeDtypeStruct((2, 4, 128, 128), HALF)),
         10 * width * width * width,
         8 * width * width * 4,
-        scratch_shapes=[pltpu.VMEM((width, width), f32), pltpu.VMEM((width, rows), HALF)],
-    )(mine.astype(f32), other.astype(f32), own, across)
+        scratch_shapes=[pltpu.VMEM((width, width), f32)],
+    )(mine.astype(f32), other.astype(f32))
+    last, inverse = lax.optimization_barrier((last, inverse))
+    own = jnp.concatenate([three, came, last], axis=0)
+    across = lax.ppermute(own, "core", [(0, 1), (1, 0)])
+    weights = call(
+        weights_kernel,
+        jax.ShapeDtypeStruct((rows, width), HALF),
+        width * rows,
+        4 * width * rows,
+        scratch_shapes=[pltpu.VMEM((width, rows), HALF)],
+    )(own, across)
     return call(
         finish_kernel,
         jax.ShapeDtypeStruct((rows, cols), f32),

time: 88.2 us -> 85.5 us (0.969)
  the two profiles are of different devices: /device:TPU:2 before, /device:TPU:26 now
where the time goes in v5:
time: 85.5 us; the launch traced here: 84.9 us
  starting transfers between devices  48.2 us (56%)
  waiting for transfers between devices  19.8 us (23%)
  Pallas kernels  14.8 us (17%)
  other arithmetic  1.12 us (1%)
    all_to_all x3, starting transfers between devices, exchange(): return lax.all_to_all(blocks, axes, 0, 0, tiled=False)  30.1 us
    ppermute x4, starting transfers between devices, bring(): lax.ppermute(block, 'y', [(i, (i - ahead) % chips) for i in range(chips)])  14 us
    all_to_all x3, waiting for transfers between devices, exchange(): return lax.all_to_all(blocks, axes, 0, 0, tiled=False)  13.4 us
    pallas_call x1, Pallas kernels, on_device(): call(invert_kernel, (jax.ShapeDtypeStruct((2, 6, 128, 128), HALF), jax.Sh...  7.52 us
    ppermute x4, waiting for transfers between devices, bring(): lax.ppermute(block, 'y', [(i, (i - ahead) % chips) for i in range(chips)])  5.15 us
    pallas_call x1, Pallas kernels, on_device(): call(finish_kernel, jax.ShapeDtypeStruct((rows, cols), f32), 8 * rows * c...  2.78 us
    ppermute x1, starting transfers between devices, on_device(): across = lax.ppermute(own, 'core', [(0, 1), (1, 0)])  2.13 us
    pallas_call x1, Pallas kernels, on_device(): call(offer_kernel, (jax.ShapeDtypeStruct((parts, each, cols + 128), f32),...  2.01 us
  transfers between devices with their start and end apart: 9, of which 5 were waited for; matrix products, arithmetic and copies ran while one was open for 0% of the time, Pallas kernels for 12%

profile of v5, /device:TPU:26, one launch (start us, length us, event | category | flops | bytes accessed | tf_op | source)
XLA Modules:
  0.0 84.9 jit_solution(15366452572067286706)
XLA Ops:
  0.0 2.0 %shard_map.37 = (f32[32,16,512]{2,1,0:T(8,128)S(1)}, bf16[32,512]{1,0:T(8,128)(2,1)S(1)}) custom-call(s32[1,512]{1,0:T(1,128)} %bitcast.4, f32[512,384]{1,0:T(8,128)} %matrix_ref.1, f32[32,512]{1,0:T(8,128)} %bitcast.7), custom_call_target="tpu_custom_call" | custom-call | flops 201326592 | bytes 1572864 | tf_op jit(solution)/shard_map/pallas_call | solution.py:278
  2.0 0.9 %convert_element_type.12 = f16[32,16,512]{2,1,0:T(8,128)(2,1)} convert(f32[32,16,512]{2,1,0:T(8,128)S(1)} %get-tuple-element.21) | non-fusion elementwise | flops 262144 | bytes 1572864 | tf_op jit(solution)/shard_map/convert_element_type | solution.py:291
  2.9 0.0 copy-start
  2.9 0.0 copy-start.1
  2.9 13.6 %all-to-all-start = ((f16[32,16,512]{2,1,0:T(8,128)(2,1)}), f16[32,16,512]{2,1,0:T(8,128)(2,1)S(1)}, u32[]{:S(2)}, u32[]{:S(2)}) async-start(f16[32,16,512]{2,1,0:T(8,128)(2,1)} %convert_element_type.12), calls=%async_computation | async-start | bytes 1048576 | tf_op jit(solution)/shard_map/all_to_all | solution.py:263
  16.5 5.0 %collective-permute-start = (bf16[32,512]{1,0:T(8,128)(2,1)S(1)}, bf16[32,512]{1,0:T(8,128)(2,1)S(1)}, u32[]{:S(2)}, u32[]{:S(2)}) collective-permute-start(bf16[32,512]{1,0:T(8,128)(2,1)S(1)} %get-tuple-element.22), channel_id=1, source_target_pairs={{0,8},{2,10},{4,12},{6,14},{8,0},{10,2},{12,4},{14,6},{1,9},{3,11}... | collective-permute-start | bytes 98312 | tf_op jit(solution)/shard_map/ppermute | solution.py:301
  21.6 4.0 %collective-permute-start.1 = (bf16[32,512]{1,0:T(8,128)(2,1)S(1)}, bf16[32,512]{1,0:T(8,128)(2,1)S(1)}, u32[]{:S(2)}, u32[]{:S(2)}) collective-permute-start(bf16[32,512]{1,0:T(8,128)(2,1)S(1)} %get-tuple-element.22), channel_id=1, source_target_pairs={{0,12},{2,14},{4,0},{6,2},{8,4},{10,6},{12,8},{14,10},{1,13},{3,15... | collective-permute-start | bytes 98312 | tf_op jit(solution)/shard_map/ppermute | solution.py:301
  25.6 0.0 copy-done
  25.6 0.0 copy-done.1
  25.6 1.1 %shard_map.39 = (bf16[512,512]{1,0:T(8,128)(2,1)S(1)}, f32[512,384]{1,0:T(8,128)S(1)}) custom-call(s32[1,512]{1,0:T(1,128)S(1)} %bitcast.5, f32[512,384]{1,0:T(8,128)S(1)} %copy-done), custom_call_target="tpu_custom_call" | custom-call | flops 536870912 | bytes 3145728 | tf_op jit(solution)/shard_map/pallas_call | solution.py:293
  26.8 6.6 %all-to-all-done = f16[32,16,512]{2,1,0:T(8,128)(2,1)S(1)} async-done(((f16[32,16,512]{2,1,0:T(8,128)(2,1)}), f16[32,16,512]{2,1,0:T(8,128)(2,1)S(1)}, u32[]{:S(2)}, u32[]{:S(2)}) %all-to-all-start) | async-done | bytes 524320 | tf_op jit(solution)/shard_map/all_to_all | solution.py:263
  33.4 0.0 collective-permute-done
  33.4 0.0 collective-permute-done.1
  33.4 0.7 broadcast_in_dim.2
  34.1 10.3 %all-to-all-start.1 = ((f16[64,16,128]{2,1,0:T(8,128)(2,1)}), f16[64,16,128]{2,1,0:T(8,128)(2,1)S(1)}, u32[]{:S(2)}, u32[]{:S(2)}) async-start(f16[64,16,128]{2,1,0:T(8,128)(2,1)} %broadcast_in_dim.2), calls=%async_computation.1 | async-start | bytes 524288 | tf_op jit(solution)/shard_map/all_to_all | solution.py:263
  44.4 2.5 %collective-permute-start.2 = (bf16[96,512]{1,0:T(8,128)(2,1)S(1)}, bf16[96,512]{1,0:T(8,128)(2,1)S(1)}, u32[]{:S(2)}, u32[]{:S(2)}) collective-permute-start(bf16[96,512]{1,0:T(8,128)(2,1)S(1)} %pad_maximum_fusion), channel_id=1, source_target_pairs={{0,14},{2,0},{4,2},{6,4},{8,6},{10,8},{12,10},{14,12},{1,15},{3,1}... | collective-permute-start | bytes 294920 | tf_op jit(solution)/shard_map/ppermute | solution.py:301
  46.9 0.1 convert_element_type.13.got_ref
  47.1 1.1 %shard_map.38 = bf16[32,16,768]{2,1,0:T(8,128)(2,1)} custom-call(f32[32,16,512]{2,1,0:T(8,128)S(1)} %convert_element_type.13.got_ref), custom_call_target="tpu_custom_call" | custom-call | flops 196608 | bytes 786432 | tf_op jit(solution)/shard_map/pallas_call | solution.py:308
  48.1 5.1 %collective-permute-done.2 = bf16[96,512]{1,0:T(8,128)(2,1)S(1)} collective-permute-done((bf16[96,512]{1,0:T(8,128)(2,1)S(1)}, bf16[96,512]{1,0:T(8,128)(2,1)S(1)}, u32[]{:S(2)}, u32[]{:S(2)}) %collective-permute-start.2) | collective-permute-done | bytes 98336 | tf_op jit(solution)/shard_map/ppermute | solution.py:301
  53.3 0.7 all-to-all-done.1
  54.0 6.2 %all-to-all-start.2 = ((bf16[32,16,768]{2,1,0:T(8,128)(2,1)}), bf16[32,16,768]{2,1,0:T(8,128)(2,1)S(1)}, u32[]{:S(2)}, u32[]{:S(2)}) async-start(bf16[32,16,768]{2,1,0:T(8,128)(2,1)} %shard_map.38), calls=%async_computation.2 | async-start | bytes 1572864 | tf_op jit(solution)/shard_map/all_to_all | solution.py:263
  60.2 1.9 %collective-permute-start.3 = (f16[64,16,128]{2,1,0:T(8,128)(2,1)S(1)}, f16[64,16,128]{2,1,0:T(8,128)(2,1)S(1)}, u32[]{:S(2)}, u32[]{:S(2)}) collective-permute-start(f16[64,16,128]{2,1,0:T(8,128)(2,1)S(1)} %all-to-all-done.1), channel_id=1, source_target_pairs={{0,1},{1,0},{2,3},{3,2},{4,5},{5,4},{6,7},{7,6},{8,9},{9,8},{10,11... | collective-permute-start | bytes 786440 | tf_op jit(solution)/shard_map/ppermute | solution.py:316
  62.2 2.5 %collective-permute-start.4 = (bf16[64,512]{1,0:T(8,128)(2,1)S(1)}, bf16[64,512]{1,0:T(8,128)(2,1)S(1)}, u32[]{:S(2)}, u32[]{:S(2)}) collective-permute-start(bf16[64,512]{1,0:T(8,128)(2,1)S(1)} %pad_maximum_fusion.1), channel_id=1, source_target_pairs={{0,4},{2,6},{4,8},{6,10},{8,12},{10,14},{12,0},{14,2},{1,5},{3,7},... | collective-permute-start | bytes 196616 | tf_op jit(solution)/shard_map/ppermute | solution.py:301
  64.8 0.0 collective-permute-done.3
  64.8 7.5 %shard_map.40 = (bf16[2,6,128,128]{3,2,1,0:T(8,128)(2,1)S(1)}, bf16[2,4,128,128]{3,2,1,0:T(8,128)(2,1)S(1)}) custom-call(f32[64,16,128]{2,1,0:T(8,128)S(1)} %convert_element_type.14.mine_ref, f32[64,16,128]{2,1,0:T(8,128)S(1)} %convert_element_type.15.other_ref), custom_call_target="tpu_custom_call" | custom-call | flops 1342177280 | bytes 8388608 | tf_op jit(solution)/shard_map/pallas_call | solution.py:318
  72.3 0.0 collective-permute-done.4
  72.4 2.1 %collective-permute-start.5 = (bf16[256,512]{1,0:T(8,128)(2,1)S(1)}, bf16[256,512]{1,0:T(8,128)(2,1)S(1)}, u32[]{:S(2)}, u32[]{:S(2)}) collective-permute-start(bf16[256,512]{1,0:T(8,128)(2,1)S(1)} %constant_dynamic-update-slice_fusion.own_ref), channel_id=1, source_target_pairs={{0,1},{1,0},{2,3},{3,2},{4,5},{5,4},{6,7},{7,6},{8,9},{9,8},{10,11... | collective-permute-start | bytes 786440 | tf_op jit(solution)/shard_map/ppermute | solution.py:327
  74.5 1.3 %collective-permute-done.5.across_ref = bf16[256,512]{1,0:T(8,128)(2,1)S(1)} collective-permute-done((bf16[256,512]{1,0:T(8,128)(2,1)S(1)}, bf16[256,512]{1,0:T(8,128)(2,1)S(1)}, u32[]{:S(2)}, u32[]{:S(2)}) %collective-permute-start.5) | collective-permute-done | bytes 262176 | tf_op jit(solution)/shard_map/ppermute | solution.py:327
  75.8 0.2 shard_map.41.weights_ref
  76.0 6.1 %all-to-all-done.2.got_ref = bf16[32,16,768]{2,1,0:T(8,128)(2,1)S(1)} async-done(((bf16[32,16,768]{2,1,0:T(8,128)(2,1)}), bf16[32,16,768]{2,1,0:T(8,128)(2,1)S(1)}, u32[]{:S(2)}, u32[]{:S(2)}) %all-to-all-start.2) | async-done | bytes 786464 | tf_op jit(solution)/shard_map/all_to_all | solution.py:263
  82.2 2.8 %shard_map.42 = f32[512,384]{1,0:T(8,128)} custom-call(s32[1,512]{1,0:T(1,128)S(1)} %bitcast.6, bf16[32,16,768]{2,1,0:T(8,128)(2,1)S(1)} %all-to-all-done.2.got_ref, f32[512,384]{1,0:T(8,128)S(1)} %get-tuple-element.29.kept_ref, bf16[2,6,128,128]{3,2,1,0:T(8,128)(2,1)S(1)} %get-tuple-element.31.below_ref, ...), custom_call_target="tpu_custom_call" | custom-call | flops 805306368 | bytes 9437184 | tf_op jit(solution)/shard_map/pallas_call | solution.py:335
  (11 shorter events, 0.1 us)
Async XLA Ops:
  2.9 22.7 %copy-start = (f32[512,384]{1,0:T(8,128)S(1)}, f32[512,384]{1,0:T(8,128)}, u32[]{:S(2)}) copy-start(f32[512,384]{1,0:T(8,128)} %matrix_ref.1) | copy-start | bytes 2359300
  2.9 22.7 %copy-start.1 = (s32[512]{0:T(512)S(1)}, s32[512]{0:T(512)}, u32[]{:S(2)}) copy-start(s32[512]{0:T(512)} %param.5) | copy-start | bytes 6148
  2.9 30.4 %all-to-all-start = ((f16[32,16,512]{2,1,0:T(8,128)(2,1)}), f16[32,16,512]{2,1,0:T(8,128)(2,1)S(1)}, u32[]{:S(2)}, u32[]{:S(2)}) async-start(f16[32,16,512]{2,1,0:T(8,128)(2,1)} %convert_element_type.12), calls=%async_computation | async-start | bytes 1048576 | tf_op jit(solution)/shard_map/all_to_all | solution.py:263
  16.5 16.8 %collective-permute-start = (bf16[32,512]{1,0:T(8,128)(2,1)S(1)}, bf16[32,512]{1,0:T(8,128)(2,1)S(1)}, u32[]{:S(2)}, u32[]{:S(2)}) collective-permute-start(bf16[32,512]{1,0:T(8,128)(2,1)S(1)} %get-tuple-element.22), channel_id=1, source_target_pairs={{0,8},{2,10},{4,12},{6,14},{8,0},{10,2},{12,4},{14,6},{1,9},{3,11}... | collective-permute-start | bytes 98312 | tf_op jit(solution)/shard_map/ppermute | solution.py:301
  21.6 11.8 %collective-permute-start.1 = (bf16[32,512]{1,0:T(8,128)(2,1)S(1)}, bf16[32,512]{1,0:T(8,128)(2,1)S(1)}, u32[]{:S(2)}, u32[]{:S(2)}) collective-permute-start(bf16[32,512]{1,0:T(8,128)(2,1)S(1)} %get-tuple-element.22), channel_id=1, source_target_pairs={{0,12},{2,14},{4,0},{6,2},{8,4},{10,6},{12,8},{14,10},{1,13},{3,15... | collective-permute-start | bytes 98312 | tf_op jit(solution)/shard_map/ppermute | solution.py:301
  34.1 19.8 %all-to-all-start.1 = ((f16[64,16,128]{2,1,0:T(8,128)(2,1)}), f16[64,16,128]{2,1,0:T(8,128)(2,1)S(1)}, u32[]{:S(2)}, u32[]{:S(2)}) async-start(f16[64,16,128]{2,1,0:T(8,128)(2,1)} %broadcast_in_dim.2), calls=%async_computation.1 | async-start | bytes 524288 | tf_op jit(solution)/shard_map/all_to_all | solution.py:263
  44.4 8.8 %collective-permute-start.2 = (bf16[96,512]{1,0:T(8,128)(2,1)S(1)}, bf16[96,512]{1,0:T(8,128)(2,1)S(1)}, u32[]{:S(2)}, u32[]{:S(2)}) collective-permute-start(bf16[96,512]{1,0:T(8,128)(2,1)S(1)} %pad_maximum_fusion), channel_id=1, source_target_pairs={{0,14},{2,0},{4,2},{6,4},{8,6},{10,8},{12,10},{14,12},{1,15},{3,1}... | collective-permute-start | bytes 294920 | tf_op jit(solution)/shard_map/ppermute | solution.py:301
  54.0 28.2 %all-to-all-start.2 = ((bf16[32,16,768]{2,1,0:T(8,128)(2,1)}), bf16[32,16,768]{2,1,0:T(8,128)(2,1)S(1)}, u32[]{:S(2)}, u32[]{:S(2)}) async-start(bf16[32,16,768]{2,1,0:T(8,128)(2,1)} %shard_map.38), calls=%async_computation.2 | async-start | bytes 1572864 | tf_op jit(solution)/shard_map/all_to_all | solution.py:263
  60.2 4.5 %collective-permute-start.3 = (f16[64,16,128]{2,1,0:T(8,128)(2,1)S(1)}, f16[64,16,128]{2,1,0:T(8,128)(2,1)S(1)}, u32[]{:S(2)}, u32[]{:S(2)}) collective-permute-start(f16[64,16,128]{2,1,0:T(8,128)(2,1)S(1)} %all-to-all-done.1), channel_id=1, source_target_pairs={{0,1},{1,0},{2,3},{3,2},{4,5},{5,4},{6,7},{7,6},{8,9},{9,8},{10,11... | collective-permute-start | bytes 786440 | tf_op jit(solution)/shard_map/ppermute | solution.py:316
  62.2 10.1 %collective-permute-start.4 = (bf16[64,512]{1,0:T(8,128)(2,1)S(1)}, bf16[64,512]{1,0:T(8,128)(2,1)S(1)}, u32[]{:S(2)}, u32[]{:S(2)}) collective-permute-start(bf16[64,512]{1,0:T(8,128)(2,1)S(1)} %pad_maximum_fusion.1), channel_id=1, source_target_pairs={{0,4},{2,6},{4,8},{6,10},{8,12},{10,14},{12,0},{14,2},{1,5},{3,7},... | collective-permute-start | bytes 196616 | tf_op jit(solution)/shard_map/ppermute | solution.py:301
  72.4 3.4 %collective-permute-start.5 = (bf16[256,512]{1,0:T(8,128)(2,1)S(1)}, bf16[256,512]{1,0:T(8,128)(2,1)S(1)}, u32[]{:S(2)}, u32[]{:S(2)}) collective-permute-start(bf16[256,512]{1,0:T(8,128)(2,1)S(1)} %constant_dynamic-update-slice_fusion.own_ref), channel_id=1, source_target_pairs={{0,1},{1,0},{2,3},{3,2},{4,5},{5,4},{6,7},{7,6},{8,9},{9,8},{10,11... | collective-permute-start | bytes 786440 | tf_op jit(solution)/shard_map/ppermute | solution.py:327

commit v6 on v5

--- a/solution.py
+++ b/solution.py
@@ -130,22 +130,23 @@
         out_ref[part, :, cols:twice] = top
 
 
-def invert_block(lower):
-    n = lower.shape[0]
+def invert_blocks(lowers):
+    n = lowers[0].shape[0]
     row, col = iota((n, n), 0), iota((n, n), 1)
     unit = jnp.where(row == col, 1.0, 0.0)
-    power = jnp.where((row // 32 == col // 32) & (row > col), lower, 0.0)
-    inverse = unit - power
+    near = (row // 32 == col // 32) & (row > col)
+    powers = [jnp.where(near, lower, 0.0) for lower in lowers]
+    inverses = [unit - power for power in powers]
     for _ in range(4):
-        power = exact_dot(power, power)
-        inverse = inverse + exact_dot(inverse, power)
+        powers = [exact_dot(power, power) for power in powers]
+        inverses = [inverse + exact_dot(inverse, power) for inverse, power in zip(inverses, powers)]
     size = 32
     while size < n:
         off = (row // (2 * size) == col // (2 * size)) & (row // size > col // size)
-        below = jnp.where(off, lower, 0.0)
-        inverse = inverse - exact_dot(inverse, exact_dot(below, inverse))
+        turned = [exact_dot(jnp.where(off, lower, 0.0), inverse) for lower, inverse in zip(lowers, inverses)]
+        inverses = [inverse - exact_dot(inverse, turn) for inverse, turn in zip(inverses, turned)]
         size *= 2
-    return inverse
+    return inverses
 
 
 def invert_kernel(mine_ref, other_ref, below_ref, inverse_ref, lower_ref):
@@ -163,14 +164,15 @@
     lower_ref[...] = jnp.transpose(jnp.concatenate(lines, axis=0)) * (1.0 / SCALE)
 
     count = width // 128
-    inverses = []
-    for block in range(count):
-        here = slice(128 * block, 128 * block + 128)
-        inverses.append(invert_block(lower_ref[here, here]))
-        inverse_ref[:, block] = in_two(inverses[block])
+
+    def block_of(down, across):
+        return lower_ref[128 * down : 128 * down + 128, 128 * across : 128 * across + 128]
+
+    inverses = invert_blocks([block_of(at, at) for at in range(count)])
+    for at in range(count):
+        inverse_ref[:, at] = in_two(inverses[at])
     for at, block, place in STEPS:
-        here = slice(128 * block, 128 * block + 128)
-        below_ref[:, place] = in_two(-exact_dot(inverses[block], lower_ref[here, 128 * at : 128 * at + 128]))
+        below_ref[:, place] = in_two(-split_dot(in_two(inverses[block]), block_of(block, at)))
 
 
 def weights_kernel(own_ref, across_ref, weights_ref, gathered_ref):

time: 85.5 us -> 85.5 us (level)
  the two profiles are of different devices: /device:TPU:26 before, /device:TPU:2 now
where the time goes in v6:
time: 85.5 us; the launch traced here: 84.9 us
  starting transfers between devices  52 us (61%)
  waiting for transfers between devices  20 us (23%)
  Pallas kernels  10.8 us (13%)
  other arithmetic  1.12 us (1%)
    all_to_all x3, starting transfers between devices, exchange(): return lax.all_to_all(blocks, axes, 0, 0, tiled=False)  30.4 us
    ppermute x4, starting transfers between devices, bring(): lax.ppermute(block, 'y', [(i, (i - ahead) % chips) for i in range(chips)])  17.7 us
    all_to_all x3, waiting for transfers between devices, exchange(): return lax.all_to_all(blocks, axes, 0, 0, tiled=False)  13.8 us
    ppermute x4, waiting for transfers between devices, bring(): lax.ppermute(block, 'y', [(i, (i - ahead) % chips) for i in range(chips)])  4.71 us
    pallas_call x1, Pallas kernels, on_device(): call(invert_kernel, (jax.ShapeDtypeStruct((2, 6, 128, 128), HALF), jax.Sh...  3.5 us
    pallas_call x1, Pallas kernels, on_device(): call(finish_kernel, jax.ShapeDtypeStruct((rows, cols), f32), 8 * rows * c...  2.78 us
    pallas_call x1, Pallas kernels, on_device(): call(offer_kernel, (jax.ShapeDtypeStruct((parts, each, cols + 128), f32),...  2.01 us
    ppermute x1, starting transfers between devices, on_device(): other = lax.ppermute(mine, 'core', [(0, 1), (1, 0)])  1.92 us
  transfers between devices with their start and end apart: 9, of which 6 were waited for; matrix products, arithmetic and copies ran while one was open for 0% of the time, Pallas kernels for 7%

profile of v6, /device:TPU:2, one launch (start us, length us, event | category | flops | bytes accessed | tf_op | source)
XLA Modules:
  0.0 84.9 jit_solution(16796468120629201553)
XLA Ops:
  0.0 2.0 %shard_map.37 = (f32[32,16,512]{2,1,0:T(8,128)S(1)}, bf16[32,512]{1,0:T(8,128)(2,1)S(1)}) custom-call(s32[1,512]{1,0:T(1,128)} %bitcast.4, f32[512,384]{1,0:T(8,128)} %matrix_ref.1, f32[32,512]{1,0:T(8,128)} %bitcast.7), custom_call_target="tpu_custom_call" | custom-call | flops 201326592 | bytes 1572864 | tf_op jit(solution)/shard_map/pallas_call | solution.py:280
  2.0 0.9 %convert_element_type.12 = f16[32,16,512]{2,1,0:T(8,128)(2,1)} convert(f32[32,16,512]{2,1,0:T(8,128)S(1)} %get-tuple-element.21) | non-fusion elementwise | flops 262144 | bytes 1572864 | tf_op jit(solution)/shard_map/convert_element_type | solution.py:293
  2.9 0.0 copy-start
  2.9 0.0 copy-start.1
  2.9 13.6 %all-to-all-start = ((f16[32,16,512]{2,1,0:T(8,128)(2,1)}), f16[32,16,512]{2,1,0:T(8,128)(2,1)S(1)}, u32[]{:S(2)}, u32[]{:S(2)}) async-start(f16[32,16,512]{2,1,0:T(8,128)(2,1)} %convert_element_type.12), calls=%async_computation | async-start | bytes 1048576 | tf_op jit(solution)/shard_map/all_to_all | solution.py:265
  16.5 7.7 %collective-permute-start = (bf16[32,512]{1,0:T(8,128)(2,1)S(1)}, bf16[32,512]{1,0:T(8,128)(2,1)S(1)}, u32[]{:S(2)}, u32[]{:S(2)}) collective-permute-start(bf16[32,512]{1,0:T(8,128)(2,1)S(1)} %get-tuple-element.22), channel_id=1, source_target_pairs={{0,8},{2,10},{4,12},{6,14},{8,0},{10,2},{12,4},{14,6},{1,9},{3,11}... | collective-permute-start | bytes 98312 | tf_op jit(solution)/shard_map/ppermute | solution.py:303
  24.3 2.2 %collective-permute-start.1 = (bf16[32,512]{1,0:T(8,128)(2,1)S(1)}, bf16[32,512]{1,0:T(8,128)(2,1)S(1)}, u32[]{:S(2)}, u32[]{:S(2)}) collective-permute-start(bf16[32,512]{1,0:T(8,128)(2,1)S(1)} %get-tuple-element.22), channel_id=1, source_target_pairs={{0,12},{2,14},{4,0},{6,2},{8,4},{10,6},{12,8},{14,10},{1,13},{3,15... | collective-permute-start | bytes 98312 | tf_op jit(solution)/shard_map/ppermute | solution.py:303
  26.5 0.0 copy-done
  26.5 0.0 copy-done.1
  26.5 1.1 %shard_map.39 = (bf16[512,512]{1,0:T(8,128)(2,1)S(1)}, f32[512,384]{1,0:T(8,128)S(1)}) custom-call(s32[1,512]{1,0:T(1,128)S(1)} %bitcast.5, f32[512,384]{1,0:T(8,128)S(1)} %copy-done), custom_call_target="tpu_custom_call" | custom-call | flops 536870912 | bytes 3145728 | tf_op jit(solution)/shard_map/pallas_call | solution.py:295
  27.7 5.7 %all-to-all-done = f16[32,16,512]{2,1,0:T(8,128)(2,1)S(1)} async-done(((f16[32,16,512]{2,1,0:T(8,128)(2,1)}), f16[32,16,512]{2,1,0:T(8,128)(2,1)S(1)}, u32[]{:S(2)}, u32[]{:S(2)}) %all-to-all-start) | async-done | bytes 524320 | tf_op jit(solution)/shard_map/all_to_all | solution.py:265
  33.4 0.0 collective-permute-done
  33.4 0.0 collective-permute-done.1
  33.4 0.7 broadcast_in_dim.2
  34.1 10.6 %all-to-all-start.1 = ((f16[64,16,128]{2,1,0:T(8,128)(2,1)}), f16[64,16,128]{2,1,0:T(8,128)(2,1)S(1)}, u32[]{:S(2)}, u32[]{:S(2)}) async-start(f16[64,16,128]{2,1,0:T(8,128)(2,1)} %broadcast_in_dim.2), calls=%async_computation.1 | async-start | bytes 524288 | tf_op jit(solution)/shard_map/all_to_all | solution.py:265
  44.8 4.6 %collective-permute-start.2 = (bf16[96,512]{1,0:T(8,128)(2,1)S(1)}, bf16[96,512]{1,0:T(8,128)(2,1)S(1)}, u32[]{:S(2)}, u32[]{:S(2)}) collective-permute-start(bf16[96,512]{1,0:T(8,128)(2,1)S(1)} %pad_maximum_fusion), channel_id=1, source_target_pairs={{0,14},{2,0},{4,2},{6,4},{8,6},{10,8},{12,10},{14,12},{1,15},{3,1}... | collective-permute-start | bytes 294920 | tf_op jit(solution)/shard_map/ppermute | solution.py:303
  49.4 0.1 convert_element_type.13.got_ref
  49.5 1.1 %shard_map.38 = bf16[32,16,768]{2,1,0:T(8,128)(2,1)} custom-call(f32[32,16,512]{2,1,0:T(8,128)S(1)} %convert_element_type.13.got_ref), custom_call_target="tpu_custom_call" | custom-call | flops 196608 | bytes 786432 | tf_op jit(solution)/shard_map/pallas_call | solution.py:310
  50.6 1.5 %collective-permute-done.2 = bf16[96,512]{1,0:T(8,128)(2,1)S(1)} collective-permute-done((bf16[96,512]{1,0:T(8,128)(2,1)S(1)}, bf16[96,512]{1,0:T(8,128)(2,1)S(1)}, u32[]{:S(2)}, u32[]{:S(2)}) %collective-permute-start.2) | collective-permute-done | bytes 98336 | tf_op jit(solution)/shard_map/ppermute | solution.py:303
  52.1 3.6 %all-to-all-done.1 = f16[64,16,128]{2,1,0:T(8,128)(2,1)S(1)} async-done(((f16[64,16,128]{2,1,0:T(8,128)(2,1)}), f16[64,16,128]{2,1,0:T(8,128)(2,1)S(1)}, u32[]{:S(2)}, u32[]{:S(2)}) %all-to-all-start.1) | async-done | bytes 262176 | tf_op jit(solution)/shard_map/all_to_all | solution.py:265
  55.7 6.2 %all-to-all-start.2 = ((bf16[32,16,768]{2,1,0:T(8,128)(2,1)}), bf16[32,16,768]{2,1,0:T(8,128)(2,1)S(1)}, u32[]{:S(2)}, u32[]{:S(2)}) async-start(bf16[32,16,768]{2,1,0:T(8,128)(2,1)} %shard_map.38), calls=%async_computation.2 | async-start | bytes 1572864 | tf_op jit(solution)/shard_map/all_to_all | solution.py:265
  61.9 1.9 %collective-permute-start.3 = (f16[64,16,128]{2,1,0:T(8,128)(2,1)S(1)}, f16[64,16,128]{2,1,0:T(8,128)(2,1)S(1)}, u32[]{:S(2)}, u32[]{:S(2)}) collective-permute-start(f16[64,16,128]{2,1,0:T(8,128)(2,1)S(1)} %all-to-all-done.1), channel_id=1, source_target_pairs={{0,1},{1,0},{2,3},{3,2},{4,5},{5,4},{6,7},{7,6},{8,9},{9,8},{10,11... | collective-permute-start | bytes 786440 | tf_op jit(solution)/shard_map/ppermute | solution.py:318
  64.0 3.2 %collective-permute-start.4 = (bf16[64,512]{1,0:T(8,128)(2,1)S(1)}, bf16[64,512]{1,0:T(8,128)(2,1)S(1)}, u32[]{:S(2)}, u32[]{:S(2)}) collective-permute-start(bf16[64,512]{1,0:T(8,128)(2,1)S(1)} %pad_maximum_fusion.1), channel_id=1, source_target_pairs={{0,4},{2,6},{4,8},{6,10},{8,12},{10,14},{12,0},{14,2},{1,5},{3,7},... | collective-permute-start | bytes 196616 | tf_op jit(solution)/shard_map/ppermute | solution.py:303
  67.1 0.0 collective-permute-done.3
  67.2 3.5 %shard_map.40 = (bf16[2,6,128,128]{3,2,1,0:T(8,128)(2,1)S(1)}, bf16[2,4,128,128]{3,2,1,0:T(8,128)(2,1)S(1)}) custom-call(f32[64,16,128]{2,1,0:T(8,128)S(1)} %convert_element_type.14.mine_ref, f32[64,16,128]{2,1,0:T(8,128)S(1)} %convert_element_type.15.other_ref), custom_call_target="tpu_custom_call" | custom-call | flops 1342177280 | bytes 8388608 | tf_op jit(solution)/shard_map/pallas_call | solution.py:320
  70.7 3.2 %collective-permute-done.4 = bf16[64,512]{1,0:T(8,128)(2,1)S(1)} collective-permute-done((bf16[64,512]{1,0:T(8,128)(2,1)S(1)}, bf16[64,512]{1,0:T(8,128)(2,1)S(1)}, u32[]{:S(2)}, u32[]{:S(2)}) %collective-permute-start.4) | collective-permute-done | bytes 65568 | tf_op jit(solution)/shard_map/ppermute | solution.py:303
  73.9 1.9 %collective-permute-start.5 = (bf16[256,512]{1,0:T(8,128)(2,1)S(1)}, bf16[256,512]{1,0:T(8,128)(2,1)S(1)}, u32[]{:S(2)}, u32[]{:S(2)}) collective-permute-start(bf16[256,512]{1,0:T(8,128)(2,1)S(1)} %constant_dynamic-update-slice_fusion.own_ref), channel_id=1, source_target_pairs={{0,1},{1,0},{2,3},{3,2},{4,5},{5,4},{6,7},{7,6},{8,9},{9,8},{10,11... | collective-permute-start | bytes 786440 | tf_op jit(solution)/shard_map/ppermute | solution.py:329
  75.8 1.5 %collective-permute-done.5.across_ref = bf16[256,512]{1,0:T(8,128)(2,1)S(1)} collective-permute-done((bf16[256,512]{1,0:T(8,128)(2,1)S(1)}, bf16[256,512]{1,0:T(8,128)(2,1)S(1)}, u32[]{:S(2)}, u32[]{:S(2)}) %collective-permute-start.5) | collective-permute-done | bytes 262176 | tf_op jit(solution)/shard_map/ppermute | solution.py:329
  77.3 0.2 shard_map.41.weights_ref
  77.5 4.5 %all-to-all-done.2.got_ref = bf16[32,16,768]{2,1,0:T(8,128)(2,1)S(1)} async-done(((bf16[32,16,768]{2,1,0:T(8,128)(2,1)}), bf16[32,16,768]{2,1,0:T(8,128)(2,1)S(1)}, u32[]{:S(2)}, u32[]{:S(2)}) %all-to-all-start.2) | async-done | bytes 786464 | tf_op jit(solution)/shard_map/all_to_all | solution.py:265
  82.1 2.8 %shard_map.42 = f32[512,384]{1,0:T(8,128)} custom-call(s32[1,512]{1,0:T(1,128)S(1)} %bitcast.6, bf16[32,16,768]{2,1,0:T(8,128)(2,1)S(1)} %all-to-all-done.2.got_ref, f32[512,384]{1,0:T(8,128)S(1)} %get-tuple-element.29.kept_ref, bf16[2,6,128,128]{3,2,1,0:T(8,128)(2,1)S(1)} %get-tuple-element.31.below_ref, ...), custom_call_target="tpu_custom_call" | custom-call | flops 805306368 | bytes 9437184 | tf_op jit(solution)/shard_map/pallas_call | solution.py:337
  (11 shorter events, 0.1 us)
Async XLA Ops:
  2.9 23.6 %copy-start = (f32[512,384]{1,0:T(8,128)S(1)}, f32[512,384]{1,0:T(8,128)}, u32[]{:S(2)}) copy-start(f32[512,384]{1,0:T(8,128)} %matrix_ref.1) | copy-start | bytes 2359300
  2.9 23.6 %copy-start.1 = (s32[512]{0:T(512)S(1)}, s32[512]{0:T(512)}, u32[]{:S(2)}) copy-start(s32[512]{0:T(512)} %param.5) | copy-start | bytes 6148
  2.9 30.4 %all-to-all-start = ((f16[32,16,512]{2,1,0:T(8,128)(2,1)}), f16[32,16,512]{2,1,0:T(8,128)(2,1)S(1)}, u32[]{:S(2)}, u32[]{:S(2)}) async-start(f16[32,16,512]{2,1,0:T(8,128)(2,1)} %convert_element_type.12), calls=%async_computation | async-start | bytes 1048576 | tf_op jit(solution)/shard_map/all_to_all | solution.py:265
  16.5 16.8 %collective-permute-start = (bf16[32,512]{1,0:T(8,128)(2,1)S(1)}, bf16[32,512]{1,0:T(8,128)(2,1)S(1)}, u32[]{:S(2)}, u32[]{:S(2)}) collective-permute-start(bf16[32,512]{1,0:T(8,128)(2,1)S(1)} %get-tuple-element.22), channel_id=1, source_target_pairs={{0,8},{2,10},{4,12},{6,14},{8,0},{10,2},{12,4},{14,6},{1,9},{3,11}... | collective-permute-start | bytes 98312 | tf_op jit(solution)/shard_map/ppermute | solution.py:303
  24.3 9.1 %collective-permute-start.1 = (bf16[32,512]{1,0:T(8,128)(2,1)S(1)}, bf16[32,512]{1,0:T(8,128)(2,1)S(1)}, u32[]{:S(2)}, u32[]{:S(2)}) collective-permute-start(bf16[32,512]{1,0:T(8,128)(2,1)S(1)} %get-tuple-element.22), channel_id=1, source_target_pairs={{0,12},{2,14},{4,0},{6,2},{8,4},{10,6},{12,8},{14,10},{1,13},{3,15... | collective-permute-start | bytes 98312 | tf_op jit(solution)/shard_map/ppermute | solution.py:303
  34.1 21.6 %all-to-all-start.1 = ((f16[64,16,128]{2,1,0:T(8,128)(2,1)}), f16[64,16,128]{2,1,0:T(8,128)(2,1)S(1)}, u32[]{:S(2)}, u32[]{:S(2)}) async-start(f16[64,16,128]{2,1,0:T(8,128)(2,1)} %broadcast_in_dim.2), calls=%async_computation.1 | async-start | bytes 524288 | tf_op jit(solution)/shard_map/all_to_all | solution.py:265
  44.8 7.3 %collective-permute-start.2 = (bf16[96,512]{1,0:T(8,128)(2,1)S(1)}, bf16[96,512]{1,0:T(8,128)(2,1)S(1)}, u32[]{:S(2)}, u32[]{:S(2)}) collective-permute-start(bf16[96,512]{1,0:T(8,128)(2,1)S(1)} %pad_maximum_fusion), channel_id=1, source_target_pairs={{0,14},{2,0},{4,2},{6,4},{8,6},{10,8},{12,10},{14,12},{1,15},{3,1}... | collective-permute-start | bytes 294920 | tf_op jit(solution)/shard_map/ppermute | solution.py:303
  55.7 26.3 %all-to-all-start.2 = ((bf16[32,16,768]{2,1,0:T(8,128)(2,1)}), bf16[32,16,768]{2,1,0:T(8,128)(2,1)S(1)}, u32[]{:S(2)}, u32[]{:S(2)}) async-start(bf16[32,16,768]{2,1,0:T(8,128)(2,1)} %shard_map.38), calls=%async_computation.2 | async-start | bytes 1572864 | tf_op jit(solution)/shard_map/all_to_all | solution.py:265
  61.9 5.2 %collective-permute-start.3 = (f16[64,16,128]{2,1,0:T(8,128)(2,1)S(1)}, f16[64,16,128]{2,1,0:T(8,128)(2,1)S(1)}, u32[]{:S(2)}, u32[]{:S(2)}) collective-permute-start(f16[64,16,128]{2,1,0:T(8,128)(2,1)S(1)} %all-to-all-done.1), channel_id=1, source_target_pairs={{0,1},{1,0},{2,3},{3,2},{4,5},{5,4},{6,7},{7,6},{8,9},{9,8},{10,11... | collective-permute-start | bytes 786440 | tf_op jit(solution)/shard_map/ppermute | solution.py:318
  64.0 9.9 %collective-permute-start.4 = (bf16[64,512]{1,0:T(8,128)(2,1)S(1)}, bf16[64,512]{1,0:T(8,128)(2,1)S(1)}, u32[]{:S(2)}, u32[]{:S(2)}) collective-permute-start(bf16[64,512]{1,0:T(8,128)(2,1)S(1)} %pad_maximum_fusion.1), channel_id=1, source_target_pairs={{0,4},{2,6},{4,8},{6,10},{8,12},{10,14},{12,0},{14,2},{1,5},{3,7},... | collective-permute-start | bytes 196616 | tf_op jit(solution)/shard_map/ppermute | solution.py:303
  73.9 3.4 %collective-permute-start.5 = (bf16[256,512]{1,0:T(8,128)(2,1)S(1)}, bf16[256,512]{1,0:T(8,128)(2,1)S(1)}, u32[]{:S(2)}, u32[]{:S(2)}) collective-permute-start(bf16[256,512]{1,0:T(8,128)(2,1)S(1)} %constant_dynamic-update-slice_fusion.own_ref), channel_id=1, source_target_pairs={{0,1},{1,0},{2,3},{3,2},{4,5},{5,4},{6,7},{7,6},{8,9},{9,8},{10,11... | collective-permute-start | bytes 786440 | tf_op jit(solution)/shard_map/ppermute | solution.py:329

commit v7 on v6

--- a/solution.py
+++ b/solution.py
@@ -6,6 +6,7 @@
 from jax.sharding import Mesh, PartitionSpec as P
 
 GRID_ROW = ("z", "x")
+PARTNERS = ("x", "z")
 SCALE = 65536.0
 ARRIVALS = (0, 4, 2, 1, 5, 3, 6, 7)
 STEPS = ((0, 1, 0), (0, 2, 1), (0, 3, 2), (1, 2, 3), (1, 3, 4), (2, 3, 5))
@@ -100,11 +101,12 @@
     block = (block * jnp.exp2(power)).astype(HALF)
     corner = (iota((each, wide - cols), 0) == 0) & (iota((each, wide - cols), 1) == 0)
     holders = columns.shape[0] // 4
+    planes = parts // holders
     for holder in range(holders):
         high = 4 * holder
         piece = jnp.concatenate([columns[high : high + 4, 128 * q : 128 * q + 128] for q in range(4)], axis=0)
         piece = jnp.where(corner, power, piece)
-        for part in range(holder, parts, holders):
+        for part in range(planes * holder, planes * holder + planes):
             out_ref[part, :, cols:wide] = piece
 
     @pl.when(myself == 0)
@@ -290,7 +292,7 @@
             pltpu.SemaphoreType.DMA((6,)),
         ],
     )(in_hbm(sources), in_hbm(matrix), in_hbm(columns))
-    got = exchange(offer.astype(SHORT), GRID_ROW)
+    got = exchange(offer.astype(SHORT), PARTNERS)
 
     choose, kept = call(
         choose_kernel,
@@ -314,7 +316,7 @@
     came = bring(three, 1)
     collected, mine, came = lax.optimization_barrier((collected, mine, came))
     last = bring(jnp.concatenate([own, came[0:32]], axis=0), 6)
-    arrived = exchange(collected, GRID_ROW)
+    arrived = exchange(collected, PARTNERS)
     other = lax.ppermute(mine, "core", [(0, 1), (1, 0)])
 
     below, inverse = call(

time: 85.5 us -> 85 us (level)
  the two profiles are of different devices: /device:TPU:2 before, /device:TPU:24 now
where the time goes in v7:
time: 85 us; the launch traced here: 84.4 us
  starting transfers between devices  46.4 us (55%)
  waiting for transfers between devices  26.1 us (31%)
  Pallas kernels  9.84 us (12%)
  other arithmetic  1.12 us (1%)
    all_to_all x3, starting transfers between devices, exchange(): return lax.all_to_all(blocks, axes, 0, 0, tiled=False)  28.3 us
    all_to_all x3, waiting for transfers between devices, exchange(): return lax.all_to_all(blocks, axes, 0, 0, tiled=False)  17 us
    ppermute x4, starting transfers between devices, bring(): lax.ppermute(block, 'y', [(i, (i - ahead) % chips) for i in range(chips)])  14.3 us
    ppermute x4, waiting for transfers between devices, bring(): lax.ppermute(block, 'y', [(i, (i - ahead) % chips) for i in range(chips)])  7.56 us
    pallas_call x1, Pallas kernels, on_device(): call(invert_kernel, (jax.ShapeDtypeStruct((2, 6, 128, 128), HALF), jax.Sh...  3.49 us
    pallas_call x1, Pallas kernels, on_device(): call(finish_kernel, jax.ShapeDtypeStruct((rows, cols), f32), 8 * rows * c...  2.27 us
    ppermute x1, starting transfers between devices, on_device(): other = lax.ppermute(mine, 'core', [(0, 1), (1, 0)])  1.92 us
    ppermute x1, starting transfers between devices, on_device(): across = lax.ppermute(own, 'core', [(0, 1), (1, 0)])  1.91 us
  transfers between devices with their start and end apart: 9, of which 6 were waited for; matrix products, arithmetic and copies ran while one was open for 0% of the time, Pallas kernels for 7%

profile of v7, /device:TPU:24, one launch (start us, length us, event | category | flops | bytes accessed | tf_op | source)
XLA Modules:
  0.0 84.4 jit_solution(233638817676940787)
XLA Ops:
  0.0 1.6 %shard_map.37 = (f32[32,16,512]{2,1,0:T(8,128)S(1)}, bf16[32,512]{1,0:T(8,128)(2,1)S(1)}) custom-call(s32[1,512]{1,0:T(1,128)} %bitcast.4, f32[512,384]{1,0:T(8,128)} %matrix_ref.1, f32[32,512]{1,0:T(8,128)} %bitcast.7), custom_call_target="tpu_custom_call" | custom-call | flops 201326592 | bytes 1572864 | tf_op jit(solution)/shard_map/pallas_call | solution.py:282
  1.6 0.9 %convert_element_type.12 = f16[32,16,512]{2,1,0:T(8,128)(2,1)} convert(f32[32,16,512]{2,1,0:T(8,128)S(1)} %get-tuple-element.21) | non-fusion elementwise | flops 262144 | bytes 1572864 | tf_op jit(solution)/shard_map/convert_element_type | solution.py:295
  2.5 0.0 copy-start
  2.5 0.0 copy-start.1
  2.5 13.7 %all-to-all-start = ((f16[32,16,512]{2,1,0:T(8,128)(2,1)}), f16[32,16,512]{2,1,0:T(8,128)(2,1)S(1)}, u32[]{:S(2)}, u32[]{:S(2)}) async-start(f16[32,16,512]{2,1,0:T(8,128)(2,1)} %convert_element_type.12), calls=%async_computation | async-start | bytes 1048576 | tf_op jit(solution)/shard_map/all_to_all | solution.py:267
  16.2 5.0 %collective-permute-start = (bf16[32,512]{1,0:T(8,128)(2,1)S(1)}, bf16[32,512]{1,0:T(8,128)(2,1)S(1)}, u32[]{:S(2)}, u32[]{:S(2)}) collective-permute-start(bf16[32,512]{1,0:T(8,128)(2,1)S(1)} %get-tuple-element.22), channel_id=1, source_target_pairs={{0,8},{2,10},{4,12},{6,14},{8,0},{10,2},{12,4},{14,6},{1,9},{3,11}... | collective-permute-start | bytes 98312 | tf_op jit(solution)/shard_map/ppermute | solution.py:305
  21.3 4.0 %collective-permute-start.1 = (bf16[32,512]{1,0:T(8,128)(2,1)S(1)}, bf16[32,512]{1,0:T(8,128)(2,1)S(1)}, u32[]{:S(2)}, u32[]{:S(2)}) collective-permute-start(bf16[32,512]{1,0:T(8,128)(2,1)S(1)} %get-tuple-element.22), channel_id=1, source_target_pairs={{0,12},{2,14},{4,0},{6,2},{8,4},{10,6},{12,8},{14,10},{1,13},{3,15... | collective-permute-start | bytes 98312 | tf_op jit(solution)/shard_map/ppermute | solution.py:305
  25.3 0.0 copy-done
  25.3 0.0 copy-done.1
  25.4 1.1 %shard_map.39 = (bf16[512,512]{1,0:T(8,128)(2,1)S(1)}, f32[512,384]{1,0:T(8,128)S(1)}) custom-call(s32[1,512]{1,0:T(1,128)S(1)} %bitcast.5, f32[512,384]{1,0:T(8,128)S(1)} %copy-done), custom_call_target="tpu_custom_call" | custom-call | flops 536870912 | bytes 3145728 | tf_op jit(solution)/shard_map/pallas_call | solution.py:297
  26.5 7.1 %all-to-all-done = f16[32,16,512]{2,1,0:T(8,128)(2,1)S(1)} async-done(((f16[32,16,512]{2,1,0:T(8,128)(2,1)}), f16[32,16,512]{2,1,0:T(8,128)(2,1)S(1)}, u32[]{:S(2)}, u32[]{:S(2)}) %all-to-all-start) | async-done | bytes 524320 | tf_op jit(solution)/shard_map/all_to_all | solution.py:267
  33.6 0.0 collective-permute-done
  33.6 0.0 collective-permute-done.1
  33.6 0.7 broadcast_in_dim.2
  34.3 9.8 %all-to-all-start.1 = ((f16[64,16,128]{2,1,0:T(8,128)(2,1)}), f16[64,16,128]{2,1,0:T(8,128)(2,1)S(1)}, u32[]{:S(2)}, u32[]{:S(2)}) async-start(f16[64,16,128]{2,1,0:T(8,128)(2,1)} %broadcast_in_dim.2), calls=%async_computation.1 | async-start | bytes 524288 | tf_op jit(solution)/shard_map/all_to_all | solution.py:267
  44.2 2.5 %collective-permute-start.2 = (bf16[96,512]{1,0:T(8,128)(2,1)S(1)}, bf16[96,512]{1,0:T(8,128)(2,1)S(1)}, u32[]{:S(2)}, u32[]{:S(2)}) collective-permute-start(bf16[96,512]{1,0:T(8,128)(2,1)S(1)} %pad_maximum_fusion), channel_id=1, source_target_pairs={{0,14},{2,0},{4,2},{6,4},{8,6},{10,8},{12,10},{14,12},{1,15},{3,1}... | collective-permute-start | bytes 294920 | tf_op jit(solution)/shard_map/ppermute | solution.py:305
  46.6 0.1 convert_element_type.13.got_ref
  46.8 1.1 %shard_map.38 = bf16[32,16,768]{2,1,0:T(8,128)(2,1)} custom-call(f32[32,16,512]{2,1,0:T(8,128)S(1)} %convert_element_type.13.got_ref), custom_call_target="tpu_custom_call" | custom-call | flops 196608 | bytes 786432 | tf_op jit(solution)/shard_map/pallas_call | solution.py:312
  47.9 5.1 %collective-permute-done.2 = bf16[96,512]{1,0:T(8,128)(2,1)S(1)} collective-permute-done((bf16[96,512]{1,0:T(8,128)(2,1)S(1)}, bf16[96,512]{1,0:T(8,128)(2,1)S(1)}, u32[]{:S(2)}, u32[]{:S(2)}) %collective-permute-start.2) | collective-permute-done | bytes 98336 | tf_op jit(solution)/shard_map/ppermute | solution.py:305
  53.0 2.3 %all-to-all-done.1 = f16[64,16,128]{2,1,0:T(8,128)(2,1)S(1)} async-done(((f16[64,16,128]{2,1,0:T(8,128)(2,1)}), f16[64,16,128]{2,1,0:T(8,128)(2,1)S(1)}, u32[]{:S(2)}, u32[]{:S(2)}) %all-to-all-start.1) | async-done | bytes 262176 | tf_op jit(solution)/shard_map/all_to_all | solution.py:267
  55.3 4.8 %all-to-all-start.2 = ((bf16[32,16,768]{2,1,0:T(8,128)(2,1)}), bf16[32,16,768]{2,1,0:T(8,128)(2,1)S(1)}, u32[]{:S(2)}, u32[]{:S(2)}) async-start(bf16[32,16,768]{2,1,0:T(8,128)(2,1)} %shard_map.38), calls=%async_computation.2 | async-start | bytes 1572864 | tf_op jit(solution)/shard_map/all_to_all | solution.py:267
  60.1 1.9 %collective-permute-start.3 = (f16[64,16,128]{2,1,0:T(8,128)(2,1)S(1)}, f16[64,16,128]{2,1,0:T(8,128)(2,1)S(1)}, u32[]{:S(2)}, u32[]{:S(2)}) collective-permute-start(f16[64,16,128]{2,1,0:T(8,128)(2,1)S(1)} %all-to-all-done.1), channel_id=1, source_target_pairs={{0,1},{1,0},{2,3},{3,2},{4,5},{5,4},{6,7},{7,6},{8,9},{9,8},{10,11... | collective-permute-start | bytes 786440 | tf_op jit(solution)/shard_map/ppermute | solution.py:320
  62.1 2.7 %collective-permute-start.4 = (bf16[64,512]{1,0:T(8,128)(2,1)S(1)}, bf16[64,512]{1,0:T(8,128)(2,1)S(1)}, u32[]{:S(2)}, u32[]{:S(2)}) collective-permute-start(bf16[64,512]{1,0:T(8,128)(2,1)S(1)} %pad_maximum_fusion.1), channel_id=1, source_target_pairs={{0,4},{2,6},{4,8},{6,10},{8,12},{10,14},{12,0},{14,2},{1,5},{3,7},... | collective-permute-start | bytes 196616 | tf_op jit(solution)/shard_map/ppermute | solution.py:305
  64.8 0.0 collective-permute-done.3
  64.9 3.5 %shard_map.40 = (bf16[2,6,128,128]{3,2,1,0:T(8,128)(2,1)S(1)}, bf16[2,4,128,128]{3,2,1,0:T(8,128)(2,1)S(1)}) custom-call(f32[64,16,128]{2,1,0:T(8,128)S(1)} %convert_element_type.14.mine_ref, f32[64,16,128]{2,1,0:T(8,128)S(1)} %convert_element_type.15.other_ref), custom_call_target="tpu_custom_call" | custom-call | flops 1342177280 | bytes 8388608 | tf_op jit(solution)/shard_map/pallas_call | solution.py:322
  68.4 2.4 %collective-permute-done.4 = bf16[64,512]{1,0:T(8,128)(2,1)S(1)} collective-permute-done((bf16[64,512]{1,0:T(8,128)(2,1)S(1)}, bf16[64,512]{1,0:T(8,128)(2,1)S(1)}, u32[]{:S(2)}, u32[]{:S(2)}) %collective-permute-start.4) | collective-permute-done | bytes 65568 | tf_op jit(solution)/shard_map/ppermute | solution.py:305
  70.8 1.9 %collective-permute-start.5 = (bf16[256,512]{1,0:T(8,128)(2,1)S(1)}, bf16[256,512]{1,0:T(8,128)(2,1)S(1)}, u32[]{:S(2)}, u32[]{:S(2)}) collective-permute-start(bf16[256,512]{1,0:T(8,128)(2,1)S(1)} %constant_dynamic-update-slice_fusion.own_ref), channel_id=1, source_target_pairs={{0,1},{1,0},{2,3},{3,2},{4,5},{5,4},{6,7},{7,6},{8,9},{9,8},{10,11... | collective-permute-start | bytes 786440 | tf_op jit(solution)/shard_map/ppermute | solution.py:331
  72.7 1.5 %collective-permute-done.5.across_ref = bf16[256,512]{1,0:T(8,128)(2,1)S(1)} collective-permute-done((bf16[256,512]{1,0:T(8,128)(2,1)S(1)}, bf16[256,512]{1,0:T(8,128)(2,1)S(1)}, u32[]{:S(2)}, u32[]{:S(2)}) %collective-permute-start.5) | collective-permute-done | bytes 262176 | tf_op jit(solution)/shard_map/ppermute | solution.py:331
  74.2 0.2 shard_map.41.weights_ref
  74.5 7.7 %all-to-all-done.2.got_ref = bf16[32,16,768]{2,1,0:T(8,128)(2,1)S(1)} async-done(((bf16[32,16,768]{2,1,0:T(8,128)(2,1)}), bf16[32,16,768]{2,1,0:T(8,128)(2,1)S(1)}, u32[]{:S(2)}, u32[]{:S(2)}) %all-to-all-start.2) | async-done | bytes 786464 | tf_op jit(solution)/shard_map/all_to_all | solution.py:267
  82.2 2.3 %shard_map.42 = f32[512,384]{1,0:T(8,128)} custom-call(s32[1,512]{1,0:T(1,128)S(1)} %bitcast.6, bf16[32,16,768]{2,1,0:T(8,128)(2,1)S(1)} %all-to-all-done.2.got_ref, f32[512,384]{1,0:T(8,128)S(1)} %get-tuple-element.29.kept_ref, bf16[2,6,128,128]{3,2,1,0:T(8,128)(2,1)S(1)} %get-tuple-element.31.below_ref, ...), custom_call_target="tpu_custom_call" | custom-call | flops 805306368 | bytes 9437184 | tf_op jit(solution)/shard_map/pallas_call | solution.py:339
  (11 shorter events, 0.1 us)
Async XLA Ops:
  2.5 22.8 %copy-start = (f32[512,384]{1,0:T(8,128)S(1)}, f32[512,384]{1,0:T(8,128)}, u32[]{:S(2)}) copy-start(f32[512,384]{1,0:T(8,128)} %matrix_ref.1) | copy-start | bytes 2359300
  2.5 22.8 %copy-start.1 = (s32[512]{0:T(512)S(1)}, s32[512]{0:T(512)}, u32[]{:S(2)}) copy-start(s32[512]{0:T(512)} %param.5) | copy-start | bytes 6148
  2.5 31.0 %all-to-all-start = ((f16[32,16,512]{2,1,0:T(8,128)(2,1)}), f16[32,16,512]{2,1,0:T(8,128)(2,1)S(1)}, u32[]{:S(2)}, u32[]{:S(2)}) async-start(f16[32,16,512]{2,1,0:T(8,128)(2,1)} %convert_element_type.12), calls=%async_computation | async-start | bytes 1048576 | tf_op jit(solution)/shard_map/all_to_all | solution.py:267
  16.2 17.3 %collective-permute-start = (bf16[32,512]{1,0:T(8,128)(2,1)S(1)}, bf16[32,512]{1,0:T(8,128)(2,1)S(1)}, u32[]{:S(2)}, u32[]{:S(2)}) collective-permute-start(bf16[32,512]{1,0:T(8,128)(2,1)S(1)} %get-tuple-element.22), channel_id=1, source_target_pairs={{0,8},{2,10},{4,12},{6,14},{8,0},{10,2},{12,4},{14,6},{1,9},{3,11}... | collective-permute-start | bytes 98312 | tf_op jit(solution)/shard_map/ppermute | solution.py:305
  21.3 12.3 %collective-permute-start.1 = (bf16[32,512]{1,0:T(8,128)(2,1)S(1)}, bf16[32,512]{1,0:T(8,128)(2,1)S(1)}, u32[]{:S(2)}, u32[]{:S(2)}) collective-permute-start(bf16[32,512]{1,0:T(8,128)(2,1)S(1)} %get-tuple-element.22), channel_id=1, source_target_pairs={{0,12},{2,14},{4,0},{6,2},{8,4},{10,6},{12,8},{14,10},{1,13},{3,15... | collective-permute-start | bytes 98312 | tf_op jit(solution)/shard_map/ppermute | solution.py:305
  34.3 21.0 %all-to-all-start.1 = ((f16[64,16,128]{2,1,0:T(8,128)(2,1)}), f16[64,16,128]{2,1,0:T(8,128)(2,1)S(1)}, u32[]{:S(2)}, u32[]{:S(2)}) async-start(f16[64,16,128]{2,1,0:T(8,128)(2,1)} %broadcast_in_dim.2), calls=%async_computation.1 | async-start | bytes 524288 | tf_op jit(solution)/shard_map/all_to_all | solution.py:267
  44.2 8.8 %collective-permute-start.2 = (bf16[96,512]{1,0:T(8,128)(2,1)S(1)}, bf16[96,512]{1,0:T(8,128)(2,1)S(1)}, u32[]{:S(2)}, u32[]{:S(2)}) collective-permute-start(bf16[96,512]{1,0:T(8,128)(2,1)S(1)} %pad_maximum_fusion), channel_id=1, source_target_pairs={{0,14},{2,0},{4,2},{6,4},{8,6},{10,8},{12,10},{14,12},{1,15},{3,1}... | collective-permute-start | bytes 294920 | tf_op jit(solution)/shard_map/ppermute | solution.py:305
  55.3 26.9 %all-to-all-start.2 = ((bf16[32,16,768]{2,1,0:T(8,128)(2,1)}), bf16[32,16,768]{2,1,0:T(8,128)(2,1)S(1)}, u32[]{:S(2)}, u32[]{:S(2)}) async-start(bf16[32,16,768]{2,1,0:T(8,128)(2,1)} %shard_map.38), calls=%async_computation.2 | async-start | bytes 1572864 | tf_op jit(solution)/shard_map/all_to_all | solution.py:267
  60.1 4.8 %collective-permute-start.3 = (f16[64,16,128]{2,1,0:T(8,128)(2,1)S(1)}, f16[64,16,128]{2,1,0:T(8,128)(2,1)S(1)}, u32[]{:S(2)}, u32[]{:S(2)}) collective-permute-start(f16[64,16,128]{2,1,0:T(8,128)(2,1)S(1)} %all-to-all-done.1), channel_id=1, source_target_pairs={{0,1},{1,0},{2,3},{3,2},{4,5},{5,4},{6,7},{7,6},{8,9},{9,8},{10,11... | collective-permute-start | bytes 786440 | tf_op jit(solution)/shard_map/ppermute | solution.py:320
  62.1 8.7 %collective-permute-start.4 = (bf16[64,512]{1,0:T(8,128)(2,1)S(1)}, bf16[64,512]{1,0:T(8,128)(2,1)S(1)}, u32[]{:S(2)}, u32[]{:S(2)}) collective-permute-start(bf16[64,512]{1,0:T(8,128)(2,1)S(1)} %pad_maximum_fusion.1), channel_id=1, source_target_pairs={{0,4},{2,6},{4,8},{6,10},{8,12},{10,14},{12,0},{14,2},{1,5},{3,7},... | collective-permute-start | bytes 196616 | tf_op jit(solution)/shard_map/ppermute | solution.py:305
  70.8 3.4 %collective-permute-start.5 = (bf16[256,512]{1,0:T(8,128)(2,1)S(1)}, bf16[256,512]{1,0:T(8,128)(2,1)S(1)}, u32[]{:S(2)}, u32[]{:S(2)}) collective-permute-start(bf16[256,512]{1,0:T(8,128)(2,1)S(1)} %constant_dynamic-update-slice_fusion.own_ref), channel_id=1, source_target_pairs={{0,1},{1,0},{2,3},{3,2},{4,5},{5,4},{6,7},{7,6},{8,9},{9,8},{10,11... | collective-permute-start | bytes 786440 | tf_op jit(solution)/shard_map/ppermute | solution.py:331

commit v8 on v7

--- a/solution.py
+++ b/solution.py
@@ -161,7 +161,7 @@
         for half in pair:
             lanes = []
             for q in range(4):
-                lanes.append(jnp.concatenate([half[8 * x + at, 4 * q : 4 * q + 4] for x in range(8)], axis=0))
+                lanes.append(jnp.concatenate([half[8 * at + x, 4 * q : 4 * q + 4] for x in range(8)], axis=0))
             lines.append(jnp.concatenate(lanes, axis=1))
     lower_ref[...] = jnp.transpose(jnp.concatenate(lines, axis=0)) * (1.0 / SCALE)
 
@@ -216,13 +216,15 @@
     width = sources_ref.shape[1]
     myself = grid_row()
     sources = sources_ref[...]
-    moved = half_dot(choose_ref[...], got_ref[:, :, cols : 2 * cols].reshape(width, cols))
-    found = got_ref[:, :, 0:cols].reshape(width, cols).astype(jnp.float32)
+    moved = half_dot(choose_ref[...], got_ref[:, :, cols : 2 * cols].reshape(width, cols)).astype(HALF)
+    found = got_ref[:, :, 0:cols].reshape(width, cols)
     pivots = jnp.where(as_column(sources) >= width, found, moved)
     count = width // 128
     upper = []
     for block in range(count):
-        upper.append(split_dot(inverse_ref[:, block], pivots[128 * block : 128 * block + 128]))
+        right = pivots[128 * block : 128 * block + 128]
+        sides = jnp.concatenate([inverse_ref[0, block], inverse_ref[1, block]], axis=1)
+        upper.append(half_dot(sides, jnp.concatenate([right, right], axis=0)))
     first = 0
     for at in range(count - 1):
         more = count - 1 - at
@@ -247,11 +249,11 @@
 
     @pl.when(myself != 0)
     def _():
-        fills, half = moved.astype(HALF), upper.astype(HALF)
+        half = upper.astype(HALF)
         for at in range(4):
             here = slice(at * quarter, at * quarter + quarter)
             lands = one_hot(sources - (myself * rows + at * quarter) == iota((quarter, width), 0))
-            change = half_dot(lands, fills) + half_dot(weights_ref[here, :], half)
+            change = half_dot(lands, moved) + half_dot(weights_ref[here, :], half)
             out_ref[here, :] = kept_ref[here, :] + change
             copies[at].start()
 
@@ -307,7 +309,7 @@
     came = [bring(own, 4), bring(own, 2)]
     piece = got[0, :, cols:]
     piece, came, choose, kept = lax.optimization_barrier((piece, came, choose, kept))
-    mine = exchange(everyone(piece, 8 * chips), ("x", "y"))
+    mine = exchange(everyone(piece, 8 * chips), ("y", "x"))
 
     collected = call(
         collect_kernel, jax.ShapeDtypeStruct((parts, each, 2 * cols), HALF), parts * each * cols, 4 * parts * each * cols

time: 85 us -> 84.8 us (level)
  no operation moved by 1% of the time
where the time goes in v8:
time: 84.8 us; the launch traced here: 84.2 us
  starting transfers between devices  46.7 us (55%)
  waiting for transfers between devices  25.6 us (30%)
  Pallas kernels  9.81 us (12%)
  other arithmetic  1.12 us (1%)
    all_to_all x3, starting transfers between devices, exchange(): return lax.all_to_all(blocks, axes, 0, 0, tiled=False)  28.7 us
    all_to_all x3, waiting for transfers between devices, exchange(): return lax.all_to_all(blocks, axes, 0, 0, tiled=False)  16.5 us
    ppermute x4, starting transfers between devices, bring(): lax.ppermute(block, 'y', [(i, (i - ahead) % chips) for i in range(chips)])  14.2 us
    ppermute x4, waiting for transfers between devices, bring(): lax.ppermute(block, 'y', [(i, (i - ahead) % chips) for i in range(chips)])  7.65 us
    pallas_call x1, Pallas kernels, on_device(): call(invert_kernel, (jax.ShapeDtypeStruct((2, 6, 128, 128), HALF), jax.Sh...  3.5 us
    pallas_call x1, Pallas kernels, on_device(): call(finish_kernel, jax.ShapeDtypeStruct((rows, cols), f32), 8 * rows * c...  2.23 us
    ppermute x1, starting transfers between devices, on_device(): other = lax.ppermute(mine, 'core', [(0, 1), (1, 0)])  1.92 us
    ppermute x1, starting transfers between devices, on_device(): across = lax.ppermute(own, 'core', [(0, 1), (1, 0)])  1.91 us
  transfers between devices with their start and end apart: 9, of which 6 were waited for; matrix products, arithmetic and copies ran while one was open for 0% of the time, Pallas kernels for 7%

profile of v8, /device:TPU:24, one launch (start us, length us, event | category | flops | bytes accessed | tf_op | source)
XLA Modules:
  0.0 84.2 jit_solution(10192763273406618880)
XLA Ops:
  0.0 1.6 %shard_map.37 = (f32[32,16,512]{2,1,0:T(8,128)S(1)}, bf16[32,512]{1,0:T(8,128)(2,1)S(1)}) custom-call(s32[1,512]{1,0:T(1,128)} %bitcast.4, f32[512,384]{1,0:T(8,128)} %matrix_ref.1, f32[32,512]{1,0:T(8,128)} %bitcast.7), custom_call_target="tpu_custom_call" | custom-call | flops 201326592 | bytes 1572864 | tf_op jit(solution)/shard_map/pallas_call | solution.py:284
  1.6 0.9 %convert_element_type.12 = f16[32,16,512]{2,1,0:T(8,128)(2,1)} convert(f32[32,16,512]{2,1,0:T(8,128)S(1)} %get-tuple-element.21) | non-fusion elementwise | flops 262144 | bytes 1572864 | tf_op jit(solution)/shard_map/convert_element_type | solution.py:297
  2.5 0.0 copy-start
  2.5 0.0 copy-start.1
  2.5 13.7 %all-to-all-start = ((f16[32,16,512]{2,1,0:T(8,128)(2,1)}), f16[32,16,512]{2,1,0:T(8,128)(2,1)S(1)}, u32[]{:S(2)}, u32[]{:S(2)}) async-start(f16[32,16,512]{2,1,0:T(8,128)(2,1)} %convert_element_type.12), calls=%async_computation | async-start | bytes 1048576 | tf_op jit(solution)/shard_map/all_to_all | solution.py:269
  16.2 5.0 %collective-permute-start = (bf16[32,512]{1,0:T(8,128)(2,1)S(1)}, bf16[32,512]{1,0:T(8,128)(2,1)S(1)}, u32[]{:S(2)}, u32[]{:S(2)}) collective-permute-start(bf16[32,512]{1,0:T(8,128)(2,1)S(1)} %get-tuple-element.22), channel_id=1, source_target_pairs={{0,8},{2,10},{4,12},{6,14},{8,0},{10,2},{12,4},{14,6},{1,9},{3,11}... | collective-permute-start | bytes 98312 | tf_op jit(solution)/shard_map/ppermute | solution.py:307
  21.3 4.0 %collective-permute-start.1 = (bf16[32,512]{1,0:T(8,128)(2,1)S(1)}, bf16[32,512]{1,0:T(8,128)(2,1)S(1)}, u32[]{:S(2)}, u32[]{:S(2)}) collective-permute-start(bf16[32,512]{1,0:T(8,128)(2,1)S(1)} %get-tuple-element.22), channel_id=1, source_target_pairs={{0,12},{2,14},{4,0},{6,2},{8,4},{10,6},{12,8},{14,10},{1,13},{3,15... | collective-permute-start | bytes 98312 | tf_op jit(solution)/shard_map/ppermute | solution.py:307
  25.3 0.0 copy-done
  25.3 0.0 copy-done.1
  25.4 1.1 %shard_map.39 = (bf16[512,512]{1,0:T(8,128)(2,1)S(1)}, f32[512,384]{1,0:T(8,128)S(1)}) custom-call(s32[1,512]{1,0:T(1,128)S(1)} %bitcast.5, f32[512,384]{1,0:T(8,128)S(1)} %copy-done), custom_call_target="tpu_custom_call" | custom-call | flops 536870912 | bytes 3145728 | tf_op jit(solution)/shard_map/pallas_call | solution.py:299
  26.5 7.1 %all-to-all-done = f16[32,16,512]{2,1,0:T(8,128)(2,1)S(1)} async-done(((f16[32,16,512]{2,1,0:T(8,128)(2,1)}), f16[32,16,512]{2,1,0:T(8,128)(2,1)S(1)}, u32[]{:S(2)}, u32[]{:S(2)}) %all-to-all-start) | async-done | bytes 524320 | tf_op jit(solution)/shard_map/all_to_all | solution.py:269
  33.6 0.0 collective-permute-done
  33.6 0.0 collective-permute-done.1
  33.6 0.7 broadcast_in_dim.2
  34.3 9.9 %all-to-all-start.1 = ((f16[64,16,128]{2,1,0:T(8,128)(2,1)}), f16[64,16,128]{2,1,0:T(8,128)(2,1)S(1)}, u32[]{:S(2)}, u32[]{:S(2)}) async-start(f16[64,16,128]{2,1,0:T(8,128)(2,1)} %broadcast_in_dim.2), calls=%async_computation.1 | async-start | bytes 524288 | tf_op jit(solution)/shard_map/all_to_all | solution.py:269
  44.2 2.4 %collective-permute-start.2 = (bf16[96,512]{1,0:T(8,128)(2,1)S(1)}, bf16[96,512]{1,0:T(8,128)(2,1)S(1)}, u32[]{:S(2)}, u32[]{:S(2)}) collective-permute-start(bf16[96,512]{1,0:T(8,128)(2,1)S(1)} %pad_maximum_fusion), channel_id=1, source_target_pairs={{0,14},{2,0},{4,2},{6,4},{8,6},{10,8},{12,10},{14,12},{1,15},{3,1}... | collective-permute-start | bytes 294920 | tf_op jit(solution)/shard_map/ppermute | solution.py:307
  46.7 0.1 convert_element_type.13.got_ref
  46.8 1.1 %shard_map.38 = bf16[32,16,768]{2,1,0:T(8,128)(2,1)} custom-call(f32[32,16,512]{2,1,0:T(8,128)S(1)} %convert_element_type.13.got_ref), custom_call_target="tpu_custom_call" | custom-call | flops 196608 | bytes 786432 | tf_op jit(solution)/shard_map/pallas_call | solution.py:314
  47.9 5.2 %collective-permute-done.2 = bf16[96,512]{1,0:T(8,128)(2,1)S(1)} collective-permute-done((bf16[96,512]{1,0:T(8,128)(2,1)S(1)}, bf16[96,512]{1,0:T(8,128)(2,1)S(1)}, u32[]{:S(2)}, u32[]{:S(2)}) %collective-permute-start.2) | collective-permute-done | bytes 98336 | tf_op jit(solution)/shard_map/ppermute | solution.py:307
  53.1 1.8 %all-to-all-done.1 = f16[64,16,128]{2,1,0:T(8,128)(2,1)S(1)} async-done(((f16[64,16,128]{2,1,0:T(8,128)(2,1)}), f16[64,16,128]{2,1,0:T(8,128)(2,1)S(1)}, u32[]{:S(2)}, u32[]{:S(2)}) %all-to-all-start.1) | async-done | bytes 262176 | tf_op jit(solution)/shard_map/all_to_all | solution.py:269
  54.9 5.1 %all-to-all-start.2 = ((bf16[32,16,768]{2,1,0:T(8,128)(2,1)}), bf16[32,16,768]{2,1,0:T(8,128)(2,1)S(1)}, u32[]{:S(2)}, u32[]{:S(2)}) async-start(bf16[32,16,768]{2,1,0:T(8,128)(2,1)} %shard_map.38), calls=%async_computation.2 | async-start | bytes 1572864 | tf_op jit(solution)/shard_map/all_to_all | solution.py:269
  60.0 1.9 %collective-permute-start.3 = (f16[64,16,128]{2,1,0:T(8,128)(2,1)S(1)}, f16[64,16,128]{2,1,0:T(8,128)(2,1)S(1)}, u32[]{:S(2)}, u32[]{:S(2)}) collective-permute-start(f16[64,16,128]{2,1,0:T(8,128)(2,1)S(1)} %all-to-all-done.1), channel_id=1, source_target_pairs={{0,1},{1,0},{2,3},{3,2},{4,5},{5,4},{6,7},{7,6},{8,9},{9,8},{10,11... | collective-permute-start | bytes 786440 | tf_op jit(solution)/shard_map/ppermute | solution.py:322
  62.0 2.7 %collective-permute-start.4 = (bf16[64,512]{1,0:T(8,128)(2,1)S(1)}, bf16[64,512]{1,0:T(8,128)(2,1)S(1)}, u32[]{:S(2)}, u32[]{:S(2)}) collective-permute-start(bf16[64,512]{1,0:T(8,128)(2,1)S(1)} %pad_maximum_fusion.1), channel_id=1, source_target_pairs={{0,4},{2,6},{4,8},{6,10},{8,12},{10,14},{12,0},{14,2},{1,5},{3,7},... | collective-permute-start | bytes 196616 | tf_op jit(solution)/shard_map/ppermute | solution.py:307
  64.7 0.0 collective-permute-done.3
  64.8 3.5 %shard_map.40 = (bf16[2,6,128,128]{3,2,1,0:T(8,128)(2,1)S(1)}, bf16[2,4,128,128]{3,2,1,0:T(8,128)(2,1)S(1)}) custom-call(f32[64,16,128]{2,1,0:T(8,128)S(1)} %convert_element_type.14.mine_ref, f32[64,16,128]{2,1,0:T(8,128)S(1)} %convert_element_type.15.other_ref), custom_call_target="tpu_custom_call" | custom-call | flops 1342177280 | bytes 8388608 | tf_op jit(solution)/shard_map/pallas_call | solution.py:324
  68.3 2.4 %collective-permute-done.4 = bf16[64,512]{1,0:T(8,128)(2,1)S(1)} collective-permute-done((bf16[64,512]{1,0:T(8,128)(2,1)S(1)}, bf16[64,512]{1,0:T(8,128)(2,1)S(1)}, u32[]{:S(2)}, u32[]{:S(2)}) %collective-permute-start.4) | collective-permute-done | bytes 65568 | tf_op jit(solution)/shard_map/ppermute | solution.py:307
  70.7 1.9 %collective-permute-start.5 = (bf16[256,512]{1,0:T(8,128)(2,1)S(1)}, bf16[256,512]{1,0:T(8,128)(2,1)S(1)}, u32[]{:S(2)}, u32[]{:S(2)}) collective-permute-start(bf16[256,512]{1,0:T(8,128)(2,1)S(1)} %constant_dynamic-update-slice_fusion.own_ref), channel_id=1, source_target_pairs={{0,1},{1,0},{2,3},{3,2},{4,5},{5,4},{6,7},{7,6},{8,9},{9,8},{10,11... | collective-permute-start | bytes 786440 | tf_op jit(solution)/shard_map/ppermute | solution.py:333
  72.6 1.5 %collective-permute-done.5.across_ref = bf16[256,512]{1,0:T(8,128)(2,1)S(1)} collective-permute-done((bf16[256,512]{1,0:T(8,128)(2,1)S(1)}, bf16[256,512]{1,0:T(8,128)(2,1)S(1)}, u32[]{:S(2)}, u32[]{:S(2)}) %collective-permute-start.5) | collective-permute-done | bytes 262176 | tf_op jit(solution)/shard_map/ppermute | solution.py:333
  74.1 0.2 shard_map.41.weights_ref
  74.4 7.6 %all-to-all-done.2.got_ref = bf16[32,16,768]{2,1,0:T(8,128)(2,1)S(1)} async-done(((bf16[32,16,768]{2,1,0:T(8,128)(2,1)}), bf16[32,16,768]{2,1,0:T(8,128)(2,1)S(1)}, u32[]{:S(2)}, u32[]{:S(2)}) %all-to-all-start.2) | async-done | bytes 786464 | tf_op jit(solution)/shard_map/all_to_all | solution.py:269
  82.0 2.2 %shard_map.42 = f32[512,384]{1,0:T(8,128)} custom-call(s32[1,512]{1,0:T(1,128)S(1)} %bitcast.6, bf16[32,16,768]{2,1,0:T(8,128)(2,1)S(1)} %all-to-all-done.2.got_ref, f32[512,384]{1,0:T(8,128)S(1)} %get-tuple-element.29.kept_ref, bf16[2,6,128,128]{3,2,1,0:T(8,128)(2,1)S(1)} %get-tuple-element.31.below_ref, ...), custom_call_target="tpu_custom_call" | custom-call | flops 805306368 | bytes 9437184 | tf_op jit(solution)/shard_map/pallas_call | solution.py:341
  (11 shorter events, 0.1 us)
Async XLA Ops:
  2.5 22.8 %copy-start = (f32[512,384]{1,0:T(8,128)S(1)}, f32[512,384]{1,0:T(8,128)}, u32[]{:S(2)}) copy-start(f32[512,384]{1,0:T(8,128)} %matrix_ref.1) | copy-start | bytes 2359300
  2.5 22.8 %copy-start.1 = (s32[512]{0:T(512)S(1)}, s32[512]{0:T(512)}, u32[]{:S(2)}) copy-start(s32[512]{0:T(512)} %param.5) | copy-start | bytes 6148
  2.5 31.0 %all-to-all-start = ((f16[32,16,512]{2,1,0:T(8,128)(2,1)}), f16[32,16,512]{2,1,0:T(8,128)(2,1)S(1)}, u32[]{:S(2)}, u32[]{:S(2)}) async-start(f16[32,16,512]{2,1,0:T(8,128)(2,1)} %convert_element_type.12), calls=%async_computation | async-start | bytes 1048576 | tf_op jit(solution)/shard_map/all_to_all | solution.py:269
  16.2 17.3 %collective-permute-start = (bf16[32,512]{1,0:T(8,128)(2,1)S(1)}, bf16[32,512]{1,0:T(8,128)(2,1)S(1)}, u32[]{:S(2)}, u32[]{:S(2)}) collective-permute-start(bf16[32,512]{1,0:T(8,128)(2,1)S(1)} %get-tuple-element.22), channel_id=1, source_target_pairs={{0,8},{2,10},{4,12},{6,14},{8,0},{10,2},{12,4},{14,6},{1,9},{3,11}... | collective-permute-start | bytes 98312 | tf_op jit(solution)/shard_map/ppermute | solution.py:307
  21.3 12.3 %collective-permute-start.1 = (bf16[32,512]{1,0:T(8,128)(2,1)S(1)}, bf16[32,512]{1,0:T(8,128)(2,1)S(1)}, u32[]{:S(2)}, u32[]{:S(2)}) collective-permute-start(bf16[32,512]{1,0:T(8,128)(2,1)S(1)} %get-tuple-element.22), channel_id=1, source_target_pairs={{0,12},{2,14},{4,0},{6,2},{8,4},{10,6},{12,8},{14,10},{1,13},{3,15... | collective-permute-start | bytes 98312 | tf_op jit(solution)/shard_map/ppermute | solution.py:307
  34.3 20.6 %all-to-all-start.1 = ((f16[64,16,128]{2,1,0:T(8,128)(2,1)}), f16[64,16,128]{2,1,0:T(8,128)(2,1)S(1)}, u32[]{:S(2)}, u32[]{:S(2)}) async-start(f16[64,16,128]{2,1,0:T(8,128)(2,1)} %broadcast_in_dim.2), calls=%async_computation.1 | async-start | bytes 524288 | tf_op jit(solution)/shard_map/all_to_all | solution.py:269
  44.2 8.9 %collective-permute-start.2 = (bf16[96,512]{1,0:T(8,128)(2,1)S(1)}, bf16[96,512]{1,0:T(8,128)(2,1)S(1)}, u32[]{:S(2)}, u32[]{:S(2)}) collective-permute-start(bf16[96,512]{1,0:T(8,128)(2,1)S(1)} %pad_maximum_fusion), channel_id=1, source_target_pairs={{0,14},{2,0},{4,2},{6,4},{8,6},{10,8},{12,10},{14,12},{1,15},{3,1}... | collective-permute-start | bytes 294920 | tf_op jit(solution)/shard_map/ppermute | solution.py:307
  54.9 27.1 %all-to-all-start.2 = ((bf16[32,16,768]{2,1,0:T(8,128)(2,1)}), bf16[32,16,768]{2,1,0:T(8,128)(2,1)S(1)}, u32[]{:S(2)}, u32[]{:S(2)}) async-start(bf16[32,16,768]{2,1,0:T(8,128)(2,1)} %shard_map.38), calls=%async_computation.2 | async-start | bytes 1572864 | tf_op jit(solution)/shard_map/all_to_all | solution.py:269
  60.0 4.7 %collective-permute-start.3 = (f16[64,16,128]{2,1,0:T(8,128)(2,1)S(1)}, f16[64,16,128]{2,1,0:T(8,128)(2,1)S(1)}, u32[]{:S(2)}, u32[]{:S(2)}) collective-permute-start(f16[64,16,128]{2,1,0:T(8,128)(2,1)S(1)} %all-to-all-done.1), channel_id=1, source_target_pairs={{0,1},{1,0},{2,3},{3,2},{4,5},{5,4},{6,7},{7,6},{8,9},{9,8},{10,11... | collective-permute-start | bytes 786440 | tf_op jit(solution)/shard_map/ppermute | solution.py:322
  62.0 8.7 %collective-permute-start.4 = (bf16[64,512]{1,0:T(8,128)(2,1)S(1)}, bf16[64,512]{1,0:T(8,128)(2,1)S(1)}, u32[]{:S(2)}, u32[]{:S(2)}) collective-permute-start(bf16[64,512]{1,0:T(8,128)(2,1)S(1)} %pad_maximum_fusion.1), channel_id=1, source_target_pairs={{0,4},{2,6},{4,8},{6,10},{8,12},{10,14},{12,0},{14,2},{1,5},{3,7},... | collective-permute-start | bytes 196616 | tf_op jit(solution)/shard_map/ppermute | solution.py:307
  70.7 3.4 %collective-permute-start.5 = (bf16[256,512]{1,0:T(8,128)(2,1)S(1)}, bf16[256,512]{1,0:T(8,128)(2,1)S(1)}, u32[]{:S(2)}, u32[]{:S(2)}) collective-permute-start(bf16[256,512]{1,0:T(8,128)(2,1)S(1)} %constant_dynamic-update-slice_fusion.own_ref), channel_id=1, source_target_pairs={{0,1},{1,0},{2,3},{3,2},{4,5},{5,4},{6,7},{7,6},{8,9},{9,8},{10,11... | collective-permute-start | bytes 786440 | tf_op jit(solution)/shard_map/ppermute | solution.py:333

commit v9 on v8

--- a/solution.py
+++ b/solution.py
@@ -94,20 +94,21 @@
     own_ref[...] = columns.astype(HALF)
     columns = columns * SCALE
     picks = one_hot(as_column(sources_ref[...]) - myself * rows == iota((width, rows), 1))
-    for copy in large:
-        copy.wait()
-    block = matrix_ref[...]
-    power = range_power(block)
-    block = (block * jnp.exp2(power)).astype(HALF)
-    corner = (iota((each, wide - cols), 0) == 0) & (iota((each, wide - cols), 1) == 0)
     holders = columns.shape[0] // 4
     planes = parts // holders
     for holder in range(holders):
         high = 4 * holder
         piece = jnp.concatenate([columns[high : high + 4, 128 * q : 128 * q + 128] for q in range(4)], axis=0)
-        piece = jnp.where(corner, power, piece)
         for part in range(planes * holder, planes * holder + planes):
             out_ref[part, :, cols:wide] = piece
+
+    for copy in large:
+        copy.wait()
+    block = matrix_ref[...]
+    power = range_power(block)
+    for part in range(parts):
+        out_ref[part, 0:1, cols : cols + 1] = power
+    block = (block * jnp.exp2(power)).astype(HALF)
 
     @pl.when(myself == 0)
     def _():

time: 84.8 us -> 84.8 us (level)
  no operation moved by 1% of the time
where the time goes in v9:
time: 84.8 us; the launch traced here: 84.2 us
  starting transfers between devices  46.7 us (55%)
  waiting for transfers between devices  25.6 us (30%)
  Pallas kernels  9.81 us (12%)
  other arithmetic  1.12 us (1%)
    all_to_all x3, starting transfers between devices, exchange(): return lax.all_to_all(blocks, axes, 0, 0, tiled=False)  28.7 us
    all_to_all x3, waiting for transfers between devices, exchange(): return lax.all_to_all(blocks, axes, 0, 0, tiled=False)  16.5 us
    ppermute x4, starting transfers between devices, bring(): lax.ppermute(block, 'y', [(i, (i - ahead) % chips) for i in range(chips)])  14.2 us
    ppermute x4, waiting for transfers between devices, bring(): lax.ppermute(block, 'y', [(i, (i - ahead) % chips) for i in range(chips)])  7.65 us
    pallas_call x1, Pallas kernels, on_device(): call(invert_kernel, (jax.ShapeDtypeStruct((2, 6, 128, 128), HALF), jax.Sh...  3.5 us
    pallas_call x1, Pallas kernels, on_device(): call(finish_kernel, jax.ShapeDtypeStruct((rows, cols), f32), 8 * rows * c...  2.23 us
    ppermute x1, starting transfers between devices, on_device(): other = lax.ppermute(mine, 'core', [(0, 1), (1, 0)])  1.92 us
    ppermute x1, starting transfers between devices, on_device(): across = lax.ppermute(own, 'core', [(0, 1), (1, 0)])  1.91 us
  transfers between devices with their start and end apart: 9, of which 6 were waited for; matrix products, arithmetic and copies ran while one was open for 0% of the time, Pallas kernels for 7%

profile of v9, /device:TPU:24, one launch (start us, length us, event | category | flops | bytes accessed | tf_op | source)
XLA Modules:
  0.0 84.2 jit_solution(10257525002995780267)
XLA Ops:
  0.0 1.6 %shard_map.37 = (f32[32,16,512]{2,1,0:T(8,128)S(1)}, bf16[32,512]{1,0:T(8,128)(2,1)S(1)}) custom-call(s32[1,512]{1,0:T(1,128)} %bitcast.4, f32[512,384]{1,0:T(8,128)} %matrix_ref.1, f32[32,512]{1,0:T(8,128)} %bitcast.7), custom_call_target="tpu_custom_call" | custom-call | flops 201326592 | bytes 1572864 | tf_op jit(solution)/shard_map/pallas_call | solution.py:285
  1.6 0.9 %convert_element_type.12 = f16[32,16,512]{2,1,0:T(8,128)(2,1)} convert(f32[32,16,512]{2,1,0:T(8,128)S(1)} %get-tuple-element.21) | non-fusion elementwise | flops 262144 | bytes 1572864 | tf_op jit(solution)/shard_map/convert_element_type | solution.py:298
  2.5 0.0 copy-start
  2.5 0.0 copy-start.1
  2.5 13.7 %all-to-all-start = ((f16[32,16,512]{2,1,0:T(8,128)(2,1)}), f16[32,16,512]{2,1,0:T(8,128)(2,1)S(1)}, u32[]{:S(2)}, u32[]{:S(2)}) async-start(f16[32,16,512]{2,1,0:T(8,128)(2,1)} %convert_element_type.12), calls=%async_computation | async-start | bytes 1048576 | tf_op jit(solution)/shard_map/all_to_all | solution.py:270
  16.2 5.0 %collective-permute-start = (bf16[32,512]{1,0:T(8,128)(2,1)S(1)}, bf16[32,512]{1,0:T(8,128)(2,1)S(1)}, u32[]{:S(2)}, u32[]{:S(2)}) collective-permute-start(bf16[32,512]{1,0:T(8,128)(2,1)S(1)} %get-tuple-element.22), channel_id=1, source_target_pairs={{0,8},{2,10},{4,12},{6,14},{8,0},{10,2},{12,4},{14,6},{1,9},{3,11}... | collective-permute-start | bytes 98312 | tf_op jit(solution)/shard_map/ppermute | solution.py:308
  21.3 4.0 %collective-permute-start.1 = (bf16[32,512]{1,0:T(8,128)(2,1)S(1)}, bf16[32,512]{1,0:T(8,128)(2,1)S(1)}, u32[]{:S(2)}, u32[]{:S(2)}) collective-permute-start(bf16[32,512]{1,0:T(8,128)(2,1)S(1)} %get-tuple-element.22), channel_id=1, source_target_pairs={{0,12},{2,14},{4,0},{6,2},{8,4},{10,6},{12,8},{14,10},{1,13},{3,15... | collective-permute-start | bytes 98312 | tf_op jit(solution)/shard_map/ppermute | solution.py:308
  25.3 0.0 copy-done
  25.3 0.0 copy-done.1
  25.4 1.1 %shard_map.39 = (bf16[512,512]{1,0:T(8,128)(2,1)S(1)}, f32[512,384]{1,0:T(8,128)S(1)}) custom-call(s32[1,512]{1,0:T(1,128)S(1)} %bitcast.5, f32[512,384]{1,0:T(8,128)S(1)} %copy-done), custom_call_target="tpu_custom_call" | custom-call | flops 536870912 | bytes 3145728 | tf_op jit(solution)/shard_map/pallas_call | solution.py:300
  26.5 7.1 %all-to-all-done = f16[32,16,512]{2,1,0:T(8,128)(2,1)S(1)} async-done(((f16[32,16,512]{2,1,0:T(8,128)(2,1)}), f16[32,16,512]{2,1,0:T(8,128)(2,1)S(1)}, u32[]{:S(2)}, u32[]{:S(2)}) %all-to-all-start) | async-done | bytes 524320 | tf_op jit(solution)/shard_map/all_to_all | solution.py:270
  33.6 0.0 collective-permute-done
  33.6 0.0 collective-permute-done.1
  33.6 0.7 broadcast_in_dim.2
  34.3 9.9 %all-to-all-start.1 = ((f16[64,16,128]{2,1,0:T(8,128)(2,1)}), f16[64,16,128]{2,1,0:T(8,128)(2,1)S(1)}, u32[]{:S(2)}, u32[]{:S(2)}) async-start(f16[64,16,128]{2,1,0:T(8,128)(2,1)} %broadcast_in_dim.2), calls=%async_computation.1 | async-start | bytes 524288 | tf_op jit(solution)/shard_map/all_to_all | solution.py:270
  44.2 2.4 %collective-permute-start.2 = (bf16[96,512]{1,0:T(8,128)(2,1)S(1)}, bf16[96,512]{1,0:T(8,128)(2,1)S(1)}, u32[]{:S(2)}, u32[]{:S(2)}) collective-permute-start(bf16[96,512]{1,0:T(8,128)(2,1)S(1)} %pad_maximum_fusion), channel_id=1, source_target_pairs={{0,14},{2,0},{4,2},{6,4},{8,6},{10,8},{12,10},{14,12},{1,15},{3,1}... | collective-permute-start | bytes 294920 | tf_op jit(solution)/shard_map/ppermute | solution.py:308
  46.7 0.1 convert_element_type.13.got_ref
  46.8 1.1 %shard_map.38 = bf16[32,16,768]{2,1,0:T(8,128)(2,1)} custom-call(f32[32,16,512]{2,1,0:T(8,128)S(1)} %convert_element_type.13.got_ref), custom_call_target="tpu_custom_call" | custom-call | flops 196608 | bytes 786432 | tf_op jit(solution)/shard_map/pallas_call | solution.py:315
  47.9 5.2 %collective-permute-done.2 = bf16[96,512]{1,0:T(8,128)(2,1)S(1)} collective-permute-done((bf16[96,512]{1,0:T(8,128)(2,1)S(1)}, bf16[96,512]{1,0:T(8,128)(2,1)S(1)}, u32[]{:S(2)}, u32[]{:S(2)}) %collective-permute-start.2) | collective-permute-done | bytes 98336 | tf_op jit(solution)/shard_map/ppermute | solution.py:308
  53.1 1.8 %all-to-all-done.1 = f16[64,16,128]{2,1,0:T(8,128)(2,1)S(1)} async-done(((f16[64,16,128]{2,1,0:T(8,128)(2,1)}), f16[64,16,128]{2,1,0:T(8,128)(2,1)S(1)}, u32[]{:S(2)}, u32[]{:S(2)}) %all-to-all-start.1) | async-done | bytes 262176 | tf_op jit(solution)/shard_map/all_to_all | solution.py:270
  54.9 5.1 %all-to-all-start.2 = ((bf16[32,16,768]{2,1,0:T(8,128)(2,1)}), bf16[32,16,768]{2,1,0:T(8,128)(2,1)S(1)}, u32[]{:S(2)}, u32[]{:S(2)}) async-start(bf16[32,16,768]{2,1,0:T(8,128)(2,1)} %shard_map.38), calls=%async_computation.2 | async-start | bytes 1572864 | tf_op jit(solution)/shard_map/all_to_all | solution.py:270
  60.0 1.9 %collective-permute-start.3 = (f16[64,16,128]{2,1,0:T(8,128)(2,1)S(1)}, f16[64,16,128]{2,1,0:T(8,128)(2,1)S(1)}, u32[]{:S(2)}, u32[]{:S(2)}) collective-permute-start(f16[64,16,128]{2,1,0:T(8,128)(2,1)S(1)} %all-to-all-done.1), channel_id=1, source_target_pairs={{0,1},{1,0},{2,3},{3,2},{4,5},{5,4},{6,7},{7,6},{8,9},{9,8},{10,11... | collective-permute-start | bytes 786440 | tf_op jit(solution)/shard_map/ppermute | solution.py:323
  62.0 2.7 %collective-permute-start.4 = (bf16[64,512]{1,0:T(8,128)(2,1)S(1)}, bf16[64,512]{1,0:T(8,128)(2,1)S(1)}, u32[]{:S(2)}, u32[]{:S(2)}) collective-permute-start(bf16[64,512]{1,0:T(8,128)(2,1)S(1)} %pad_maximum_fusion.1), channel_id=1, source_target_pairs={{0,4},{2,6},{4,8},{6,10},{8,12},{10,14},{12,0},{14,2},{1,5},{3,7},... | collective-permute-start | bytes 196616 | tf_op jit(solution)/shard_map/ppermute | solution.py:308
  64.7 0.0 collective-permute-done.3
  64.8 3.5 %shard_map.40 = (bf16[2,6,128,128]{3,2,1,0:T(8,128)(2,1)S(1)}, bf16[2,4,128,128]{3,2,1,0:T(8,128)(2,1)S(1)}) custom-call(f32[64,16,128]{2,1,0:T(8,128)S(1)} %convert_element_type.14.mine_ref, f32[64,16,128]{2,1,0:T(8,128)S(1)} %convert_element_type.15.other_ref), custom_call_target="tpu_custom_call" | custom-call | flops 1342177280 | bytes 8388608 | tf_op jit(solution)/shard_map/pallas_call | solution.py:325
  68.3 2.4 %collective-permute-done.4 = bf16[64,512]{1,0:T(8,128)(2,1)S(1)} collective-permute-done((bf16[64,512]{1,0:T(8,128)(2,1)S(1)}, bf16[64,512]{1,0:T(8,128)(2,1)S(1)}, u32[]{:S(2)}, u32[]{:S(2)}) %collective-permute-start.4) | collective-permute-done | bytes 65568 | tf_op jit(solution)/shard_map/ppermute | solution.py:308
  70.7 1.9 %collective-permute-start.5 = (bf16[256,512]{1,0:T(8,128)(2,1)S(1)}, bf16[256,512]{1,0:T(8,128)(2,1)S(1)}, u32[]{:S(2)}, u32[]{:S(2)}) collective-permute-start(bf16[256,512]{1,0:T(8,128)(2,1)S(1)} %constant_dynamic-update-slice_fusion.own_ref), channel_id=1, source_target_pairs={{0,1},{1,0},{2,3},{3,2},{4,5},{5,4},{6,7},{7,6},{8,9},{9,8},{10,11... | collective-permute-start | bytes 786440 | tf_op jit(solution)/shard_map/ppermute | solution.py:334
  72.6 1.5 %collective-permute-done.5.across_ref = bf16[256,512]{1,0:T(8,128)(2,1)S(1)} collective-permute-done((bf16[256,512]{1,0:T(8,128)(2,1)S(1)}, bf16[256,512]{1,0:T(8,128)(2,1)S(1)}, u32[]{:S(2)}, u32[]{:S(2)}) %collective-permute-start.5) | collective-permute-done | bytes 262176 | tf_op jit(solution)/shard_map/ppermute | solution.py:334
  74.1 0.2 shard_map.41.weights_ref
  74.4 7.6 %all-to-all-done.2.got_ref = bf16[32,16,768]{2,1,0:T(8,128)(2,1)S(1)} async-done(((bf16[32,16,768]{2,1,0:T(8,128)(2,1)}), bf16[32,16,768]{2,1,0:T(8,128)(2,1)S(1)}, u32[]{:S(2)}, u32[]{:S(2)}) %all-to-all-start.2) | async-done | bytes 786464 | tf_op jit(solution)/shard_map/all_to_all | solution.py:270
  82.0 2.2 %shard_map.42 = f32[512,384]{1,0:T(8,128)} custom-call(s32[1,512]{1,0:T(1,128)S(1)} %bitcast.6, bf16[32,16,768]{2,1,0:T(8,128)(2,1)S(1)} %all-to-all-done.2.got_ref, f32[512,384]{1,0:T(8,128)S(1)} %get-tuple-element.29.kept_ref, bf16[2,6,128,128]{3,2,1,0:T(8,128)(2,1)S(1)} %get-tuple-element.31.below_ref, ...), custom_call_target="tpu_custom_call" | custom-call | flops 805306368 | bytes 9437184 | tf_op jit(solution)/shard_map/pallas_call | solution.py:342
  (11 shorter events, 0.1 us)
Async XLA Ops:
  2.5 22.8 %copy-start = (f32[512,384]{1,0:T(8,128)S(1)}, f32[512,384]{1,0:T(8,128)}, u32[]{:S(2)}) copy-start(f32[512,384]{1,0:T(8,128)} %matrix_ref.1) | copy-start | bytes 2359300
  2.5 22.8 %copy-start.1 = (s32[512]{0:T(512)S(1)}, s32[512]{0:T(512)}, u32[]{:S(2)}) copy-start(s32[512]{0:T(512)} %param.5) | copy-start | bytes 6148
  2.5 31.0 %all-to-all-start = ((f16[32,16,512]{2,1,0:T(8,128)(2,1)}), f16[32,16,512]{2,1,0:T(8,128)(2,1)S(1)}, u32[]{:S(2)}, u32[]{:S(2)}) async-start(f16[32,16,512]{2,1,0:T(8,128)(2,1)} %convert_element_type.12), calls=%async_computation | async-start | bytes 1048576 | tf_op jit(solution)/shard_map/all_to_all | solution.py:270
  16.2 17.3 %collective-permute-start = (bf16[32,512]{1,0:T(8,128)(2,1)S(1)}, bf16[32,512]{1,0:T(8,128)(2,1)S(1)}, u32[]{:S(2)}, u32[]{:S(2)}) collective-permute-start(bf16[32,512]{1,0:T(8,128)(2,1)S(1)} %get-tuple-element.22), channel_id=1, source_target_pairs={{0,8},{2,10},{4,12},{6,14},{8,0},{10,2},{12,4},{14,6},{1,9},{3,11}... | collective-permute-start | bytes 98312 | tf_op jit(solution)/shard_map/ppermute | solution.py:308
  21.3 12.3 %collective-permute-start.1 = (bf16[32,512]{1,0:T(8,128)(2,1)S(1)}, bf16[32,512]{1,0:T(8,128)(2,1)S(1)}, u32[]{:S(2)}, u32[]{:S(2)}) collective-permute-start(bf16[32,512]{1,0:T(8,128)(2,1)S(1)} %get-tuple-element.22), channel_id=1, source_target_pairs={{0,12},{2,14},{4,0},{6,2},{8,4},{10,6},{12,8},{14,10},{1,13},{3,15... | collective-permute-start | bytes 98312 | tf_op jit(solution)/shard_map/ppermute | solution.py:308
  34.3 20.6 %all-to-all-start.1 = ((f16[64,16,128]{2,1,0:T(8,128)(2,1)}), f16[64,16,128]{2,1,0:T(8,128)(2,1)S(1)}, u32[]{:S(2)}, u32[]{:S(2)}) async-start(f16[64,16,128]{2,1,0:T(8,128)(2,1)} %broadcast_in_dim.2), calls=%async_computation.1 | async-start | bytes 524288 | tf_op jit(solution)/shard_map/all_to_all | solution.py:270
  44.2 8.9 %collective-permute-start.2 = (bf16[96,512]{1,0:T(8,128)(2,1)S(1)}, bf16[96,512]{1,0:T(8,128)(2,1)S(1)}, u32[]{:S(2)}, u32[]{:S(2)}) collective-permute-start(bf16[96,512]{1,0:T(8,128)(2,1)S(1)} %pad_maximum_fusion), channel_id=1, source_target_pairs={{0,14},{2,0},{4,2},{6,4},{8,6},{10,8},{12,10},{14,12},{1,15},{3,1}... | collective-permute-start | bytes 294920 | tf_op jit(solution)/shard_map/ppermute | solution.py:308
  54.9 27.1 %all-to-all-start.2 = ((bf16[32,16,768]{2,1,0:T(8,128)(2,1)}), bf16[32,16,768]{2,1,0:T(8,128)(2,1)S(1)}, u32[]{:S(2)}, u32[]{:S(2)}) async-start(bf16[32,16,768]{2,1,0:T(8,128)(2,1)} %shard_map.38), calls=%async_computation.2 | async-start | bytes 1572864 | tf_op jit(solution)/shard_map/all_to_all | solution.py:270
  60.0 4.7 %collective-permute-start.3 = (f16[64,16,128]{2,1,0:T(8,128)(2,1)S(1)}, f16[64,16,128]{2,1,0:T(8,128)(2,1)S(1)}, u32[]{:S(2)}, u32[]{:S(2)}) collective-permute-start(f16[64,16,128]{2,1,0:T(8,128)(2,1)S(1)} %all-to-all-done.1), channel_id=1, source_target_pairs={{0,1},{1,0},{2,3},{3,2},{4,5},{5,4},{6,7},{7,6},{8,9},{9,8},{10,11... | collective-permute-start | bytes 786440 | tf_op jit(solution)/shard_map/ppermute | solution.py:323
  62.0 8.7 %collective-permute-start.4 = (bf16[64,512]{1,0:T(8,128)(2,1)S(1)}, bf16[64,512]{1,0:T(8,128)(2,1)S(1)}, u32[]{:S(2)}, u32[]{:S(2)}) collective-permute-start(bf16[64,512]{1,0:T(8,128)(2,1)S(1)} %pad_maximum_fusion.1), channel_id=1, source_target_pairs={{0,4},{2,6},{4,8},{6,10},{8,12},{10,14},{12,0},{14,2},{1,5},{3,7},... | collective-permute-start | bytes 196616 | tf_op jit(solution)/shard_map/ppermute | solution.py:308
  70.7 3.4 %collective-permute-start.5 = (bf16[256,512]{1,0:T(8,128)(2,1)S(1)}, bf16[256,512]{1,0:T(8,128)(2,1)S(1)}, u32[]{:S(2)}, u32[]{:S(2)}) collective-permute-start(bf16[256,512]{1,0:T(8,128)(2,1)S(1)} %constant_dynamic-update-slice_fusion.own_ref), channel_id=1, source_target_pairs={{0,1},{1,0},{2,3},{3,2},{4,5},{5,4},{6,7},{7,6},{8,9},{9,8},{10,11... | collective-permute-start | bytes 786440 | tf_op jit(solution)/shard_map/ppermute | solution.py:334

commit v10 on v9

--- a/solution.py
+++ b/solution.py
@@ -85,14 +85,14 @@
     for at in range(4):
         here = pl.ds(at * quarter, quarter)
         large.append(pltpu.make_async_copy(matrix_hbm.at[here], matrix_ref.at[here], sems.at[2 + at]))
-    for copy in small + large:
+    for copy in small[1:] + large + small[:1]:
         copy.start()
-    for copy in small:
-        copy.wait()
+    small[1].wait()
 
     columns = columns_ref[...]
     own_ref[...] = columns.astype(HALF)
     columns = columns * SCALE
+    small[0].wait()
     picks = one_hot(as_column(sources_ref[...]) - myself * rows == iota((width, rows), 1))
     holders = columns.shape[0] // 4
     planes = parts // holders

time: 84.8 us -> 84.9 us (level)
  no operation moved by 1% of the time
where the time goes in v10:
time: 84.9 us; the launch traced here: 84.3 us
  starting transfers between devices  46.7 us (55%)
  waiting for transfers between devices  25.6 us (30%)
  Pallas kernels  9.9 us (12%)
  other arithmetic  1.12 us (1%)
    all_to_all x3, starting transfers between devices, exchange(): return lax.all_to_all(blocks, axes, 0, 0, tiled=False)  28.7 us
    all_to_all x3, waiting for transfers between devices, exchange(): return lax.all_to_all(blocks, axes, 0, 0, tiled=False)  16.5 us
    ppermute x4, starting transfers between devices, bring(): lax.ppermute(block, 'y', [(i, (i - ahead) % chips) for i in range(chips)])  14.2 us
    ppermute x4, waiting for transfers between devices, bring(): lax.ppermute(block, 'y', [(i, (i - ahead) % chips) for i in range(chips)])  7.65 us
    pallas_call x1, Pallas kernels, on_device(): call(invert_kernel, (jax.ShapeDtypeStruct((2, 6, 128, 128), HALF), jax.Sh...  3.5 us
    pallas_call x1, Pallas kernels, on_device(): call(finish_kernel, jax.ShapeDtypeStruct((rows, cols), f32), 8 * rows * c...  2.24 us
    ppermute x1, starting transfers between devices, on_device(): other = lax.ppermute(mine, 'core', [(0, 1), (1, 0)])  1.92 us
    ppermute x1, starting transfers between devices, on_device(): across = lax.ppermute(own, 'core', [(0, 1), (1, 0)])  1.91 us
  transfers between devices with their start and end apart: 9, of which 6 were waited for; matrix products, arithmetic and copies ran while one was open for 0% of the time, Pallas kernels for 7%

profile of v10, /device:TPU:24, one launch (start us, length us, event | category | flops | bytes accessed | tf_op | source)
XLA Modules:
  0.0 84.3 jit_solution(14572720299516505906)
XLA Ops:
  0.0 1.7 %shard_map.37 = (f32[32,16,512]{2,1,0:T(8,128)S(1)}, bf16[32,512]{1,0:T(8,128)(2,1)S(1)}) custom-call(s32[1,512]{1,0:T(1,128)} %bitcast.4, f32[512,384]{1,0:T(8,128)} %matrix_ref.1, f32[32,512]{1,0:T(8,128)} %bitcast.7), custom_call_target="tpu_custom_call" | custom-call | flops 201326592 | bytes 1572864 | tf_op jit(solution)/shard_map/pallas_call | solution.py:285
  1.7 0.9 %convert_element_type.12 = f16[32,16,512]{2,1,0:T(8,128)(2,1)} convert(f32[32,16,512]{2,1,0:T(8,128)S(1)} %get-tuple-element.21) | non-fusion elementwise | flops 262144 | bytes 1572864 | tf_op jit(solution)/shard_map/convert_element_type | solution.py:298
  2.6 0.0 copy-start
  2.6 0.0 copy-start.1
  2.6 13.7 %all-to-all-start = ((f16[32,16,512]{2,1,0:T(8,128)(2,1)}), f16[32,16,512]{2,1,0:T(8,128)(2,1)S(1)}, u32[]{:S(2)}, u32[]{:S(2)}) async-start(f16[32,16,512]{2,1,0:T(8,128)(2,1)} %convert_element_type.12), calls=%async_computation | async-start | bytes 1048576 | tf_op jit(solution)/shard_map/all_to_all | solution.py:270
  16.3 5.0 %collective-permute-start = (bf16[32,512]{1,0:T(8,128)(2,1)S(1)}, bf16[32,512]{1,0:T(8,128)(2,1)S(1)}, u32[]{:S(2)}, u32[]{:S(2)}) collective-permute-start(bf16[32,512]{1,0:T(8,128)(2,1)S(1)} %get-tuple-element.22), channel_id=1, source_target_pairs={{0,8},{2,10},{4,12},{6,14},{8,0},{10,2},{12,4},{14,6},{1,9},{3,11}... | collective-permute-start | bytes 98312 | tf_op jit(solution)/shard_map/ppermute | solution.py:308
  21.4 4.0 %collective-permute-start.1 = (bf16[32,512]{1,0:T(8,128)(2,1)S(1)}, bf16[32,512]{1,0:T(8,128)(2,1)S(1)}, u32[]{:S(2)}, u32[]{:S(2)}) collective-permute-start(bf16[32,512]{1,0:T(8,128)(2,1)S(1)} %get-tuple-element.22), channel_id=1, source_target_pairs={{0,12},{2,14},{4,0},{6,2},{8,4},{10,6},{12,8},{14,10},{1,13},{3,15... | collective-permute-start | bytes 98312 | tf_op jit(solution)/shard_map/ppermute | solution.py:308
  25.4 0.0 copy-done
  25.4 0.0 copy-done.1
  25.4 1.1 %shard_map.39 = (bf16[512,512]{1,0:T(8,128)(2,1)S(1)}, f32[512,384]{1,0:T(8,128)S(1)}) custom-call(s32[1,512]{1,0:T(1,128)S(1)} %bitcast.5, f32[512,384]{1,0:T(8,128)S(1)} %copy-done), custom_call_target="tpu_custom_call" | custom-call | flops 536870912 | bytes 3145728 | tf_op jit(solution)/shard_map/pallas_call | solution.py:300
  26.6 7.1 %all-to-all-done = f16[32,16,512]{2,1,0:T(8,128)(2,1)S(1)} async-done(((f16[32,16,512]{2,1,0:T(8,128)(2,1)}), f16[32,16,512]{2,1,0:T(8,128)(2,1)S(1)}, u32[]{:S(2)}, u32[]{:S(2)}) %all-to-all-start) | async-done | bytes 524320 | tf_op jit(solution)/shard_map/all_to_all | solution.py:270
  33.7 0.0 collective-permute-done
  33.7 0.0 collective-permute-done.1
  33.7 0.7 broadcast_in_dim.2
  34.4 9.9 %all-to-all-start.1 = ((f16[64,16,128]{2,1,0:T(8,128)(2,1)}), f16[64,16,128]{2,1,0:T(8,128)(2,1)S(1)}, u32[]{:S(2)}, u32[]{:S(2)}) async-start(f16[64,16,128]{2,1,0:T(8,128)(2,1)} %broadcast_in_dim.2), calls=%async_computation.1 | async-start | bytes 524288 | tf_op jit(solution)/shard_map/all_to_all | solution.py:270
  44.3 2.4 %collective-permute-start.2 = (bf16[96,512]{1,0:T(8,128)(2,1)S(1)}, bf16[96,512]{1,0:T(8,128)(2,1)S(1)}, u32[]{:S(2)}, u32[]{:S(2)}) collective-permute-start(bf16[96,512]{1,0:T(8,128)(2,1)S(1)} %pad_maximum_fusion), channel_id=1, source_target_pairs={{0,14},{2,0},{4,2},{6,4},{8,6},{10,8},{12,10},{14,12},{1,15},{3,1}... | collective-permute-start | bytes 294920 | tf_op jit(solution)/shard_map/ppermute | solution.py:308
  46.7 0.1 convert_element_type.13.got_ref
  46.9 1.1 %shard_map.38 = bf16[32,16,768]{2,1,0:T(8,128)(2,1)} custom-call(f32[32,16,512]{2,1,0:T(8,128)S(1)} %convert_element_type.13.got_ref), custom_call_target="tpu_custom_call" | custom-call | flops 196608 | bytes 786432 | tf_op jit(solution)/shard_map/pallas_call | solution.py:315
  48.0 5.2 %collective-permute-done.2 = bf16[96,512]{1,0:T(8,128)(2,1)S(1)} collective-permute-done((bf16[96,512]{1,0:T(8,128)(2,1)S(1)}, bf16[96,512]{1,0:T(8,128)(2,1)S(1)}, u32[]{:S(2)}, u32[]{:S(2)}) %collective-permute-start.2) | collective-permute-done | bytes 98336 | tf_op jit(solution)/shard_map/ppermute | solution.py:308
  53.2 1.8 %all-to-all-done.1 = f16[64,16,128]{2,1,0:T(8,128)(2,1)S(1)} async-done(((f16[64,16,128]{2,1,0:T(8,128)(2,1)}), f16[64,16,128]{2,1,0:T(8,128)(2,1)S(1)}, u32[]{:S(2)}, u32[]{:S(2)}) %all-to-all-start.1) | async-done | bytes 262176 | tf_op jit(solution)/shard_map/all_to_all | solution.py:270
  55.0 5.1 %all-to-all-start.2 = ((bf16[32,16,768]{2,1,0:T(8,128)(2,1)}), bf16[32,16,768]{2,1,0:T(8,128)(2,1)S(1)}, u32[]{:S(2)}, u32[]{:S(2)}) async-start(bf16[32,16,768]{2,1,0:T(8,128)(2,1)} %shard_map.38), calls=%async_computation.2 | async-start | bytes 1572864 | tf_op jit(solution)/shard_map/all_to_all | solution.py:270
  60.1 1.9 %collective-permute-start.3 = (f16[64,16,128]{2,1,0:T(8,128)(2,1)S(1)}, f16[64,16,128]{2,1,0:T(8,128)(2,1)S(1)}, u32[]{:S(2)}, u32[]{:S(2)}) collective-permute-start(f16[64,16,128]{2,1,0:T(8,128)(2,1)S(1)} %all-to-all-done.1), channel_id=1, source_target_pairs={{0,1},{1,0},{2,3},{3,2},{4,5},{5,4},{6,7},{7,6},{8,9},{9,8},{10,11... | collective-permute-start | bytes 786440 | tf_op jit(solution)/shard_map/ppermute | solution.py:323
  62.1 2.7 %collective-permute-start.4 = (bf16[64,512]{1,0:T(8,128)(2,1)S(1)}, bf16[64,512]{1,0:T(8,128)(2,1)S(1)}, u32[]{:S(2)}, u32[]{:S(2)}) collective-permute-start(bf16[64,512]{1,0:T(8,128)(2,1)S(1)} %pad_maximum_fusion.1), channel_id=1, source_target_pairs={{0,4},{2,6},{4,8},{6,10},{8,12},{10,14},{12,0},{14,2},{1,5},{3,7},... | collective-permute-start | bytes 196616 | tf_op jit(solution)/shard_map/ppermute | solution.py:308
  64.8 0.0 collective-permute-done.3
  64.9 3.5 %shard_map.40 = (bf16[2,6,128,128]{3,2,1,0:T(8,128)(2,1)S(1)}, bf16[2,4,128,128]{3,2,1,0:T(8,128)(2,1)S(1)}) custom-call(f32[64,16,128]{2,1,0:T(8,128)S(1)} %convert_element_type.14.mine_ref, f32[64,16,128]{2,1,0:T(8,128)S(1)} %convert_element_type.15.other_ref), custom_call_target="tpu_custom_call" | custom-call | flops 1342177280 | bytes 8388608 | tf_op jit(solution)/shard_map/pallas_call | solution.py:325
  68.4 2.4 %collective-permute-done.4 = bf16[64,512]{1,0:T(8,128)(2,1)S(1)} collective-permute-done((bf16[64,512]{1,0:T(8,128)(2,1)S(1)}, bf16[64,512]{1,0:T(8,128)(2,1)S(1)}, u32[]{:S(2)}, u32[]{:S(2)}) %collective-permute-start.4) | collective-permute-done | bytes 65568 | tf_op jit(solution)/shard_map/ppermute | solution.py:308
  70.8 1.9 %collective-permute-start.5 = (bf16[256,512]{1,0:T(8,128)(2,1)S(1)}, bf16[256,512]{1,0:T(8,128)(2,1)S(1)}, u32[]{:S(2)}, u32[]{:S(2)}) collective-permute-start(bf16[256,512]{1,0:T(8,128)(2,1)S(1)} %constant_dynamic-update-slice_fusion.own_ref), channel_id=1, source_target_pairs={{0,1},{1,0},{2,3},{3,2},{4,5},{5,4},{6,7},{7,6},{8,9},{9,8},{10,11... | collective-permute-start | bytes 786440 | tf_op jit(solution)/shard_map/ppermute | solution.py:334
  72.7 1.5 %collective-permute-done.5.across_ref = bf16[256,512]{1,0:T(8,128)(2,1)S(1)} collective-permute-done((bf16[256,512]{1,0:T(8,128)(2,1)S(1)}, bf16[256,512]{1,0:T(8,128)(2,1)S(1)}, u32[]{:S(2)}, u32[]{:S(2)}) %collective-permute-start.5) | collective-permute-done | bytes 262176 | tf_op jit(solution)/shard_map/ppermute | solution.py:334
  74.2 0.2 shard_map.41.weights_ref
  74.5 7.6 %all-to-all-done.2.got_ref = bf16[32,16,768]{2,1,0:T(8,128)(2,1)S(1)} async-done(((bf16[32,16,768]{2,1,0:T(8,128)(2,1)}), bf16[32,16,768]{2,1,0:T(8,128)(2,1)S(1)}, u32[]{:S(2)}, u32[]{:S(2)}) %all-to-all-start.2) | async-done | bytes 786464 | tf_op jit(solution)/shard_map/all_to_all | solution.py:270
  82.1 2.2 %shard_map.42 = f32[512,384]{1,0:T(8,128)} custom-call(s32[1,512]{1,0:T(1,128)S(1)} %bitcast.6, bf16[32,16,768]{2,1,0:T(8,128)(2,1)S(1)} %all-to-all-done.2.got_ref, f32[512,384]{1,0:T(8,128)S(1)} %get-tuple-element.29.kept_ref, bf16[2,6,128,128]{3,2,1,0:T(8,128)(2,1)S(1)} %get-tuple-element.31.below_ref, ...), custom_call_target="tpu_custom_call" | custom-call | flops 805306368 | bytes 9437184 | tf_op jit(solution)/shard_map/pallas_call | solution.py:342
  (11 shorter events, 0.1 us)
Async XLA Ops:
  2.6 22.8 %copy-start = (f32[512,384]{1,0:T(8,128)S(1)}, f32[512,384]{1,0:T(8,128)}, u32[]{:S(2)}) copy-start(f32[512,384]{1,0:T(8,128)} %matrix_ref.1) | copy-start | bytes 2359300
  2.6 22.8 %copy-start.1 = (s32[512]{0:T(512)S(1)}, s32[512]{0:T(512)}, u32[]{:S(2)}) copy-start(s32[512]{0:T(512)} %param.5) | copy-start | bytes 6148
  2.6 31.0 %all-to-all-start = ((f16[32,16,512]{2,1,0:T(8,128)(2,1)}), f16[32,16,512]{2,1,0:T(8,128)(2,1)S(1)}, u32[]{:S(2)}, u32[]{:S(2)}) async-start(f16[32,16,512]{2,1,0:T(8,128)(2,1)} %convert_element_type.12), calls=%async_computation | async-start | bytes 1048576 | tf_op jit(solution)/shard_map/all_to_all | solution.py:270
  16.3 17.3 %collective-permute-start = (bf16[32,512]{1,0:T(8,128)(2,1)S(1)}, bf16[32,512]{1,0:T(8,128)(2,1)S(1)}, u32[]{:S(2)}, u32[]{:S(2)}) collective-permute-start(bf16[32,512]{1,0:T(8,128)(2,1)S(1)} %get-tuple-element.22), channel_id=1, source_target_pairs={{0,8},{2,10},{4,12},{6,14},{8,0},{10,2},{12,4},{14,6},{1,9},{3,11}... | collective-permute-start | bytes 98312 | tf_op jit(solution)/shard_map/ppermute | solution.py:308
  21.4 12.3 %collective-permute-start.1 = (bf16[32,512]{1,0:T(8,128)(2,1)S(1)}, bf16[32,512]{1,0:T(8,128)(2,1)S(1)}, u32[]{:S(2)}, u32[]{:S(2)}) collective-permute-start(bf16[32,512]{1,0:T(8,128)(2,1)S(1)} %get-tuple-element.22), channel_id=1, source_target_pairs={{0,12},{2,14},{4,0},{6,2},{8,4},{10,6},{12,8},{14,10},{1,13},{3,15... | collective-permute-start | bytes 98312 | tf_op jit(solution)/shard_map/ppermute | solution.py:308
  34.4 20.6 %all-to-all-start.1 = ((f16[64,16,128]{2,1,0:T(8,128)(2,1)}), f16[64,16,128]{2,1,0:T(8,128)(2,1)S(1)}, u32[]{:S(2)}, u32[]{:S(2)}) async-start(f16[64,16,128]{2,1,0:T(8,128)(2,1)} %broadcast_in_dim.2), calls=%async_computation.1 | async-start | bytes 524288 | tf_op jit(solution)/shard_map/all_to_all | solution.py:270
  44.3 8.9 %collective-permute-start.2 = (bf16[96,512]{1,0:T(8,128)(2,1)S(1)}, bf16[96,512]{1,0:T(8,128)(2,1)S(1)}, u32[]{:S(2)}, u32[]{:S(2)}) collective-permute-start(bf16[96,512]{1,0:T(8,128)(2,1)S(1)} %pad_maximum_fusion), channel_id=1, source_target_pairs={{0,14},{2,0},{4,2},{6,4},{8,6},{10,8},{12,10},{14,12},{1,15},{3,1}... | collective-permute-start | bytes 294920 | tf_op jit(solution)/shard_map/ppermute | solution.py:308
  55.0 27.1 %all-to-all-start.2 = ((bf16[32,16,768]{2,1,0:T(8,128)(2,1)}), bf16[32,16,768]{2,1,0:T(8,128)(2,1)S(1)}, u32[]{:S(2)}, u32[]{:S(2)}) async-start(bf16[32,16,768]{2,1,0:T(8,128)(2,1)} %shard_map.38), calls=%async_computation.2 | async-start | bytes 1572864 | tf_op jit(solution)/shard_map/all_to_all | solution.py:270
  60.1 4.7 %collective-permute-start.3 = (f16[64,16,128]{2,1,0:T(8,128)(2,1)S(1)}, f16[64,16,128]{2,1,0:T(8,128)(2,1)S(1)}, u32[]{:S(2)}, u32[]{:S(2)}) collective-permute-start(f16[64,16,128]{2,1,0:T(8,128)(2,1)S(1)} %all-to-all-done.1), channel_id=1, source_target_pairs={{0,1},{1,0},{2,3},{3,2},{4,5},{5,4},{6,7},{7,6},{8,9},{9,8},{10,11... | collective-permute-start | bytes 786440 | tf_op jit(solution)/shard_map/ppermute | solution.py:323
  62.1 8.7 %collective-permute-start.4 = (bf16[64,512]{1,0:T(8,128)(2,1)S(1)}, bf16[64,512]{1,0:T(8,128)(2,1)S(1)}, u32[]{:S(2)}, u32[]{:S(2)}) collective-permute-start(bf16[64,512]{1,0:T(8,128)(2,1)S(1)} %pad_maximum_fusion.1), channel_id=1, source_target_pairs={{0,4},{2,6},{4,8},{6,10},{8,12},{10,14},{12,0},{14,2},{1,5},{3,7},... | collective-permute-start | bytes 196616 | tf_op jit(solution)/shard_map/ppermute | solution.py:308
  70.8 3.4 %collective-permute-start.5 = (bf16[256,512]{1,0:T(8,128)(2,1)S(1)}, bf16[256,512]{1,0:T(8,128)(2,1)S(1)}, u32[]{:S(2)}, u32[]{:S(2)}) collective-permute-start(bf16[256,512]{1,0:T(8,128)(2,1)S(1)} %constant_dynamic-update-slice_fusion.own_ref), channel_id=1, source_target_pairs={{0,1},{1,0},{2,3},{3,2},{4,5},{5,4},{6,7},{7,6},{8,9},{9,8},{10,11... | collective-permute-start | bytes 786440 | tf_op jit(solution)/shard_map/ppermute | solution.py:334
